TPU v7x, 32 devices: a whole 2x2x4 slice. The times are simulated.
32 devices in a mesh: rep: 8 (over z, y), shard: 4 (over x, core).
Axes of the slice: x: 2, y: 2, z: 4, core: 2. Of those that a mesh axis runs over, the one named last changes fastest.
Arguments:
- inputs: bfloat16 [64, 1024, 512], P(('rep', 'shard')), may hold values from -6 to 6
- lengths: int32 [64], P(('rep', 'shard')), may hold values from 256 to 1024, as said below
- w_qkv: bfloat16 [512, 1536], P('shard'), may hold values from -0.25 to 0.25
- w_out: bfloat16 [512, 512], P('shard'), may hold values from -2 to 2
- w_in: bfloat16 [512, 2048], P('shard'), may hold values from -0.25 to 0.25
- w_back: bfloat16 [2048, 512], P('shard'), may hold values from -0.125 to 0.125
- vectors: bfloat16 [32, 512], P('shard'), may hold values from -5 to 5
- cotangent: bfloat16 [64, 1024, 512], P(('rep', 'shard')), may hold values from -6 to 6
Outputs:
- output: bfloat16 [64, 1024, 512], P(('rep', 'shard'))
- grad_inputs: bfloat16 [64, 1024, 512], P(('rep', 'shard'))
- grad_qkv: float32 [512, 1536], P('shard')
- grad_out: float32 [512, 512], P('shard')
- grad_in: float32 [512, 2048], P('shard')
- grad_back: float32 [2048, 512], P('shard')
- grad_vectors: float32 [32, 512], P('shard')
Inputs may be any that keep to these rules, and one draw needn't show every extreme that they name: `lengths`: valid tokens are a sequence's first slots; some sequence has exactly 1024 and some exactly 256.
All inputs are finite; a program needn't handle non-finite values.
Results may differ from a plain program's by a relative error of at most 0.019.
Values may be sent and summed in bfloat16 or wider, within the bound.
No kernel may reach another device: no remote copies, remote signals or barrier semaphores. Data moves between devices by JAX's collectives and lax.ppermute only.
A program may use at most 192 MiB of HBM per device.

v0:
```python
import math
from functools import partial

import jax
import jax.numpy as jnp
from jax import lax
from jax.experimental import pallas as pl
from jax.experimental.pallas import tpu as pltpu
from jax.sharding import PartitionSpec as P

D = 512
HEADS = 8
HDIM = 64
FF = 2048
MEM = 20
TILE = 256
PAIRS = HEADS // 2
SCALE = HDIM**-0.5
QSCALE = SCALE * math.log2(math.e)
LN2 = math.log(2.0)
F32 = jnp.float32
BF16 = jnp.bfloat16
VROWS = 80
VMEM_LIMIT = 62 * 2**20


def nn(a, b):
    return lax.dot_general(a, b, (((1,), (0,)), ((), ())), preferred_element_type=F32)


def nt(a, b):
    return lax.dot_general(a, b, (((1,), (1,)), ((), ())), preferred_element_type=F32)


def tn(a, b):
    return lax.dot_general(a, b, (((0,), (0,)), ((), ())), preferred_element_type=F32)


def key_sizes(seq_rows):
    top = -(-(seq_rows + MEM) // 32) * 32
    return [rows for rows in range(512, top, 256)] + [top]


def column_max(values):
    parts = [values[i : i + 128] for i in range(0, values.shape[0] - 127, 128)]
    while len(parts) > 1:
        odd = parts[len(parts) - len(parts) % 2 :]
        parts = [jnp.maximum(a, b) for a, b in zip(parts[::2], parts[1::2])] + odd
    top = jnp.max(parts[0], axis=0, keepdims=True)
    rest = values.shape[0] % 128
    if rest:
        top = jnp.maximum(top, jnp.max(values[-rest:], axis=0, keepdims=True))
    return top


AHEAD = 2
BODY_HEADS = 4


def cdiv(a, b):
    return (a + b - 1) // b


def pick_memory(rows_ref, memory, length):
    edge = pl.multiple_of(length // 128 * 128, 128)
    fix = pl.ds(edge, TILE)
    row = lax.broadcasted_iota(jnp.int32, (TILE, 1), 0) + edge
    lane = lax.broadcasted_iota(jnp.int32, (TILE, 32), 1)
    pick = lax.broadcasted_iota(jnp.int32, (TILE, 32), 0) + (edge - length) == lane
    placed = nn(jnp.where(pick, 1.0, 0.0).astype(BF16), memory)
    rows_ref[fix, :] = jnp.where(row < length, rows_ref[fix, :].astype(F32), placed).astype(BF16)


def memory_rows(vec_ref):
    inside = lax.broadcasted_iota(jnp.int32, (32, D), 0) < MEM
    return jnp.where(inside, vec_ref[...].astype(F32), 0.0).astype(BF16)


def for_size(seq_rows, total, run):
    sizes = key_sizes(seq_rows)
    for index, kr in enumerate(sizes):
        least = sizes[index - 1] if index else 0

        @pl.when(jnp.logical_and(total > least, total <= kr))
        def _(kr=kr):
            run(kr)


def prepare_kernel(shards, me_ref, *refs):
    pieces = refs[:shards]
    w_ref, wqt_ref, wvt_ref, vec_ref, few_rows, sems = refs[shards:]
    me = me_ref[0]
    part, few = D // shards, 32 // shards
    copies, small = [], []
    for m in range(shards):
        at = pl.multiple_of((me ^ m) * part, part)
        small.append(
            pltpu.make_async_copy(
                pieces[m].at[pl.ds(part, SPARE), pl.ds(0, D)], few_rows.at[m], sems.at[m, 1]
            )
        )
        copies.append(
            pltpu.make_async_copy(
                pieces[m].at[pl.ds(0, part), :], w_ref.at[pl.ds(at, part), :], sems.at[m, 0]
            )
        )
    for copy in small + copies:
        copy.start()
    for copy in small:
        copy.wait()
    owner = lax.broadcasted_iota(jnp.int32, (32, D), 0) // few
    rows = jnp.zeros((32, D), F32)
    for m in range(shards):
        values = few_rows[m].astype(F32)[:few]
        rows = jnp.where(owner == (me ^ m), jnp.concatenate([values] * shards, 0), rows)
    vec_ref[...] = rows.astype(BF16)
    for copy in copies:
        copy.wait()
    wqt_ref[...] = w_ref[:, :D].T
    wvt_ref[...] = w_ref[:, 2 * D :].T


SPARE = 16


def pack(w_qkv, vectors):
    below = ((0, SPARE - vectors.shape[0]), (0, w_qkv.shape[1] - vectors.shape[1]))
    return jnp.concatenate([w_qkv, jnp.pad(vectors, below)], 0)


def prepare(me, pieces):
    shards = len(pieces)
    vm = pl.BlockSpec(memory_space=pltpu.VMEM)
    return pl.pallas_call(
        partial(prepare_kernel, shards),
        out_shape=(
            jax.ShapeDtypeStruct((D, 3 * D), BF16),
            jax.ShapeDtypeStruct((D, D), BF16),
            jax.ShapeDtypeStruct((D, D), BF16),
            jax.ShapeDtypeStruct((32, D), BF16),
        ),
        in_specs=[pl.BlockSpec(memory_space=pltpu.SMEM)]
        + [pl.BlockSpec(memory_space=pl.ANY)] * shards,
        out_specs=(vm, vm, vm, vm),
        scratch_shapes=[
            pltpu.VMEM((shards, SPARE, D), BF16),
            pltpu.SemaphoreType.DMA((shards, 2)),
        ],
        compiler_params=pltpu.CompilerParams(vmem_limit_bytes=24 * 2**20),
        name="prepare",
    )(me, *pieces)


def fwd_kernel(
    seq_rows, seq, len_ref, x_hbm, wk_ref, wqt_ref, wvt_ref, vec_ref,
    e_hbm, qt_hbm, mixt_hbm, inv_ref,
    rows, keys, vt, qpad, queries, mixed_t, ebuf, sems, io_sems,
):
    length = len_ref[seq]
    total = length + MEM
    load = pltpu.make_async_copy(x_hbm.at[seq], rows.at[pl.ds(0, seq_rows), :], io_sems.at[0])
    load.start()
    memory = memory_rows(vec_ref)
    vec_cols = vec_ref[...].astype(F32).T
    bias_q = vec_cols[:, MEM : MEM + 1]
    bias_v = vec_cols[:, MEM + 1 : MEM + 2]
    mixed_t[...] = jnp.zeros(mixed_t.shape, BF16)
    inv_ref[...] = jnp.zeros(inv_ref.shape, F32)
    for head in range(HEADS):
        spare = HDIM * (1 - head % 2)
        qpad[head, spare : spare + HDIM, :] = jnp.zeros((HDIM, qpad.shape[2]), BF16)
    vt[:, HDIM:, :] = jnp.ones((HEADS, VROWS - HDIM, vt.shape[2]), BF16)
    n_tiles = cdiv(length, TILE)
    chunks = cdiv(total, TILE)
    load.wait()

    rows[seq_rows:, :] = jnp.zeros((rows.shape[0] - seq_rows, D), BF16)
    pick_memory(rows, memory, length)

    def project(chunk, _):
        here = pl.ds(pl.multiple_of(chunk * TILE, TILE), TILE)
        joined = rows[here, :]
        key_rows = nn(joined, wk_ref[...]).astype(BF16)
        for pair in range(PAIRS):
            keys[pair, here, :] = key_rows[:, pair * 128 : pair * 128 + 128]
        values = (nt(wvt_ref[...], joined) + bias_v).astype(BF16)
        found = ((nt(wqt_ref[...], joined) + bias_q) * QSCALE).astype(BF16)
        queries[:, here] = found
        for head in range(HEADS):
            low = (head % 2) * HDIM
            vt[head, :HDIM, here] = values[head * HDIM : (head + 1) * HDIM]
            qpad[head, low : low + HDIM, here] = found[head * HDIM : (head + 1) * HDIM]
        return 0

    lax.fori_loop(0, chunks, project, 0)
    save = pltpu.make_async_copy(queries.at[:, pl.ds(0, seq_rows)], qt_hbm, io_sems.at[1])
    save.start()

    def attend(kr):
        tail = kr - TILE if kr % TILE == 0 else kr - kr % TILE
        row = lax.broadcasted_iota(jnp.int32, (kr - tail, TILE), 0) + tail
        mask = row < total

        def copies(tile, pair):
            return pltpu.make_async_copy(
                ebuf.at[pair, :, pl.ds(0, kr), :],
                e_hbm.at[tile, pl.ds(pair * 2, 2), pl.ds(0, kr), :],
                sems.at[pair],
            )

        turns = HEADS // BODY_HEADS

        def step(unit, _):
            tile, turn = unit // turns, unit % turns
            here = pl.ds(pl.multiple_of(tile * TILE, TILE), TILE)
            base = turn * BODY_HEADS

            def score(i):
                pair = turn * (BODY_HEADS // 2) + i // 2
                scores = nn(keys[pair, :kr, :], qpad[base + i, :, here])
                scores = jnp.concatenate(
                    [scores[:tail], jnp.where(mask, scores[tail:], -1e30)], 0
                )
                return scores, column_max(scores)

            live = {i: score(i) for i in range(AHEAD)}
            for i in range(BODY_HEADS):
                pair, sub = turn * (BODY_HEADS // 2) + i // 2, i % 2
                scores, top = live.pop(i)
                if sub == 0:
                    copies(tile, pair).wait()
                if i + AHEAD < BODY_HEADS:
                    live[i + AHEAD] = score(i + AHEAD)
                expo = jnp.exp2(scores - top).astype(BF16)
                ebuf[pair, sub, :kr, :] = expo
                mixed = nn(vt[base + i, :, :kr], expo)
                inverse = 1.0 / mixed[HDIM : HDIM + 1]
                spot = pl.ds(pl.multiple_of((base + i) * HDIM, HDIM), HDIM)
                mixed_t[spot, here] = (mixed[:HDIM] * inverse).astype(BF16)
                inv_ref[pl.ds(base + i, 1), here] = inverse
                if sub == 1:
                    copies(tile, pair).start()
            return 0

        for pair in range(PAIRS):
            copies(0, pair).start()
        lax.fori_loop(0, n_tiles * turns, step, 0)
        out = pltpu.make_async_copy(mixed_t, mixt_hbm, io_sems.at[2])
        out.start()
        for pair in range(PAIRS):
            copies(n_tiles - 1, pair).wait()
        save.wait()
        out.wait()

    for_size(seq_rows, total, attend)


def attention_forward(seq, lengths, x, w_qkv, wqt, wvt, vectors):
    seq_rows = x.shape[1]
    top = key_sizes(seq_rows)[-1]
    padded = cdiv(seq_rows + MEM, TILE) * TILE
    tiles = seq_rows // TILE
    vm = pl.BlockSpec(memory_space=pltpu.VMEM)
    hbm = pl.BlockSpec(memory_space=pl.ANY)
    return pl.pallas_call(
        partial(fwd_kernel, seq_rows, seq),
        out_shape=(
            jax.ShapeDtypeStruct((tiles, HEADS, top, TILE), BF16),
            jax.ShapeDtypeStruct((D, seq_rows), BF16),
            jax.ShapeDtypeStruct((D, seq_rows), BF16),
            jax.ShapeDtypeStruct((HEADS, seq_rows), F32),
        ),
        grid=(1,),
        in_specs=[
            pl.BlockSpec(memory_space=pltpu.SMEM),
            hbm,
            pl.BlockSpec((D, D), lambda i: (0, 1)),
            vm,
            vm,
            vm,
        ],
        out_specs=(hbm, hbm, hbm, vm),
        scratch_shapes=[
            pltpu.VMEM((padded, D), BF16),
            pltpu.VMEM((PAIRS, padded, 128), BF16),
            pltpu.VMEM((HEADS, VROWS, padded), BF16),
            pltpu.VMEM((HEADS, 128, padded), BF16),
            pltpu.VMEM((D, padded), BF16),
            pltpu.VMEM((D, seq_rows), BF16),
            pltpu.VMEM((PAIRS, 2, top, TILE), BF16),
            pltpu.SemaphoreType.DMA((PAIRS,)),
            pltpu.SemaphoreType.DMA((3,)),
        ],
        compiler_params=pltpu.CompilerParams(vmem_limit_bytes=VMEM_LIMIT),
        cost_estimate=pl.CostEstimate(
            flops=8 * 10**9, bytes_accessed=24 * 10**6, transcendentals=8 * 10**6
        ),
        name="attention_forward",
    )(lengths, x, w_qkv, wqt, wvt, vectors)


def norm_forward(values):
    center = values - jnp.mean(values, axis=-1, keepdims=True)
    inverse = lax.rsqrt(jnp.mean(center * center, axis=-1, keepdims=True) + 1e-05)
    return center * inverse, inverse


def norm_backward(grad, normed, inverse):
    return inverse * (
        grad
        - jnp.mean(grad, axis=-1, keepdims=True)
        - normed * jnp.mean(grad * normed, axis=-1, keepdims=True)
    )


def col_sum(values):
    return jnp.sum(values, axis=0, keepdims=True)


GELU_A = math.sqrt(2.0 / math.pi)
GELU_B = GELU_A * 0.044715
BLOCKS = FF // D


def piece_order(shards):
    bits = shards.bit_length() - 1
    return [int(format(i, "b").zfill(bits)[::-1], 2) if bits else 0 for i in range(shards)]


def piece_spots(pair, shards, rows):
    half = max(shards // 2, 1)
    for index, m in enumerate(piece_order(shards)):
        yield m, pair[index // half], index % half * rows


def ffn_kernel(
    seq_rows, shards, len_ref, me_ref, x_hbm, cot_hbm, mixt0, mixt1, inv0, inv1, *refs,
):
    wi_p, wb_p = refs[:shards], refs[shards : 2 * shards]
    vec_ref, out_hbm, gh_hbm, dot_hbm = refs[2 * shards : 2 * shards + 4]
    grads = refs[2 * shards + 4 : 2 * shards + 8]
    (
        sums_ref, x_ref, cot_ref, mixt_ref, inv_ref, wo_ref, wi_ref, wb_ref,
        out_ref, gh_ref, dot_ref, acc_o, acc_i, acc_b, slopes, actives,
        s_normed1, s_first, s_gsecond, ups, sems, out_sems,
    ) = refs[2 * shards + 8 :]
    half = TILE // 2
    len0, len1 = len_ref[0], len_ref[1]
    me = me_ref[0]
    n0, n1 = cdiv(len0, half), cdiv(len1, half)
    full = seq_rows // half
    n_all = n0 + n1

    def rows_at(piece, rows):
        return pl.ds(pl.multiple_of((me ^ piece) * rows, rows), rows)

    loads = []

    def load(src, dst):
        copy = pltpu.make_async_copy(src, dst, sems.at[len(loads)])
        loads.append(copy)
        copy.start()
        return copy

    first_loads = [load(mixt0, mixt_ref.at[0]), load(mixt1, mixt_ref.at[1])]
    first_loads += [load(inv0, inv_ref.at[0]), load(inv1, inv_ref.at[1])]
    part = D // shards
    first_loads += [
        load(p.at[:, pl.ds(0, D)], wo_ref.at[rows_at(i, part), :]) for i, p in enumerate(wi_p)
    ]
    first_loads += [load(x_hbm.at[s], x_ref.at[s]) for s in range(2)]
    second_loads = [
        load(p.at[:, pl.ds(D, FF)], wi_ref.at[rows_at(i, part), :]) for i, p in enumerate(wi_p)
    ]
    second_loads += [load(p, wb_ref.at[rows_at(i, FF // shards), :]) for i, p in enumerate(wb_p)]
    third_loads = [load(cot_hbm.at[s], cot_ref.at[s]) for s in range(2)]

    out_ref[...] = jnp.zeros(out_ref.shape, BF16)
    gh_ref[...] = jnp.zeros(gh_ref.shape, BF16)
    dot_ref[...] = jnp.zeros(dot_ref.shape, BF16)
    acc_o[...] = jnp.zeros(acc_o.shape, F32)
    acc_i[...] = jnp.zeros(acc_i.shape, F32)
    acc_b[...] = jnp.zeros(acc_b.shape, F32)
    sums_ref[...] = jnp.zeros(sums_ref.shape, F32)

    def vec(index):
        return vec_ref[index : index + 1, :].astype(F32)

    bias_out = vec(MEM + 2)
    bias_back = vec(MEM + 3 + BLOCKS)
    gain_one = vec(MEM + 4 + BLOCKS)
    shift_one = vec(MEM + 5 + BLOCKS)
    gain_two = vec(MEM + 6 + BLOCKS)
    shift_two = vec(MEM + 7 + BLOCKS)

    spare_one = jnp.logical_and(n_all % 2 == 1, n1 < full)
    spare_zero = jnp.logical_and(n_all % 2 == 1, n1 >= full)

    def place(chunk):
        second = chunk >= n0
        inside = jnp.where(second, chunk - n0, chunk)
        spare = chunk >= n_all
        seq = jnp.where(spare, jnp.where(n1 < full, 1, 0), jnp.where(second, 1, 0))
        inside = jnp.where(spare, jnp.where(n1 < full, n1, n0), inside)
        return seq, pl.multiple_of(inside * half, half), jnp.where(seq == 1, len1, len0)

    def rows_of(ref, spots):
        return jnp.concatenate([ref[s, pl.ds(r, half), :] for s, r, _ in spots], 0)

    def lanes_of(ref, spots):
        return jnp.concatenate([ref[s, :, pl.ds(r, half)] for s, r, _ in spots], 1)

    def put_rows(ref, value, spots):
        for i, (s, r, _) in enumerate(spots):
            ref[s, pl.ds(r, half), :] = value[i * half : (i + 1) * half]

    def put_lanes(ref, value, spots):
        for i, (s, r, _) in enumerate(spots):
            ref[s, :, pl.ds(r, half)] = value[:, i * half : (i + 1) * half]

    def valid_of(spots):
        iota = lax.broadcasted_iota(jnp.int32, (half, 1), 0)
        return jnp.concatenate(
            [jnp.where(iota + r < count, 1.0, 0.0) for _, r, count in spots], 0
        )

    def add_sum(row, value):
        sums_ref[row : row + 1] += col_sum(value)

    def whole_tile(spots):
        count = half * len(spots)
        here = slice(0, count)
        valid = valid_of(spots)
        mixt = lanes_of(mixt_ref, spots)
        attn = nn(mixt.T, wo_ref[...]) + bias_out
        normed_one, inverse_one = norm_forward(rows_of(x_ref, spots).astype(F32) + attn)
        first = normed_one * gain_one + shift_one
        s_normed1[here] = normed_one
        low = first.astype(BF16)
        s_first[here] = low
        second = first + bias_back
        for j in range(BLOCKS):
            cols = slice(j * D, (j + 1) * D)
            up = nn(low, wi_ref[:, cols]) + vec(MEM + 3 + j)
            square = up * up
            gate = 0.5 + 0.5 * jnp.tanh(up * (GELU_A + GELU_B * square))
            active = up * gate
            slopes[here, cols] = (
                gate + active * (2.0 - 2.0 * gate) * (GELU_A + 3.0 * GELU_B * square)
            ).astype(slopes.dtype)
            actives[here, cols] = active.astype(BF16)
        second = second + nn(actives[here, :], wb_ref[...])
        normed_two, inverse_two = norm_forward(second)
        put_rows(out_ref, ((normed_two * gain_two + shift_two) * valid).astype(BF16), spots)
        grad_out = rows_of(cot_ref, spots).astype(F32) * valid
        add_sum(MEM + 6 + BLOCKS, grad_out * normed_two)
        add_sum(MEM + 7 + BLOCKS, grad_out)
        grad_second = norm_backward(grad_out * gain_two, normed_two, inverse_two)
        s_gsecond[here] = grad_second
        down = grad_second.astype(BF16)
        add_sum(MEM + 3 + BLOCKS, down.astype(F32))
        low_t = s_first[here, :].T
        for j in range(BLOCKS):
            cols = slice(j * D, (j + 1) * D)
            grad_up = (
                nt(down, wb_ref[cols, :]) * slopes[here, cols].astype(F32)
            ).astype(BF16)
            acc_b[cols, :] += tn(actives[here, cols], down)
            ups[here, cols] = grad_up
            add_sum(MEM + 3 + j, grad_up.astype(F32))
            acc_i[:, cols] += nn(low_t, grad_up)
        grad_first = s_gsecond[here] + nt(ups[here, :], wi_ref[...])
        normed_one = s_normed1[here]
        add_sum(MEM + 4 + BLOCKS, grad_first * normed_one)
        add_sum(MEM + 5 + BLOCKS, grad_first)
        grad_one = norm_backward(grad_first * gain_one, normed_one, inverse_one)
        low = grad_one.astype(BF16)
        put_rows(gh_ref, low, spots)
        add_sum(MEM + 2, low.astype(F32))
        acc_o[...] += nn(mixt, low)
        grad_mixed = nt(wo_ref[...], low)
        inverse = lanes_of(inv_ref, spots)
        scaled = [
            grad_mixed[h * HDIM : (h + 1) * HDIM] * inverse[h : h + 1] for h in range(HEADS)
        ]
        put_lanes(dot_ref, jnp.concatenate(scaled, 0).astype(BF16), spots)

    def send(ref, hbm, sem, seq, row, lanes=False):
        here = pl.ds(row, half)
        src = ref.at[seq, :, here] if lanes else ref.at[seq, here, :]
        dst = hbm.at[seq, :, here] if lanes else hbm.at[seq, here, :]
        pltpu.make_async_copy(src, dst, out_sems.at[sem]).start()

    def send_all(seq, row):
        send(out_ref, out_hbm, 0, seq, row)
        send(gh_ref, gh_hbm, 1, seq, row)
        send(dot_ref, dot_hbm, 2, seq, row, True)

    for copy in first_loads + second_loads + third_loads:
        copy.wait()

    def step(index, _):
        spots = [place(index * 4 + i) for i in range(4)]
        whole_tile(spots)
        for seq, row, _ in spots:
            send_all(seq, row)
        return 0

    left = lax.rem(n_all, 4)
    bigs = n_all // 4 + jnp.where(left == 3, 1, 0)
    lax.fori_loop(0, bigs, step, 0)

    @pl.when(jnp.logical_or(left == 1, left == 2))
    def _():
        spots = [place(bigs * 4 + i) for i in range(2)]
        whole_tile(spots)
        for seq, row, _ in spots:
            send_all(seq, row)

    def rest(seq):
        def one(chunk, _):
            send_all(seq, pl.multiple_of(chunk * half, half))
            return 0

        return one

    lax.fori_loop(n0 + jnp.where(spare_zero, 1, 0), full, rest(0), 0)
    lax.fori_loop(n1 + jnp.where(spare_one, 1, 0), full, rest(1), 0)

    part = D // shards
    deep = FF // shards
    block = part * (1 + BLOCKS)
    for m, piece, row in piece_spots(grads[:2], shards, block):
        at = pl.multiple_of((me ^ m) * part, part)
        piece[row : row + part, :] = acc_o[pl.ds(at, part), :].astype(BF16)
        for j in range(BLOCKS):
            row += part
            piece[row : row + part, :] = acc_i[
                pl.ds(at, part), j * D : (j + 1) * D
            ].astype(BF16)
    for m, piece, row in piece_spots(grads[2:], shards, deep):
        at = pl.multiple_of((me ^ m) * deep, deep)
        piece[row : row + deep, :] = acc_b[pl.ds(at, deep), :].astype(BF16)
    for ref, hbm, sem in ((out_ref, out_hbm, 0), (gh_ref, gh_hbm, 1), (dot_ref, dot_hbm, 2)):
        pltpu.make_async_copy(ref, hbm, out_sems.at[sem]).wait()


def feed_forward(lengths, me, x, cot, mixts, invs, w_up, w_back, vectors):
    count, seq_rows = x.shape[:2]
    shards = len(w_up)
    vm = pl.BlockSpec(memory_space=pltpu.VMEM)
    hbm = pl.BlockSpec(memory_space=pl.ANY)
    smem = pl.BlockSpec(memory_space=pltpu.SMEM)
    return pl.pallas_call(
        partial(ffn_kernel, seq_rows, shards),
        out_shape=(
            jax.ShapeDtypeStruct((count, seq_rows, D), BF16),
            jax.ShapeDtypeStruct((count, seq_rows, D), BF16),
            jax.ShapeDtypeStruct((count, D, seq_rows), BF16),
            *[
                jax.ShapeDtypeStruct((rows, D), BF16)
                for rows in (D * (1 + BLOCKS) // 2, FF // 2)
                for _ in range(2)
            ],
            jax.ShapeDtypeStruct((32, D), F32),
        ),
        in_specs=[smem, smem] + [hbm] * (6 + 2 * shards) + [vm],
        out_specs=(hbm, hbm, hbm) + (vm,) * 5,
        scratch_shapes=[
            pltpu.VMEM((count, seq_rows, D), BF16),
            pltpu.VMEM((count, seq_rows, D), BF16),
            pltpu.VMEM((count, D, seq_rows), BF16),
            pltpu.VMEM((count, HEADS, seq_rows), F32),
            pltpu.VMEM((D, D), BF16),
            pltpu.VMEM((D, FF), BF16),
            pltpu.VMEM((FF, D), BF16),
            pltpu.VMEM((count, seq_rows, D), BF16),
            pltpu.VMEM((count, seq_rows, D), BF16),
            pltpu.VMEM((count, D, seq_rows), BF16),
            pltpu.VMEM((D, D), F32),
            pltpu.VMEM((D, FF), F32),
            pltpu.VMEM((FF, D), F32),
            pltpu.VMEM((2 * TILE, FF), F32),
            pltpu.VMEM((2 * TILE, FF), BF16),
            pltpu.VMEM((2 * TILE, D), F32),
            pltpu.VMEM((2 * TILE, D), BF16),
            pltpu.VMEM((2 * TILE, D), F32),
            pltpu.VMEM((2 * TILE, FF), BF16),
            pltpu.SemaphoreType.DMA((8 + 3 * shards,)),
            pltpu.SemaphoreType.DMA((3,)),
        ],
        compiler_params=pltpu.CompilerParams(vmem_limit_bytes=VMEM_LIMIT),
        cost_estimate=pl.CostEstimate(
            flops=27 * 10**9, bytes_accessed=24 * 10**6, transcendentals=4 * 10**6
        ),
        name="feed_forward",
    )(lengths, me, x, cot, *mixts, *invs, *w_up, *w_back, vectors)


def bwd_kernel(seq_rows, groups, group, seq, shards, chained, closing, waits, *refs):
    gp = PAIRS // groups
    gcols = gp * 128
    width = 3 * gcols
    refs = list(refs)
    len_ref, me_ref, wk_ref, wv_ref, vec_ref = refs[:5]
    x_hbm, dot_hbm, qt_hbm, mixt_hbm, e_hbm = refs[5:10]
    refs = refs[10:]
    acc_in, extra_in = (refs.pop(0), refs.pop(0)) if chained else (None, None)
    other_rows = [refs.pop(0) for _ in range(closing)]
    refs = refs[waits:]
    proj_hbm = refs.pop(0)
    last = chained
    if last:
        pieces = [refs.pop(0), refs.pop(0)]
    else:
        acc_hbm = refs.pop(0)
    extra_ref = None if closing else refs.pop(0)
    token = refs.pop(0)
    token[...] = jnp.zeros(token.shape, F32)
    (
        rows, qts, mixts, dots, wkt, kt, values, qpad, dpad, dqt, dk, dv, ebuf, acc, proj,
        extra, table, sems, io_sems, out_sem, acc_sem,
    ) = refs
    base = group * gcols
    mine = pl.ds(base, gcols)
    length = len_ref[seq]
    total = length + MEM
    n_tiles = cdiv(length, TILE)
    chunks = cdiv(total, TILE)
    pairs = [
        (x_hbm.at[seq], rows.at[pl.ds(0, seq_rows), :]),
        (qt_hbm.at[mine, :], qts),
        (mixt_hbm.at[mine, :], mixts),
        (dot_hbm.at[seq, mine, :], dots),
    ]
    loads = [pltpu.make_async_copy(a, b, io_sems.at[i]) for i, (a, b) in enumerate(pairs)]

    def copies_of(kr):
        def copies(tile, slot):
            return pltpu.make_async_copy(
                e_hbm.at[tile, pl.ds(group * gp * 2, gp * 2), pl.ds(0, kr), :],
                ebuf.at[slot, :, pl.ds(0, kr), :],
                sems.at[slot],
            )

        return copies

    for copy in loads:
        copy.start()
    if chained:
        fetch = pltpu.make_async_copy(acc_in, acc, acc_sem)
        fetch.start()
    for_size(seq_rows, total, lambda kr: copies_of(kr)(0, 0).start())
    memory = memory_rows(vec_ref)
    bias_v = vec_ref[MEM + 1 : MEM + 2, base : base + gcols].astype(F32)
    wkt[...] = wk_ref[...].T
    if chained:
        extra[...] = extra_in[...]
        for other in other_rows:
            extra[...] += other[...]
    else:
        acc[...] = jnp.zeros(acc.shape, F32)
        extra[...] = jnp.zeros(extra.shape, F32)
    for head in range(gp * 2):
        spare = HDIM * (1 - head % 2)
        qpad[head, spare : spare + HDIM, :] = jnp.zeros((HDIM, TILE), BF16)
        dpad[head, spare : spare + HDIM, :] = jnp.zeros((HDIM, TILE), BF16)
    rows[seq_rows:, :] = jnp.zeros((rows.shape[0] - seq_rows, D), BF16)
    loads[0].wait()
    edge = pl.multiple_of(length // 128 * 128, 128)
    fix = pl.ds(edge, TILE)
    pick_memory(rows, memory, length)

    def project(chunk, _):
        here = pl.ds(pl.multiple_of(chunk * TILE, TILE), TILE)
        joined = rows[here, :]
        value_rows = (nn(joined, wv_ref[...]) + bias_v).astype(BF16)
        for pair in range(gp):
            values[pair, here, :] = value_rows[:, pair * 128 : pair * 128 + 128]
            dk[pair, here, :] = jnp.zeros((TILE, 128), F32)
            dv[pair, here, :] = jnp.zeros((TILE, 128), F32)
        kt[:, here] = nt(wkt[...], joined).astype(BF16)
        dqt[:, here] = jnp.zeros((gcols, TILE), BF16)
        return 0

    lax.fori_loop(0, chunks, project, 0)
    for copy in loads[1:]:
        copy.wait()

    def attend(kr):
        copies = copies_of(kr)

        def step(tile, _):
            slot = lax.rem(tile, 2)
            here = pl.ds(pl.multiple_of(tile * TILE, TILE), TILE)

            @pl.when(tile + 1 < n_tiles)
            def _():
                copies(tile + 1, 1 - slot).start()

            copies(tile, slot).wait()
            inners = []
            for head in range(gp * 2):
                low = (head % 2) * HDIM
                local = slice(head * HDIM, (head + 1) * HDIM)
                outer = dots[local, here]
                dpad[head, low : low + HDIM, :] = outer
                qpad[head, low : low + HDIM, :] = qts[local, here]
                inners.append(col_sum(outer.astype(F32) * mixts[local, here].astype(F32)))

            def outer_product(head):
                return nn(values[head // 2, :kr, :], dpad[head])

            live = {head: outer_product(head) for head in range(AHEAD)}
            grads = []
            for head in range(gp * 2):
                pair = head // 2
                product = live.pop(head)
                if head + AHEAD < gp * 2:
                    live[head + AHEAD] = outer_product(head + AHEAD)
                local = slice(head * HDIM, (head + 1) * HDIM)
                grad = (
                    ebuf[slot, head, :kr, :].astype(F32) * (product - inners[head])
                ).astype(BF16)
                grads.append(grad)
                dqt[local, here] = (nn(kt[local, :kr], grad) * SCALE).astype(BF16)
                if head % 2:
                    both = [ebuf[slot, h, :kr, :] for h in (head - 1, head)]
                    dv[pair, :kr, :] += nt(
                        jnp.concatenate(both, 1),
                        jnp.concatenate([dpad[head - 1], dpad[head]], 1),
                    )
                    dk[pair, :kr, :] += nt(
                        jnp.concatenate(grads[-2:], 1),
                        jnp.concatenate([qpad[head - 1], qpad[head]], 1),
                    )
            return 0

        lax.fori_loop(0, n_tiles, step, 0)

    for_size(seq_rows, total, attend)
    if chained:
        fetch.wait()

    def send(chunk):
        here = pl.ds(pl.multiple_of(chunk * TILE, TILE), TILE)
        return pltpu.make_async_copy(proj.at[here, :], proj_hbm.at[here, :], out_sem)

    def finish(chunk, sums):
        here = pl.ds(pl.multiple_of(chunk * TILE, TILE), TILE)
        parts = [dqt[:, here].T]
        parts += [(dk[pair, here, :] * LN2).astype(BF16) for pair in range(gp)]
        parts += [dv[pair, here, :].astype(BF16) for pair in range(gp)]
        grad = jnp.concatenate(parts, 1)
        proj[here, :] = grad
        send(chunk).start()
        acc[...] += tn(rows[here, :], grad)
        return sums + col_sum(grad.astype(F32))

    sums = lax.fori_loop(0, chunks, finish, jnp.zeros((1, width), F32))
    extra[MEM : MEM + 1, base : base + gcols] += sums[:, :gcols]
    extra[MEM + 1 : MEM + 2, base : base + gcols] += sums[:, 2 * gcols :]
    turned = (
        lax.broadcasted_iota(jnp.int32, (32, TILE), 1) + (edge - length)
        == lax.broadcasted_iota(jnp.int32, (32, TILE), 0)
    )
    turned = jnp.logical_and(turned, lax.broadcasted_iota(jnp.int32, (32, TILE), 0) < MEM)
    turned = jnp.where(turned, 1.0, 0.0).astype(BF16)
    found_k = jnp.concatenate([dk[pair, fix, :] * LN2 for pair in range(gp)], 1)
    found_v = jnp.concatenate([dv[pair, fix, :] for pair in range(gp)], 1)
    grad_memory = nt(nn(turned, found_k.astype(BF16)).astype(BF16), wk_ref[...])
    grad_memory += nt(nn(turned, found_v.astype(BF16)).astype(BF16), wv_ref[...])
    extra[...] += grad_memory

    if last:
        me = me_ref[0]
        part, few = D // shards, 32 // shards
        if closing:
            for s in range(shards):
                table[s, :few, :] = extra[s * few : (s + 1) * few]
        for m, piece, row in piece_spots(pieces, shards, part):
            spot = slice(row, row + part)
            at = pl.multiple_of((me ^ m) * part, part)
            piece[spot, :width] = acc[pl.ds(at, part), :].astype(BF16)
            if closing:
                mine_rows = table[me ^ m]
                lanes = [mine_rows[:, j : j + 128] for j in range(0, D, 128)]
                empty = part - mine_rows.shape[0] * len(lanes)
                if empty:
                    lanes.append(jnp.zeros((empty, 128), F32))
                piece[spot, width:] = jnp.concatenate(lanes, 0).astype(BF16)
    else:
        store = pltpu.make_async_copy(acc, acc_hbm, acc_sem)
        store.start()
        store.wait()
    if extra_ref is not None:
        extra_ref[...] = extra[...]

    def drain(chunk, _):
        send(chunk).wait()
        return 0

    lax.fori_loop(0, chunks, drain, 0)


def attention_backward(
    seq, group, groups, shards, lengths, me, w_qkv, vectors, x, dot, qt, mixt, expo,
    chain=(), others=(), after=(),
):
    seq_rows = x.shape[1]
    top = key_sizes(seq_rows)[-1]
    padded = cdiv(seq_rows + MEM, TILE) * TILE
    gp = PAIRS // groups
    gcols = gp * 128
    width = 3 * gcols
    vm = pl.BlockSpec(memory_space=pltpu.VMEM)
    hbm = pl.BlockSpec(memory_space=pl.ANY)
    smem = pl.BlockSpec(memory_space=pltpu.SMEM)
    out_shape = [jax.ShapeDtypeStruct((padded, width), BF16)]
    out_specs = [hbm]
    if chain:
        wide = width + (128 if others else 0)
        out_shape += [jax.ShapeDtypeStruct((D // 2, wide), BF16)] * 2
        out_specs += [vm] * 2
    else:
        out_shape += [jax.ShapeDtypeStruct((D, width), F32)]
        out_specs += [hbm]
    if not others:
        out_shape += [jax.ShapeDtypeStruct((32, D), F32)]
        out_specs += [vm]
    out_shape += [jax.ShapeDtypeStruct((8, 128), F32)]
    out_specs += [vm]
    return pl.pallas_call(
        partial(
            bwd_kernel, seq_rows, groups, group, seq, shards, bool(chain), len(others),
            len(after),
        ),
        out_shape=tuple(out_shape),
        grid=(1,),
        in_specs=[
            smem,
            smem,
            pl.BlockSpec((D, gcols), lambda i: (0, groups + group)),
            pl.BlockSpec((D, gcols), lambda i: (0, 2 * groups + group)),
            vm,
        ]
        + [hbm] * 5
        + ([hbm, vm] if chain else [])
        + [vm] * len(others)
        + [hbm] * len(after),
        out_specs=tuple(out_specs),
        scratch_shapes=[
            pltpu.VMEM((padded, D), BF16),
            pltpu.VMEM((gcols, seq_rows), BF16),
            pltpu.VMEM((gcols, seq_rows), BF16),
            pltpu.VMEM((gcols, seq_rows), BF16),
            pltpu.VMEM((gcols, D), BF16),
            pltpu.VMEM((gcols, padded), BF16),
            pltpu.VMEM((gp, padded, 128), BF16),
            pltpu.VMEM((gp * 2, 128, TILE), BF16),
            pltpu.VMEM((gp * 2, 128, TILE), BF16),
            pltpu.VMEM((gcols, padded), BF16),
            pltpu.VMEM((gp, padded, 128), F32),
            pltpu.VMEM((gp, padded, 128), F32),
            pltpu.VMEM((2, gp * 2, top, TILE), BF16),
            pltpu.VMEM((D, width), F32),
            pltpu.VMEM((padded, width), BF16),
            pltpu.VMEM((32, D), F32),
            pltpu.VMEM((shards, max(8, 32 // shards), D), F32),
            pltpu.SemaphoreType.DMA((2,)),
            pltpu.SemaphoreType.DMA((4,)),
            pltpu.SemaphoreType.DMA,
            pltpu.SemaphoreType.DMA,
        ],
        compiler_params=pltpu.CompilerParams(vmem_limit_bytes=VMEM_LIMIT),
        cost_estimate=pl.CostEstimate(
            flops=8 * 10**9, bytes_accessed=15 * 10**6, transcendentals=0
        ),
        name="attention_backward",
    )(lengths, me, w_qkv, w_qkv, vectors, x, dot, qt, mixt, expo, *chain, *others, *after)


def input_kernel(seq_rows, groups, seq, len_ref, w_ref, gh_hbm, *refs):
    projs = refs[:groups]
    gx_ref, token, gh, blocks, sems = refs[-5:]
    token[...] = jnp.zeros(token.shape, F32)
    gcols = D // groups
    length = len_ref[seq]
    chunks = cdiv(length, TILE)

    def fetch(chunk):
        here = pl.ds(pl.multiple_of(chunk * TILE, TILE), TILE)
        slot = lax.rem(chunk, 2)
        return [
            pltpu.make_async_copy(gh_hbm.at[seq, here, :], gh.at[slot], sems.at[slot, 0])
        ] + [
            pltpu.make_async_copy(p.at[here, :], blocks.at[slot, i], sems.at[slot, 1 + i])
            for i, p in enumerate(projs)
        ]

    for copy in fetch(0):
        copy.start()
    gx_ref[...] = jnp.zeros(gx_ref.shape, BF16)

    def step(chunk, _):
        start = pl.multiple_of(chunk * TILE, TILE)
        slot = lax.rem(chunk, 2)

        @pl.when(chunk + 1 < chunks)
        def _():
            for copy in fetch(chunk + 1):
                copy.start()

        for copy in fetch(chunk):
            copy.wait()
        joint = jnp.concatenate(
            [
                blocks[slot, g, :, kind * gcols : (kind + 1) * gcols]
                for kind in range(3)
                for g in range(groups)
            ],
            1,
        )
        grad = nt(joint, w_ref[...])
        row = lax.broadcasted_iota(jnp.int32, (TILE, 1), 0) + start
        gx_ref[0, pl.ds(start, TILE), :] = jnp.where(
            row < length, grad + gh[slot].astype(F32), 0.0
        ).astype(BF16)
        return 0

    lax.fori_loop(0, chunks, step, 0)


def input_gradient(seq, lengths, w_qkv, gh, projs, after=(), base=None):
    count, seq_rows = gh.shape[:2]
    groups = len(projs)
    hbm = pl.BlockSpec(memory_space=pl.ANY)
    base = () if base is None else (base,)
    return pl.pallas_call(
        partial(input_kernel, seq_rows, groups, seq),
        out_shape=(
            jax.ShapeDtypeStruct((count, seq_rows, D), BF16),
            jax.ShapeDtypeStruct((8, 128), F32),
        ),
        grid=(1,),
        in_specs=[
            pl.BlockSpec(memory_space=pltpu.SMEM),
            pl.BlockSpec(memory_space=pltpu.VMEM),
        ]
        + [hbm] * (1 + groups + len(after) + len(base)),
        out_specs=(
            pl.BlockSpec((1, seq_rows, D), lambda i: (seq, 0, 0)),
            pl.BlockSpec(memory_space=pltpu.VMEM),
        ),
        input_output_aliases={3 + groups + len(after): 0} if base else {},
        scratch_shapes=[
            pltpu.VMEM((2, TILE, D), BF16),
            pltpu.VMEM((2, groups, TILE, 3 * D // groups), BF16),
            pltpu.SemaphoreType.DMA((2, 1 + groups)),
        ],
        compiler_params=pltpu.CompilerParams(vmem_limit_bytes=VMEM_LIMIT),
        cost_estimate=pl.CostEstimate(
            flops=2 * 10**9, bytes_accessed=7 * 10**6, transcendentals=0
        ),
        name="input_gradient",
    )(lengths, w_qkv, gh, *projs, *after, *base)


GROUPS = 2


def powers(size):
    return [1 << i for i in range(size.bit_length() - 1)]


def exchange(value, axis, size, bit):
    return lax.ppermute(value, axis, [(i, i ^ bit) for i in range(size)])


def far_pieces(value, axis, size):
    pieces = {0: value}
    for bit in reversed(powers(size)[1:]):
        for mask in sorted(pieces):
            pieces[mask | bit] = exchange(pieces[mask], axis, size, bit)
    return pieces


def near_pieces(pieces, axis, size):
    pieces = dict(pieces)
    for mask in sorted(pieces):
        pieces[mask | 1] = exchange(pieces[mask], axis, size, 1)
    return [pieces[mask] for mask in range(size)]


def held_until(pieces, event):
    keys = list(pieces)
    return dict(zip(keys, lax.optimization_barrier((*[pieces[k] for k in keys], event))))


def combine_kernel(counts, modes, waits, place_ref, *refs):
    refs = list(refs)
    arrays = [[[refs.pop(0) for _ in range(c)] for c in group] for group in counts]
    refs = refs[waits:]
    total, token = refs.pop(), refs.pop(-1)
    token[...] = jnp.zeros(token.shape, F32)
    place = place_ref[0]
    for groups, (mode, stacked, cols) in zip(arrays, modes):
        rows = 0
        for group in groups:
            more, wide = group[0].shape
            value = group[0][...].astype(F32)
            for other in group[1:]:
                value = value + other[...].astype(F32)
            total[rows : rows + more, :wide] = value
            if wide < cols:
                total[rows : rows + more, wide:cols] = jnp.zeros((more, cols - wide), F32)
            rows += more
        if mode == "halves":
            refs.pop(0)[...] = total[: rows // 2, :cols].astype(BF16)
            refs.pop(0)[...] = total[rows // 2 : rows, :cols].astype(BF16)
        elif mode == "parts":
            one = rows // stacked
            part = one // GROUP
            for m in range(GROUP):
                target = refs.pop(0)
                at = pl.multiple_of((place ^ m) * part, part)
                for i in range(stacked):
                    target[i * part : (i + 1) * part, :] = total[
                        pl.ds(at + i * one, part), :cols
                    ].astype(BF16)
        else:
            refs.pop(0)[...] = total[:rows, :cols].astype(BF16)


def combine(place, items, after):
    vm = pl.BlockSpec(memory_space=pltpu.VMEM)
    shapes, flat, modes, most = [], [], [], 0
    for groups, mode, stacked in items:
        rows = sum(arrays[0].shape[0] for arrays in groups)
        cols = max(arrays[0].shape[1] for arrays in groups)
        flat += [a for arrays in groups for a in arrays]
        modes.append((mode, stacked, cols))
        most = max(most, rows)
        if mode == "halves":
            shapes += [(rows // 2, cols)] * 2
        elif mode == "parts":
            shapes += [(rows // GROUP, cols)] * GROUP
        else:
            shapes += [(rows, cols)]
    size = sum(a.size for a in flat) * 2
    outs = pl.pallas_call(
        partial(combine_kernel, [[len(g) for g in i[0]] for i in items], modes, len(after)),
        out_shape=tuple(jax.ShapeDtypeStruct(s, BF16) for s in shapes)
        + (jax.ShapeDtypeStruct((8, 128), F32),),
        in_specs=[pl.BlockSpec(memory_space=pltpu.SMEM)]
        + [vm] * len(flat)
        + [pl.BlockSpec(memory_space=pl.ANY)] * len(after),
        out_specs=(vm,) * (len(shapes) + 1),
        scratch_shapes=[pltpu.VMEM((most, max(m[2] for m in modes)), F32)],
        compiler_params=pltpu.CompilerParams(vmem_limit_bytes=24 * 2**20),
        cost_estimate=pl.CostEstimate(flops=size, bytes_accessed=2 * size, transcendentals=0),
        name="combine",
    )(place, *flat, *after)
    outs, token, results = list(outs[:-1]), outs[-1], []
    for mode, _, _ in modes:
        taken = {"halves": 2, "parts": GROUP, "whole": 1}[mode]
        results.append([outs.pop(0) for _ in range(taken)])
    return results, token


GROUP = 4


class Stream:
    def __init__(self, value, sizes, steps, stacked=None):
        self.value, self.steps = list(value), list(steps)
        self.reps, self.shards = sizes
        self.stacked = stacked or max(self.shards // 2, 1)

    def exchange(self):
        kind, bit = self.steps.pop(0)
        value = self.value
        if kind == "fold":
            arrays = [value[0], exchange(value[1], "shard", self.shards, bit)]
        elif kind == "group":
            arrays = [value[0]] + [
                exchange(value[j], "rep", self.reps, j) for j in range(1, GROUP)
            ]
        else:
            arrays = [value[0], exchange(value[0], "rep", self.reps, bit)]
        follow = self.steps[0][0] if self.steps else "end"
        item = ([arrays], {"fold": "halves", "group": "parts"}.get(follow, "whole"), self.stacked)
        if follow == "fold":
            self.stacked //= 2
        return item

    def alone(self, place, after=()):
        (self.value,), token = combine(place, [self.exchange()], after)
        return [token]


def advance(place, streams, items, after):
    results, token = combine(place, items, after)
    for stream, result in zip(streams, results):
        stream.value = result
    return [token]


def whole_parts(stream):
    own = stream.value[0]
    return [own] + [exchange(own, "rep", stream.reps, j) for j in range(1, GROUP)]


def spread_kernel(shards, place_ref, *refs):
    refs = list(refs)
    arrays = [[refs.pop(0) for _ in range(GROUP)] for _ in range(3)]
    qkv_ref, out_ref, in_ref, back_ref, vec_ref, table = refs
    place = place_ref[0]

    def put(target, parts, cols, first=0, count=None):
        part = count or parts[0].shape[0]
        for m in range(GROUP):
            at = pl.multiple_of((place ^ m) * part, part)
            target[pl.ds(at, part), :cols] = parts[m][first : first + part, :].astype(F32)

    part = D // shards
    put(back_ref, arrays[1], D)
    put(table, arrays[0], D)
    out_ref[...] = table[:part, :D]
    for j in range(BLOCKS):
        in_ref[:, j * D : (j + 1) * D] = table[(1 + j) * part : (2 + j) * part, :D]
    gcols = D // GROUPS
    for g in range(GROUPS):
        put(table, arrays[2], 3 * gcols + 128, g * part // GROUP, part // GROUP)
        for kind in range(3):
            at = kind * D + g * gcols
            qkv_ref[:, at : at + gcols] = table[:part, kind * gcols : (kind + 1) * gcols]
    few = 32 // shards
    width = 3 * gcols
    step = max(8, few)
    for j in range(D // 128):
        vec_ref[:, j * 128 : (j + 1) * 128] = table[j * step : j * step + few, width : width + 128]


def spread(place, shards, parts):
    part = D // shards
    vm = pl.BlockSpec(memory_space=pltpu.VMEM)
    shapes = ((part, 3 * D), (part, D), (part, FF), (FF // shards, D), (32 // shards, D))
    most = max(part * (1 + BLOCKS), part), max(p.shape[1] for p in parts)
    return pl.pallas_call(
        partial(spread_kernel, shards),
        out_shape=tuple(jax.ShapeDtypeStruct(s, F32) for s in shapes),
        in_specs=[pl.BlockSpec(memory_space=pltpu.SMEM)] + [vm] * len(parts),
        out_specs=(vm,) * len(shapes),
        scratch_shapes=[pltpu.VMEM(most, F32)],
        compiler_params=pltpu.CompilerParams(vmem_limit_bytes=24 * 2**20),
        name="spread",
    )(place, *parts)


def body(sizes, inputs, lengths, w_qkv, w_out, w_in, w_back, vectors, cotangent):
    reps, shards = sizes
    count = inputs.shape[0]
    me = lax.axis_index("shard").astype(jnp.int32).reshape(1)

    axis = ("shard", shards)
    far = far_pieces(pack(w_qkv, vectors), *axis)
    start = held_until(
        {0: jnp.concatenate([w_out, w_in], 1), 1: w_back}, far[max(far)]
    )
    far_up, far_back = far_pieces(start[0], *axis), far_pieces(start[1], *axis)
    whole, wqt, wvt, table = prepare(me, near_pieces(far, *axis))
    fwd = [
        attention_forward(s, lengths, inputs, whole, wqt, wvt, table) for s in range(count)
    ]
    far_up, far_back = held_until(far_up, fwd[-1][3]), held_until(far_back, fwd[-1][3])
    out, gh, dot, *grads, sums = feed_forward(
        lengths, me, inputs, cotangent, [f[2] for f in fwd], [f[3] for f in fwd],
        near_pieces(far_up, *axis), near_pieces(far_back, *axis), table,
    )
    place = (lax.axis_index("rep") % GROUP).astype(jnp.int32).reshape(1)
    folds = [("fold", bit) for bit in powers(shards)]
    group = [("group", 0)]
    rest = [("full", bit) for bit in powers(reps) if bit >= GROUP]
    tall = Stream(grads[:2], sizes, folds + group + rest)
    deep = Stream(grads[2:], sizes, folds[:1] + group + folds[1:] + rest)
    projs = [[None] * GROUPS for _ in range(count)]
    quarters = [None] * GROUPS
    extras, after, calls = [], [], []
    for g in range(GROUPS):
        chain = ()
        for s in range(count):
            closing = [sums] + extras if s == count - 1 and g == GROUPS - 1 else ()
            busy = [
                (tall, deep), (tall, deep), (tall, quarters[0]), (deep, quarters[0], tall)
            ][len(calls)]
            items = [stream.exchange() for stream in busy]
            res = attention_backward(
                s, g, GROUPS, shards, lengths, me, whole, table, inputs, dot, fwd[s][1],
                fwd[s][2], fwd[s][0], chain, closing, after,
            )
            after = advance(place, busy, items, [res[-1]])
            projs[s][g] = res[0]
            calls.append(res)
            chain = res[1:-1]
        quarters[g] = Stream(chain[:2], sizes, folds + [("stop", 0)])
        extras += chain[2:]
    early, last = quarters
    last.value[1] = last.value[1] + after[0][0, 0].astype(BF16)
    for stream, left in ((early, 1), (tall, 0), (deep, 1)):
        while len(stream.steps) > left:
            stream.alone(place)
    tall_parts = whole_parts(tall)
    end = deep.exchange()
    after = []
    while len(last.steps) > 2:
        after = last.alone(place)
    gx, token = input_gradient(0, lengths, whole, gh, projs[0], after)
    final = last.exchange()[0]
    both = Stream([], sizes, group + rest, stacked=GROUPS)
    after = advance(
        place, [both, deep], [([early.value] + final, "parts", GROUPS), end], [token]
    )
    for seq in range(1, count):
        gx, token = input_gradient(seq, lengths, whole, gh, projs[seq], after, gx)
    both.alone(place, [token] + tall_parts[1:])
    deep_parts = whole_parts(deep)
    while both.steps:
        both.alone(place)
    return (out, gx, *spread(place, shards, tall_parts + deep_parts + whole_parts(both)))


def solution(mesh):
    data = P(("rep", "shard"), None, None)
    rows = P("shard", None)
    return jax.shard_map(
        partial(body, (mesh.shape["rep"], mesh.shape["shard"])),
        mesh=mesh,
        in_specs=(data, P(("rep", "shard")), rows, rows, rows, rows, rows, data),
        out_specs=(data, data, rows, rows, rows, rows, rows),
        check_vma=False,
    )
```

profile of v0, /device:TPU:0, one launch (start us, length us, event | category | flops | bytes accessed | tf_op | source)
XLA Modules:
  0.0 269.2 jit_solution(8285456465943268715)
XLA Ops:
  1.7 3.0 %collective-permute-start.1 = (bf16[144,1536]{1,0:T(8,128)(2,1)S(1)}, bf16[144,1536]{1,0:T(8,128)(2,1)S(1)}, u32[]{:S(2)}, u32[]{:S(2)}) collective-permute-start(bf16[144,1536]{1,0:T(8,128)(2,1)S(1)} %fusion.1.refs_0_), channel_id=1, source_target_pairs={{0,2},{1,3},{2,0},{3,1},{4,6},{5,7},{6,4},{7,5},{8,10},{9,11},{10,... | collective-permute-start | bytes 1327112 | tf_op jit(solution)/shard_map/ppermute | solution.py:977
  4.7 10.2 %collective-permute-done.1.refs_2_ = bf16[144,1536]{1,0:T(8,128)(2,1)S(1)} collective-permute-done((bf16[144,1536]{1,0:T(8,128)(2,1)S(1)}, bf16[144,1536]{1,0:T(8,128)(2,1)S(1)}, u32[]{:S(2)}, u32[]{:S(2)}) %collective-permute-start.1) | collective-permute-done | bytes 442400 | tf_op jit(solution)/shard_map/ppermute | solution.py:977
  22.6 8.5 %attention_forward.3 = (bf16[4,8,1056,256]{3,2,1,0:T(8,128)(2,1)}, bf16[512,1024]{1,0:T(8,128)(2,1)}, bf16[512,1024]{1,0:T(8,128)(2,1)}, f32[8,1024]{1,0:T(8,128)}) custom-call(s32[2]{0:T(128)} %len_ref.9, bf16[2,1024,512]{2,1,0:T(8,128)(2,1)} %refs_5_.7, bf16[512,1536]{1,0:T(8,128)(2,1)} %copy-done, bf16[512,512]{1,0:T(8,128)(2,1)} %copy-done.19, ...), custom_call_target="tpu_custom_call" | custom-call | flops 8000000000 | bytes 24000000 | tf_op jit(solution)/shard_map/attention_forward/pallas_call | solution.py:265
  33.2 11.4 %collective-permute-done.3.refs_2_ = bf16[128,2560]{1,0:T(8,128)(2,1)S(1)} collective-permute-done((bf16[128,2560]{1,0:T(8,128)(2,1)S(1)}, bf16[128,2560]{1,0:T(8,128)(2,1)S(1)}, u32[]{:S(2)}, u32[]{:S(2)}) %collective-permute-start.3) | collective-permute-done | bytes 655392 | tf_op jit(solution)/shard_map/ppermute | solution.py:977
  45.2 21.3 %attention_forward.2 = (bf16[4,8,1056,256]{3,2,1,0:T(8,128)(2,1)}, bf16[512,1024]{1,0:T(8,128)(2,1)}, bf16[512,1024]{1,0:T(8,128)(2,1)}, f32[8,1024]{1,0:T(8,128)}) custom-call(s32[2]{0:T(128)} %len_ref.9, bf16[2,1024,512]{2,1,0:T(8,128)(2,1)} %refs_5_.7, bf16[512,1536]{1,0:T(8,128)(2,1)} %copy-done, bf16[512,512]{1,0:T(8,128)(2,1)} %copy-done.19, ...), custom_call_target="tpu_custom_call" | custom-call | flops 8000000000 | bytes 24000000 | tf_op jit(solution)/shard_map/attention_forward/pallas_call | solution.py:265
  66.5 47.3 %feed_forward.1 = (bf16[2,1024,512]{2,1,0:T(8,128)(2,1)}, bf16[2,1024,512]{2,1,0:T(8,128)(2,1)}, bf16[2,512,1024]{2,1,0:T(8,128)(2,1)}, bf16[1280,512]{1,0:T(8,1...) custom-call(s32[2]{0:T(128)} %len_ref.9, ...), custom_call_target="tpu_custom_call" | custom-call | flops 27000000512 | bytes 24000000 | tf_op jit(solution)/shard_map/feed_forward/pallas_call | solution.py:554
  113.8 3.6 %collective-permute-start.9 = (bf16[1280,512]{1,0:T(8,128)(2,1)}, bf16[1280,512]{1,0:T(8,128)(2,1)}, u32[]{:S(2)}, u32[]{:S(2)}) collective-permute-start(bf16[1280,512]{1,0:T(8,128)(2,1)} %get-tuple-element.116), channel_id=1, source_target_pairs={{0,1},{1,0},{2,3},{3,2},{4,5},{5,4},{6,7},{7,6},{8,9},{9,8},{10,11... | collective-permute-start | bytes 3932168 | tf_op jit(solution)/shard_map/ppermute | solution.py:977
  117.5 17.5 %attention_backward.4 = (bf16[1280,768]{1,0:T(8,128)(2,1)}, f32[512,768]{1,0:T(8,128)}, f32[32,512]{1,0:T(8,128)}, f32[8,128]{1,0:T(8,128)}) custom-call(s32[2]{0:T(128)} %len_ref.9, s32[1]{0:T(128)} %bitcast.me_ref.refs_1_, bf16[512,1536]{1,0:T(8,128)(2,1)} %copy-done, bf16[512,1536]{1,0:T(8,128)(2,1)} %copy-done, bf16[32,512]{1,0:T(8,128)(2,1)} %copy-done.21, ...), custom_call_target="tpu_custom_call" | custom-call | flops 8000000000 | bytes 15000000 | tf_op jit(solution)/shard_map/attention_backward/pallas_call | solution.py:833
  137.0 3.6 %combine.8 = (bf16[640,512]{1,0:T(8,128)(2,1)S(1)}, bf16[640,512]{1,0:T(8,128)(2,1)}, bf16[256,512]{1,0:T(8,128)(2,1)S(1)}, bf16[256,512]{1,0:T(8,128)(2,1)}, bf...) custom-call(s32[1]{0:T(128)} %bitcast.1.place_ref, bf16[1280,512]{1,0:T(8,128)(2,1)S(1)} %copy-done.1, ...), custom_call_target="tpu_custom_call" | custom-call | flops 4718592 | bytes 9437184 | tf_op jit(solution)/shard_map/combine/pallas_call | solution.py:1051
  141.4 13.2 %collective-permute-start.13 = (bf16[256,512]{1,0:T(8,128)(2,1)}, bf16[256,512]{1,0:T(8,128)(2,1)}, u32[]{:S(2)}, u32[]{:S(2)}) collective-permute-start(bf16[256,512]{1,0:T(8,128)(2,1)} %get-tuple-element.126), channel_id=1, source_target_pairs={{0,8},{4,12},{8,0},{12,4},{16,24},{20,28},{24,16},{28,20},{1,9},{5... | collective-permute-start | bytes 786440 | tf_op jit(solution)/shard_map/ppermute | solution.py:977
  156.7 6.7 %attention_backward.5 = (bf16[1280,768]{1,0:T(8,128)(2,1)}, bf16[256,768]{1,0:T(8,128)(2,1)}, bf16[256,768]{1,0:T(8,128)(2,1)}, f32[32,512]{1,0:T(8,128)}, f32[8,128]{1,0:T(8,128)}) custom-call(s32[2]{0:T(128)} %len_ref.9, s32[1]{0:T(128)} %bitcast.me_ref.refs_1_, bf16[512,1536]{1,0:T(8,128)(2,1)} %copy-done, bf16[512,1536]{1,0:T(8,128)(2,1)} %copy-done, ...), custom_call_target="tpu_custom_call" | custom-call | flops 8000000000 | bytes 15000000 | tf_op jit(solution)/shard_map/attention_backward/pallas_call | solution.py:833
  165.5 6.7 %collective-permute-done.11.refs_1_ = bf16[640,512]{1,0:T(8,128)(2,1)S(1)} collective-permute-done((bf16[640,512]{1,0:T(8,128)(2,1)}, bf16[640,512]{1,0:T(8,128)(2,1)S(1)}, u32[]{:S(2)}, u32[]{:S(2)}) %collective-permute-start.11) | collective-permute-done | bytes 655392 | tf_op jit(solution)/shard_map/ppermute | solution.py:977
  172.9 2.2 combine.9
  180.2 17.3 %attention_backward.6 = (bf16[1280,768]{1,0:T(8,128)(2,1)}, f32[512,768]{1,0:T(8,128)}, f32[32,512]{1,0:T(8,128)}, f32[8,128]{1,0:T(8,128)}) custom-call(s32[2]{0:T(128)} %len_ref.9, s32[1]{0:T(128)} %bitcast.me_ref.refs_1_, bf16[512,1536]{1,0:T(8,128)(2,1)} %copy-done, bf16[512,1536]{1,0:T(8,128)(2,1)} %copy-done, bf16[32,512]{1,0:T(8,128)(2,1)} %copy-done.21, ...), custom_call_target="tpu_custom_call" | custom-call | flops 8000000000 | bytes 15000000 | tf_op jit(solution)/shard_map/attention_backward/pallas_call | solution.py:833
  201.6 6.9 %attention_backward.7 = (bf16[1280,768]{1,0:T(8,128)(2,1)}, bf16[256,896]{1,0:T(8,128)(2,1)}, bf16[256,896]{1,0:T(8,128)(2,1)}, f32[8,128]{1,0:T(8,128)}) custom-call(s32[2]{0:T(128)} %len_ref.9, s32[1]{0:T(128)} %bitcast.me_ref.refs_1_, bf16[512,1536]{1,0:T(8,128)(2,1)} %copy-done, bf16[512,1536]{1,0:T(8,128)(2,1)} %copy-done, bf16[32,512]{1,0:T(8,128)(2,1)} %copy-done.21, ...), custom_call_target="tpu_custom_call" | custom-call | flops 8000000000 | bytes 15000000 | tf_op jit(solution)/shard_map/attention_backward/pallas_call | solution.py:833
  216.2 5.0 %collective-permute-start.23 = (bf16[128,896]{1,0:T(8,128)(2,1)S(1)}, bf16[128,896]{1,0:T(8,128)(2,1)S(1)}, u32[]{:S(2)}, u32[]{:S(2)}) collective-permute-start(bf16[128,896]{1,0:T(8,128)(2,1)S(1)} %get-tuple-element.154), channel_id=1, source_target_pairs={{0,2},{1,3},{2,0},{3,1},{4,6},{5,7},{6,4},{7,5},{8,10},{9,11},{10,... | collective-permute-start | bytes 688136 | tf_op jit(solution)/shard_map/ppermute | solution.py:977
  221.2 3.3 %collective-permute-start.27 = (bf16[160,512]{1,0:T(8,128)(2,1)S(1)}, bf16[160,512]{1,0:T(8,128)(2,1)S(1)}, u32[]{:S(2)}, u32[]{:S(2)}) collective-permute-start(bf16[160,512]{1,0:T(8,128)(2,1)S(1)} %get-tuple-element.163.refs_0_), channel_id=1, source_target_pairs={{0,12},{4,8},{8,4},{12,0},{16,28},{20,24},{24,20},{28,16},{1,13},{... | collective-permute-start | bytes 491528 | tf_op jit(solution)/shard_map/ppermute | solution.py:977
  226.9 5.1 %collective-permute-start.24 = (bf16[128,512]{1,0:T(8,128)(2,1)S(1)}, bf16[128,512]{1,0:T(8,128)(2,1)S(1)}, u32[]{:S(2)}, u32[]{:S(2)}) collective-permute-start(bf16[128,512]{1,0:T(8,128)(2,1)S(1)} %get-tuple-element.155.refs_3_), channel_id=1, source_target_pairs={{0,16},{4,20},{8,24},{12,28},{16,0},{20,4},{24,8},{28,12},{1,17},{... | collective-permute-start | bytes 393224 | tf_op jit(solution)/shard_map/ppermute | solution.py:977
  232.0 6.7 %input_gradient.2 = (bf16[2,1024,512]{2,1,0:T(8,128)(2,1)}, f32[8,128]{1,0:T(8,128)}) custom-call(s32[2]{0:T(128)} %len_ref.9, bf16[512,1536]{1,0:T(8,128)(2,1)} %copy-done, bf16[2,1024,512]{2,1,0:T(8,128)(2,1)} %get-tuple-element.107.gh_hbm, bf16[1280,768]{1,0:T(8,128)(2,1)} %get-tuple-element.156.refs_0_, bf16[1280,768]{1,0:T(8,128)(2,1)} %get-tuple-element.157.refs_1_, ...), custom_call_target="tpu_custom_call" | custom-call | flops 2000000000 | bytes 7000000 | tf_op jit(solution)/shard_map/input_gradient/pallas_call | solution.py:939
  240.9 3.5 %collective-permute-start.32 = (bf16[64,896]{1,0:T(8,128)(2,1)}, bf16[64,896]{1,0:T(8,128)(2,1)S(1)}, u32[]{:S(2)}, u32[]{:S(2)}) collective-permute-start(bf16[64,896]{1,0:T(8,128)(2,1)} %get-tuple-element.167), channel_id=1, source_target_pairs={{0,8},{4,12},{8,0},{12,4},{16,24},{20,28},{24,16},{28,20},{1,9},{5... | collective-permute-start | bytes 344072 | tf_op jit(solution)/shard_map/ppermute | solution.py:977
  244.4 2.9 %collective-permute-start.30 = (bf16[128,512]{1,0:T(8,128)(2,1)S(1)}, bf16[128,512]{1,0:T(8,128)(2,1)S(1)}, u32[]{:S(2)}, u32[]{:S(2)}) collective-permute-start(bf16[128,512]{1,0:T(8,128)(2,1)S(1)} %get-tuple-element.164.refs_4_), channel_id=1, source_target_pairs={{0,12},{4,8},{8,4},{12,0},{16,28},{20,24},{24,20},{28,16},{1,13},{... | collective-permute-start | bytes 393224 | tf_op jit(solution)/shard_map/ppermute | solution.py:977
  247.3 4.2 %input_gradient.3 = (bf16[2,1024,512]{2,1,0:T(8,128)(2,1)}, f32[8,128]{1,0:T(8,128)}) custom-call(s32[2]{0:T(128)} %len_ref.9, bf16[512,1536]{1,0:T(8,128)(2,1)} %copy-done, bf16[2,1024,512]{2,1,0:T(8,128)(2,1)} %get-tuple-element.107.gh_hbm, bf16[1280,768]{1,0:T(8,128)(2,1)} %get-tuple-element.121.refs_0_, ...), custom_call_target="tpu_custom_call", output_to_operand_aliasing={{0}: (6, {})} | custom-call | flops 2000000000 | bytes 7000000 | tf_op jit(solution)/shard_map/input_gradient/pallas_call | solution.py:939
  256.1 2.6 collective-permute-done.34.refs_1_
  259.3 2.5 collective-permute-start.37
  (130 shorter events, 52.4 us)
Async XLA Ops:
  1.7 13.2 %collective-permute-start.1 = (bf16[144,1536]{1,0:T(8,128)(2,1)S(1)}, bf16[144,1536]{1,0:T(8,128)(2,1)S(1)}, u32[]{:S(2)}, u32[]{:S(2)}) collective-permute-start(bf16[144,1536]{1,0:T(8,128)(2,1)S(1)} %fusion.1.refs_0_), channel_id=1, source_target_pairs={{0,2},{1,3},{2,0},{3,1},{4,6},{5,7},{6,4},{7,5},{8,10},{9,11},{10,... | collective-permute-start | bytes 1327112 | tf_op jit(solution)/shard_map/ppermute | solution.py:977
  4.7 13.4 %collective-permute-start = (bf16[144,1536]{1,0:T(8,128)(2,1)S(1)}, bf16[144,1536]{1,0:T(8,128)(2,1)S(1)}, u32[]{:S(2)}, u32[]{:S(2)}) collective-permute-start(bf16[144,1536]{1,0:T(8,128)(2,1)S(1)} %fusion.1.refs_0_), channel_id=1, source_target_pairs={{0,1},{1,0},{2,3},{3,2},{4,5},{5,4},{6,7},{7,6},{8,9},{9,8},{10,11... | collective-permute-start | bytes 1327112 | tf_op jit(solution)/shard_map/ppermute | solution.py:977
  16.0 15.1 %collective-permute-start.6 = (bf16[512,512]{1,0:T(8,128)(2,1)}, bf16[512,512]{1,0:T(8,128)(2,1)}, u32[]{:S(2)}, u32[]{:S(2)}) collective-permute-start(bf16[512,512]{1,0:T(8,128)(2,1)} %refs_4_), channel_id=1, source_target_pairs={{0,2},{1,3},{2,0},{3,1},{4,6},{5,7},{6,4},{7,5},{8,10},{9,11},{10,... | collective-permute-start | bytes 1572872 | tf_op jit(solution)/shard_map/ppermute | solution.py:977
  17.8 26.9 %collective-permute-start.3 = (bf16[128,2560]{1,0:T(8,128)(2,1)S(1)}, bf16[128,2560]{1,0:T(8,128)(2,1)S(1)}, u32[]{:S(2)}, u32[]{:S(2)}) collective-permute-start(bf16[128,2560]{1,0:T(8,128)(2,1)S(1)} %pad_maximum_fusion.refs_0_), channel_id=1, source_target_pairs={{0,2},{1,3},{2,0},{3,1},{4,6},{5,7},{6,4},{7,5},{8,10},{9,11},{10,... | collective-permute-start | bytes 1966088 | tf_op jit(solution)/shard_map/ppermute | solution.py:977
  31.1 35.4 %collective-permute-start.7 = (bf16[512,512]{1,0:T(8,128)(2,1)}, bf16[512,512]{1,0:T(8,128)(2,1)}, u32[]{:S(2)}, u32[]{:S(2)}) collective-permute-start(bf16[512,512]{1,0:T(8,128)(2,1)} %refs_4_), channel_id=1, source_target_pairs={{0,1},{1,0},{2,3},{3,2},{4,5},{5,4},{6,7},{7,6},{8,9},{9,8},{10,11... | collective-permute-start | bytes 1572872 | tf_op jit(solution)/shard_map/ppermute | solution.py:977
  33.2 33.3 %collective-permute-start.8 = (bf16[512,512]{1,0:T(8,128)(2,1)}, bf16[512,512]{1,0:T(8,128)(2,1)}, u32[]{:S(2)}, u32[]{:S(2)}) collective-permute-start(bf16[512,512]{1,0:T(8,128)(2,1)} %collective-permute-done.6.refs_6_), channel_id=1, source_target_pairs={{0,1},{1,0},{2,3},{3,2},{4,5},{5,4},{6,7},{7,6},{8,9},{9,8},{10,11... | collective-permute-start | bytes 1572872 | tf_op jit(solution)/shard_map/ppermute | solution.py:977
  44.6 21.9 %collective-permute-start.4 = (bf16[128,2560]{1,0:T(8,128)(2,1)S(1)}, bf16[128,2560]{1,0:T(8,128)(2,1)}, u32[]{:S(2)}, u32[]{:S(2)}) collective-permute-start(bf16[128,2560]{1,0:T(8,128)(2,1)S(1)} %pad_maximum_fusion.refs_0_), channel_id=1, source_target_pairs={{0,1},{1,0},{2,3},{3,2},{4,5},{5,4},{6,7},{7,6},{8,9},{9,8},{10,11... | collective-permute-start | bytes 1966088 | tf_op jit(solution)/shard_map/ppermute | solution.py:977
  44.6 21.9 %collective-permute-start.5 = (bf16[128,2560]{1,0:T(8,128)(2,1)S(1)}, bf16[128,2560]{1,0:T(8,128)(2,1)}, u32[]{:S(2)}, u32[]{:S(2)}) collective-permute-start(bf16[128,2560]{1,0:T(8,128)(2,1)S(1)} %collective-permute-done.3.refs_2_), channel_id=1, source_target_pairs={{0,1},{1,0},{2,3},{3,2},{4,5},{5,4},{6,7},{7,6},{8,9},{9,8},{10,11... | collective-permute-start | bytes 1966088 | tf_op jit(solution)/shard_map/ppermute | solution.py:977
  113.8 21.3 %collective-permute-start.9 = (bf16[1280,512]{1,0:T(8,128)(2,1)}, bf16[1280,512]{1,0:T(8,128)(2,1)}, u32[]{:S(2)}, u32[]{:S(2)}) collective-permute-start(bf16[1280,512]{1,0:T(8,128)(2,1)} %get-tuple-element.116), channel_id=1, source_target_pairs={{0,1},{1,0},{2,3},{3,2},{4,5},{5,4},{6,7},{7,6},{8,9},{9,8},{10,11... | collective-permute-start | bytes 3932168 | tf_op jit(solution)/shard_map/ppermute | solution.py:977
  117.5 17.6 %collective-permute-start.10 = (bf16[1024,512]{1,0:T(8,128)(2,1)}, bf16[1024,512]{1,0:T(8,128)(2,1)}, u32[]{:S(2)}, u32[]{:S(2)}) collective-permute-start(bf16[1024,512]{1,0:T(8,128)(2,1)} %get-tuple-element.118), channel_id=1, source_target_pairs={{0,1},{1,0},{2,3},{3,2},{4,5},{5,4},{6,7},{7,6},{8,9},{9,8},{10,11... | collective-permute-start | bytes 3145736 | tf_op jit(solution)/shard_map/ppermute | solution.py:977
  141.4 24.1 %collective-permute-start.12 = (bf16[256,512]{1,0:T(8,128)(2,1)}, bf16[256,512]{1,0:T(8,128)(2,1)}, u32[]{:S(2)}, u32[]{:S(2)}) collective-permute-start(bf16[256,512]{1,0:T(8,128)(2,1)} %get-tuple-element.125), channel_id=1, source_target_pairs={{0,4},{4,0},{8,12},{12,8},{16,20},{20,16},{24,28},{28,24},{1,5},{5... | collective-permute-start | bytes 786440 | tf_op jit(solution)/shard_map/ppermute | solution.py:977
  141.4 24.1 %collective-permute-start.13 = (bf16[256,512]{1,0:T(8,128)(2,1)}, bf16[256,512]{1,0:T(8,128)(2,1)}, u32[]{:S(2)}, u32[]{:S(2)}) collective-permute-start(bf16[256,512]{1,0:T(8,128)(2,1)} %get-tuple-element.126), channel_id=1, source_target_pairs={{0,8},{4,12},{8,0},{12,4},{16,24},{20,28},{24,16},{28,20},{1,9},{5... | collective-permute-start | bytes 786440 | tf_op jit(solution)/shard_map/ppermute | solution.py:977
  154.6 17.6 %collective-permute-start.11 = (bf16[640,512]{1,0:T(8,128)(2,1)}, bf16[640,512]{1,0:T(8,128)(2,1)S(1)}, u32[]{:S(2)}, u32[]{:S(2)}) collective-permute-start(bf16[640,512]{1,0:T(8,128)(2,1)} %get-tuple-element.123), channel_id=1, source_target_pairs={{0,2},{1,3},{2,0},{3,1},{4,6},{5,7},{6,4},{7,5},{8,10},{9,11},{10,... | collective-permute-start | bytes 1966088 | tf_op jit(solution)/shard_map/ppermute | solution.py:977
  163.4 36.2 %collective-permute-start.18 = (bf16[256,768]{1,0:T(8,128)(2,1)}, bf16[256,768]{1,0:T(8,128)(2,1)S(1)}, u32[]{:S(2)}, u32[]{:S(2)}) collective-permute-start(bf16[256,768]{1,0:T(8,128)(2,1)} %get-tuple-element.139), channel_id=1, source_target_pairs={{0,1},{1,0},{2,3},{3,2},{4,5},{5,4},{6,7},{7,6},{8,9},{9,8},{10,11... | collective-permute-start | bytes 1179656 | tf_op jit(solution)/shard_map/ppermute | solution.py:977
  176.4 23.2 %collective-permute-start.15 = (bf16[160,512]{1,0:T(8,128)(2,1)}, bf16[160,512]{1,0:T(8,128)(2,1)S(1)}, u32[]{:S(2)}, u32[]{:S(2)}) collective-permute-start(bf16[160,512]{1,0:T(8,128)(2,1)} %get-tuple-element.135), channel_id=1, source_target_pairs={{0,4},{4,0},{8,12},{12,8},{16,20},{20,16},{24,28},{28,24},{1,5},{5... | collective-permute-start | bytes 491528 | tf_op jit(solution)/shard_map/ppermute | solution.py:977
  177.5 22.1 %collective-permute-start.16 = (bf16[160,512]{1,0:T(8,128)(2,1)}, bf16[160,512]{1,0:T(8,128)(2,1)S(1)}, u32[]{:S(2)}, u32[]{:S(2)}) collective-permute-start(bf16[160,512]{1,0:T(8,128)(2,1)} %get-tuple-element.136), channel_id=1, source_target_pairs={{0,8},{4,12},{8,0},{12,4},{16,24},{20,28},{24,16},{28,20},{1,9},{5... | collective-permute-start | bytes 491528 | tf_op jit(solution)/shard_map/ppermute | solution.py:977
  179.0 20.6 %collective-permute-start.17 = (bf16[160,512]{1,0:T(8,128)(2,1)}, bf16[160,512]{1,0:T(8,128)(2,1)S(1)}, u32[]{:S(2)}, u32[]{:S(2)}) collective-permute-start(bf16[160,512]{1,0:T(8,128)(2,1)} %get-tuple-element.137), channel_id=1, source_target_pairs={{0,12},{4,8},{8,4},{12,0},{16,28},{20,24},{24,20},{28,16},{1,13},{... | collective-permute-start | bytes 491528 | tf_op jit(solution)/shard_map/ppermute | solution.py:977
  197.5 11.1 %collective-permute-start.19 = (bf16[128,512]{1,0:T(8,128)(2,1)}, bf16[128,512]{1,0:T(8,128)(2,1)}, u32[]{:S(2)}, u32[]{:S(2)}) collective-permute-start(bf16[128,512]{1,0:T(8,128)(2,1)} %get-tuple-element.144), channel_id=1, source_target_pairs={{0,2},{1,3},{2,0},{3,1},{4,6},{5,7},{6,4},{7,5},{8,10},{9,11},{10,... | collective-permute-start | bytes 393224 | tf_op jit(solution)/shard_map/ppermute | solution.py:977
  216.2 22.5 %collective-permute-start.23 = (bf16[128,896]{1,0:T(8,128)(2,1)S(1)}, bf16[128,896]{1,0:T(8,128)(2,1)S(1)}, u32[]{:S(2)}, u32[]{:S(2)}) collective-permute-start(bf16[128,896]{1,0:T(8,128)(2,1)S(1)} %get-tuple-element.154), channel_id=1, source_target_pairs={{0,2},{1,3},{2,0},{3,1},{4,6},{5,7},{6,4},{7,5},{8,10},{9,11},{10,... | collective-permute-start | bytes 688136 | tf_op jit(solution)/shard_map/ppermute | solution.py:977
  221.2 23.2 %collective-permute-start.27 = (bf16[160,512]{1,0:T(8,128)(2,1)S(1)}, bf16[160,512]{1,0:T(8,128)(2,1)S(1)}, u32[]{:S(2)}, u32[]{:S(2)}) collective-permute-start(bf16[160,512]{1,0:T(8,128)(2,1)S(1)} %get-tuple-element.163.refs_0_), channel_id=1, source_target_pairs={{0,12},{4,8},{8,4},{12,0},{16,28},{20,24},{24,20},{28,16},{1,13},{... | collective-permute-start | bytes 491528 | tf_op jit(solution)/shard_map/ppermute | solution.py:977
  224.6 19.8 %collective-permute-start.26 = (bf16[160,512]{1,0:T(8,128)(2,1)S(1)}, bf16[160,512]{1,0:T(8,128)(2,1)S(1)}, u32[]{:S(2)}, u32[]{:S(2)}) collective-permute-start(bf16[160,512]{1,0:T(8,128)(2,1)S(1)} %get-tuple-element.163.refs_0_), channel_id=1, source_target_pairs={{0,8},{4,12},{8,0},{12,4},{16,24},{20,28},{24,16},{28,20},{1,9},{5... | collective-permute-start | bytes 491528 | tf_op jit(solution)/shard_map/ppermute | solution.py:977
  225.4 26.2 %collective-permute-start.25 = (bf16[160,512]{1,0:T(8,128)(2,1)S(1)}, bf16[160,512]{1,0:T(8,128)(2,1)S(1)}, u32[]{:S(2)}, u32[]{:S(2)}) collective-permute-start(bf16[160,512]{1,0:T(8,128)(2,1)S(1)} %get-tuple-element.163.refs_0_), channel_id=1, source_target_pairs={{0,4},{4,0},{8,12},{12,8},{16,20},{20,16},{24,28},{28,24},{1,5},{5... | collective-permute-start | bytes 491528 | tf_op jit(solution)/shard_map/ppermute | solution.py:977
  226.9 11.9 %collective-permute-start.24 = (bf16[128,512]{1,0:T(8,128)(2,1)S(1)}, bf16[128,512]{1,0:T(8,128)(2,1)S(1)}, u32[]{:S(2)}, u32[]{:S(2)}) collective-permute-start(bf16[128,512]{1,0:T(8,128)(2,1)S(1)} %get-tuple-element.155.refs_3_), channel_id=1, source_target_pairs={{0,16},{4,20},{8,24},{12,28},{16,0},{20,4},{24,8},{28,12},{1,17},{... | collective-permute-start | bytes 393224 | tf_op jit(solution)/shard_map/ppermute | solution.py:977
  244.4 18.0 %collective-permute-start.30 = (bf16[128,512]{1,0:T(8,128)(2,1)S(1)}, bf16[128,512]{1,0:T(8,128)(2,1)S(1)}, u32[]{:S(2)}, u32[]{:S(2)}) collective-permute-start(bf16[128,512]{1,0:T(8,128)(2,1)S(1)} %get-tuple-element.164.refs_4_), channel_id=1, source_target_pairs={{0,12},{4,8},{8,4},{12,0},{16,28},{20,24},{24,20},{28,16},{1,13},{... | collective-permute-start | bytes 393224 | tf_op jit(solution)/shard_map/ppermute | solution.py:977
  (41 other events, 270.3 us)
where the time goes:
time: 271 us; the launch traced here: 269 us
  Pallas kernels  149 us (55%)
  starting transfers between devices  64.7 us (24%)
  waiting for transfers between devices  37.2 us (14%)
  local copies, waits for them, and re-layouts  12.9 us (5%)
  other arithmetic  3.86 us (1%)
    ppermute x38, starting transfers between devices, exchange(): return lax.ppermute(value, axis, [(i, i ^ bit) for i in range(size)])  64.7 us
    pallas_call x4, Pallas kernels, attention_backward(): pl.pallas_call(partial(bwd_kernel, seq_rows, groups, group, seq, shards,...  48.4 us
    pallas_call x1, Pallas kernels, feed_forward(): pl.pallas_call(partial(ffn_kernel, seq_rows, shards), out_shape=(jax.Shap...  47.3 us
    ppermute x38, waiting for transfers between devices, exchange(): return lax.ppermute(value, axis, [(i, i ^ bit) for i in range(size)])  37.2 us
    pallas_call x2, Pallas kernels, attention_forward(): pl.pallas_call(partial(fwd_kernel, seq_rows, seq), out_shape=(jax.ShapeDt...  29.8 us
    unnamed x54, local copies, waits for them, and re-layouts  12.4 us
    pallas_call x2, Pallas kernels, input_gradient(): pl.pallas_call(partial(input_kernel, seq_rows, groups, seq), out_shape=(j...  11 us
    pallas_call x8, Pallas kernels, combine(): pl.pallas_call(partial(combine_kernel, [[len(g) for g in i[0]] for i in i...  9.77 us
  transfers between devices with their start and end apart: 38, of which 9 were waited for; matrix products, arithmetic and copies ran while one was open for 0% of the time, Pallas kernels for 35%

commit v1 on v0

--- a/solution.py
+++ b/solution.py
@@ -758,6 +758,9 @@
         return sums + col_sum(grad.astype(F32))
 
     sums = lax.fori_loop(0, chunks, finish, jnp.zeros((1, width), F32))
+    if not last:
+        store = pltpu.make_async_copy(acc, acc_hbm, acc_sem)
+        store.start()
     extra[MEM : MEM + 1, base : base + gcols] += sums[:, :gcols]
     extra[MEM + 1 : MEM + 2, base : base + gcols] += sums[:, 2 * gcols :]
     turned = (
@@ -790,8 +793,6 @@
                     lanes.append(jnp.zeros((empty, 128), F32))
                 piece[spot, width:] = jnp.concatenate(lanes, 0).astype(BF16)
     else:
-        store = pltpu.make_async_copy(acc, acc_hbm, acc_sem)
-        store.start()
         store.wait()
     if extra_ref is not None:
         extra_ref[...] = extra[...]
@@ -882,59 +883,68 @@
 
 def input_kernel(seq_rows, groups, seq, len_ref, w_ref, gh_hbm, *refs):
     projs = refs[:groups]
-    gx_ref, token, gh, blocks, sems = refs[-5:]
+    gx_hbm, token, gh, blocks, rows, sems, out_sem = refs[-7:]
     token[...] = jnp.zeros(token.shape, F32)
     gcols = D // groups
     length = len_ref[seq]
     chunks = cdiv(length, TILE)
+    whole = seq_rows // TILE
+
+    def spot(chunk):
+        return pl.ds(pl.multiple_of(chunk * TILE, TILE), TILE)
 
     def fetch(chunk):
-        here = pl.ds(pl.multiple_of(chunk * TILE, TILE), TILE)
-        slot = lax.rem(chunk, 2)
-        return [
-            pltpu.make_async_copy(gh_hbm.at[seq, here, :], gh.at[slot], sems.at[slot, 0])
-        ] + [
-            pltpu.make_async_copy(p.at[here, :], blocks.at[slot, i], sems.at[slot, 1 + i])
+        here = spot(chunk)
+        return [pltpu.make_async_copy(gh_hbm.at[seq, here, :], gh.at[here, :], sems.at[chunk, 0])] + [
+            pltpu.make_async_copy(p.at[here, :], blocks.at[i, here, :], sems.at[chunk, 1 + i])
             for i, p in enumerate(projs)
         ]
 
-    for copy in fetch(0):
-        copy.start()
-    gx_ref[...] = jnp.zeros(gx_ref.shape, BF16)
+    def send(chunk):
+        here = spot(chunk)
+        return pltpu.make_async_copy(rows.at[here, :], gx_hbm.at[seq, here, :], out_sem)
+
+    def begin(chunk, _):
+        for copy in fetch(chunk):
+            copy.start()
+        return 0
+
+    lax.fori_loop(0, chunks, begin, 0)
+
+    def empty(chunk, _):
+        rows[spot(chunk), :] = jnp.zeros((TILE, D), BF16)
+        send(chunk).start()
+        return 0
+
+    lax.fori_loop(chunks, whole, empty, 0)
 
     def step(chunk, _):
-        start = pl.multiple_of(chunk * TILE, TILE)
-        slot = lax.rem(chunk, 2)
-
-        @pl.when(chunk + 1 < chunks)
-        def _():
-            for copy in fetch(chunk + 1):
-                copy.start()
-
+        here = spot(chunk)
         for copy in fetch(chunk):
             copy.wait()
         joint = jnp.concatenate(
             [
-                blocks[slot, g, :, kind * gcols : (kind + 1) * gcols]
+                blocks[g, here, kind * gcols : (kind + 1) * gcols]
                 for kind in range(3)
                 for g in range(groups)
             ],
             1,
         )
         grad = nt(joint, w_ref[...])
-        row = lax.broadcasted_iota(jnp.int32, (TILE, 1), 0) + start
-        gx_ref[0, pl.ds(start, TILE), :] = jnp.where(
-            row < length, grad + gh[slot].astype(F32), 0.0
-        ).astype(BF16)
+        row = lax.broadcasted_iota(jnp.int32, (TILE, 1), 0) + chunk * TILE
+        rows[here, :] = jnp.where(row < length, grad + gh[here, :].astype(F32), 0.0).astype(BF16)
+        send(chunk).start()
         return 0
 
     lax.fori_loop(0, chunks, step, 0)
+    pltpu.make_async_copy(rows, gx_hbm.at[seq], out_sem).wait()
 
 
 def input_gradient(seq, lengths, w_qkv, gh, projs, after=(), base=None):
     count, seq_rows = gh.shape[:2]
     groups = len(projs)
     hbm = pl.BlockSpec(memory_space=pl.ANY)
+    vm = pl.BlockSpec(memory_space=pltpu.VMEM)
     base = () if base is None else (base,)
     return pl.pallas_call(
         partial(input_kernel, seq_rows, groups, seq),
@@ -942,21 +952,16 @@
             jax.ShapeDtypeStruct((count, seq_rows, D), BF16),
             jax.ShapeDtypeStruct((8, 128), F32),
         ),
-        grid=(1,),
-        in_specs=[
-            pl.BlockSpec(memory_space=pltpu.SMEM),
-            pl.BlockSpec(memory_space=pltpu.VMEM),
-        ]
+        in_specs=[pl.BlockSpec(memory_space=pltpu.SMEM), vm]
         + [hbm] * (1 + groups + len(after) + len(base)),
-        out_specs=(
-            pl.BlockSpec((1, seq_rows, D), lambda i: (seq, 0, 0)),
-            pl.BlockSpec(memory_space=pltpu.VMEM),
-        ),
+        out_specs=(hbm, vm),
         input_output_aliases={3 + groups + len(after): 0} if base else {},
         scratch_shapes=[
-            pltpu.VMEM((2, TILE, D), BF16),
-            pltpu.VMEM((2, groups, TILE, 3 * D // groups), BF16),
-            pltpu.SemaphoreType.DMA((2, 1 + groups)),
+            pltpu.VMEM((seq_rows, D), BF16),
+            pltpu.VMEM((groups, seq_rows, 3 * D // groups), BF16),
+            pltpu.VMEM((seq_rows, D), BF16),
+            pltpu.SemaphoreType.DMA((seq_rows // TILE, 1 + groups)),
+            pltpu.SemaphoreType.DMA,
         ],
         compiler_params=pltpu.CompilerParams(vmem_limit_bytes=VMEM_LIMIT),
         cost_estimate=pl.CostEstimate(
@@ -997,28 +1002,27 @@
     return dict(zip(keys, lax.optimization_barrier((*[pieces[k] for k in keys], event))))
 
 
-def combine_kernel(counts, modes, waits, place_ref, *refs):
+def combine_kernel(counts, modes, waits, carried, place_ref, *refs):
     refs = list(refs)
     arrays = [[[refs.pop(0) for _ in range(c)] for c in group] for group in counts]
     refs = refs[waits:]
-    total, token = refs.pop(), refs.pop(-1)
+    total = refs.pop()
+    refs = refs[: len(refs) - carried]
+    token = refs.pop()
     token[...] = jnp.zeros(token.shape, F32)
     place = place_ref[0]
     for groups, (mode, stacked, cols) in zip(arrays, modes):
-        rows = 0
-        for group in groups:
-            more, wide = group[0].shape
-            value = group[0][...].astype(F32)
-            for other in group[1:]:
-                value = value + other[...].astype(F32)
-            total[rows : rows + more, :wide] = value
-            if wide < cols:
-                total[rows : rows + more, wide:cols] = jnp.zeros((more, cols - wide), F32)
-            rows += more
+        rows = sum(group[0].shape[0] for group in groups)
         if mode == "halves":
-            refs.pop(0)[...] = total[: rows // 2, :cols].astype(BF16)
-            refs.pop(0)[...] = total[rows // 2 : rows, :cols].astype(BF16)
+            half = rows // 2
+            for side in range(2):
+                add_rows(groups[0], side * half, half, refs.pop(0), 0, cols)
         elif mode == "parts":
+            base = 0
+            for group in groups:
+                more = group[0].shape[0]
+                add_rows(group, 0, more, total, base, cols)
+                base += more
             one = rows // stacked
             part = one // GROUP
             for m in range(GROUP):
@@ -1029,10 +1033,31 @@
                         pl.ds(at + i * one, part), :cols
                     ].astype(BF16)
         else:
-            refs.pop(0)[...] = total[:rows, :cols].astype(BF16)
-
-
-def combine(place, items, after):
+            add_rows(groups[0], 0, rows, refs.pop(0), 0, cols)
+
+
+def add_rows(group, start, rows, target, base, cols):
+    wide = group[0].shape[1]
+    step = next((s for s in (64, 32, 16) if not (rows % s or start % s or base % s)), rows)
+
+    def add(index, _):
+        def at(first):
+            if step == rows:
+                return pl.ds(first, rows)
+            return pl.ds(pl.multiple_of(first + index * step, step), step)
+
+        value = group[0][at(start), :].astype(F32)
+        for other in group[1:]:
+            value = value + other[at(start), :].astype(F32)
+        target[at(base), :wide] = value.astype(target.dtype)
+        if wide < cols:
+            target[at(base), wide:cols] = jnp.zeros((step, cols - wide), target.dtype)
+        return 0
+
+    lax.fori_loop(0, rows // step, add, 0)
+
+
+def combine(place, items, after, carry=()):
     vm = pl.BlockSpec(memory_space=pltpu.VMEM)
     shapes, flat, modes, most = [], [], [], 0
     for groups, mode, stacked in items:
@@ -1049,23 +1074,35 @@
             shapes += [(rows, cols)]
     size = sum(a.size for a in flat) * 2
     outs = pl.pallas_call(
-        partial(combine_kernel, [[len(g) for g in i[0]] for i in items], modes, len(after)),
+        partial(
+            combine_kernel,
+            [[len(g) for g in i[0]] for i in items],
+            modes,
+            len(after) + len(carry),
+            len(carry),
+        ),
         out_shape=tuple(jax.ShapeDtypeStruct(s, BF16) for s in shapes)
-        + (jax.ShapeDtypeStruct((8, 128), F32),),
+        + (jax.ShapeDtypeStruct((8, 128), F32),)
+        + tuple(jax.ShapeDtypeStruct(a.shape, a.dtype) for a in carry),
         in_specs=[pl.BlockSpec(memory_space=pltpu.SMEM)]
         + [vm] * len(flat)
-        + [pl.BlockSpec(memory_space=pl.ANY)] * len(after),
-        out_specs=(vm,) * (len(shapes) + 1),
+        + [pl.BlockSpec(memory_space=pl.ANY)] * (len(after) + len(carry)),
+        out_specs=(vm,) * (len(shapes) + 1)
+        + (pl.BlockSpec(memory_space=pl.ANY),) * len(carry),
+        input_output_aliases={
+            1 + len(flat) + len(after) + i: len(shapes) + 1 + i for i in range(len(carry))
+        },
         scratch_shapes=[pltpu.VMEM((most, max(m[2] for m in modes)), F32)],
         compiler_params=pltpu.CompilerParams(vmem_limit_bytes=24 * 2**20),
         cost_estimate=pl.CostEstimate(flops=size, bytes_accessed=2 * size, transcendentals=0),
         name="combine",
-    )(place, *flat, *after)
-    outs, token, results = list(outs[:-1]), outs[-1], []
+    )(place, *flat, *after, *carry)
+    held = list(outs[len(shapes) + 1 :])
+    outs, token, results = list(outs[: len(shapes)]), outs[len(shapes)], []
     for mode, _, _ in modes:
         taken = {"halves": 2, "parts": GROUP, "whole": 1}[mode]
         results.append([outs.pop(0) for _ in range(taken)])
-    return results, token
+    return results, [token, *held]
 
 
 GROUP = 4
@@ -1096,14 +1133,14 @@
 
     def alone(self, place, after=()):
         (self.value,), token = combine(place, [self.exchange()], after)
-        return [token]
-
-
-def advance(place, streams, items, after):
-    results, token = combine(place, items, after)
+        return token
+
+
+def advance(place, streams, items, after, carry=()):
+    results, token = combine(place, items, after, carry)
     for stream, result in zip(streams, results):
         stream.value = result
-    return [token]
+    return token
 
 
 def whole_parts(stream):
@@ -1199,14 +1236,16 @@
                 s, g, GROUPS, shards, lengths, me, whole, table, inputs, dot, fwd[s][1],
                 fwd[s][2], fwd[s][0], chain, closing, after,
             )
-            after = advance(place, busy, items, [res[-1]])
+            chain = list(res[1:-1])
+            carry = chain[1:2] if len(calls) == 3 else []
+            after, *held = advance(place, busy, items, [res[-1]], carry)
+            after = [after]
+            chain[1 : 1 + len(held)] = held
             projs[s][g] = res[0]
             calls.append(res)
-            chain = res[1:-1]
         quarters[g] = Stream(chain[:2], sizes, folds + [("stop", 0)])
         extras += chain[2:]
     early, last = quarters
-    last.value[1] = last.value[1] + after[0][0, 0].astype(BF16)
     for stream, left in ((early, 1), (tall, 0), (deep, 1)):
         while len(stream.steps) > left:
             stream.alone(place)

time: 271 us -> 272 us (level)
    unnamed x54 -> x56, local copies, waits for them, and re-layouts: 12.4 us -> 14.5 us
  transfers between devices with their start and end apart: 38 -> 38, of which waited for: 9 -> 8; matrix products, arithmetic and copies ran while one was open for 0% -> 0% of each run, Pallas kernels for 35% -> 36%
where the time goes in v1:
time: 272 us; the launch traced here: 269 us
  Pallas kernels  150 us (55%)
  starting transfers between devices  64.4 us (24%)
  waiting for transfers between devices  36.2 us (13%)
  local copies, waits for them, and re-layouts  14.5 us (5%)
    ppermute x38, starting transfers between devices, exchange(): return lax.ppermute(value, axis, [(i, i ^ bit) for i in range(size)])  64.4 us
    pallas_call x4, Pallas kernels, attention_backward(): pl.pallas_call(partial(bwd_kernel, seq_rows, groups, group, seq, shards,...  48.5 us
    pallas_call x1, Pallas kernels, feed_forward(): pl.pallas_call(partial(ffn_kernel, seq_rows, shards), out_shape=(jax.Shap...  47.3 us
    ppermute x38, waiting for transfers between devices, exchange(): return lax.ppermute(value, axis, [(i, i ^ bit) for i in range(size)])  36.2 us
    pallas_call x2, Pallas kernels, attention_forward(): pl.pallas_call(partial(fwd_kernel, seq_rows, seq), out_shape=(jax.ShapeDt...  29.8 us
    unnamed x56, local copies, waits for them, and re-layouts  14.5 us
    pallas_call x2, Pallas kernels, input_gradient(): pl.pallas_call(partial(input_kernel, seq_rows, groups, seq), out_shape=(j...  11.4 us
    pallas_call x8, Pallas kernels, combine(): pl.pallas_call(partial(combine_kernel, [[len(g) for g in i[0]] for i in i...  10.4 us
  transfers between devices with their start and end apart: 38, of which 8 were waited for; matrix products, arithmetic and copies ran while one was open for 0% of the time, Pallas kernels for 36%

profile of v1, /device:TPU:0, one launch (start us, length us, event | category | flops | bytes accessed | tf_op | source)
XLA Modules:
  0.0 268.8 jit_solution(2294173610830931866)
XLA Ops:
  1.7 3.0 %collective-permute-start.1 = (bf16[144,1536]{1,0:T(8,128)(2,1)S(1)}, bf16[144,1536]{1,0:T(8,128)(2,1)S(1)}, u32[]{:S(2)}, u32[]{:S(2)}) collective-permute-start(bf16[144,1536]{1,0:T(8,128)(2,1)S(1)} %fusion.1.refs_0_), channel_id=1, source_target_pairs={{0,2},{1,3},{2,0},{3,1},{4,6},{5,7},{6,4},{7,5},{8,10},{9,11},{10,... | collective-permute-start | bytes 1327112 | tf_op jit(solution)/shard_map/ppermute | solution.py:982
  4.7 10.2 %collective-permute-done.1.refs_2_ = bf16[144,1536]{1,0:T(8,128)(2,1)S(1)} collective-permute-done((bf16[144,1536]{1,0:T(8,128)(2,1)S(1)}, bf16[144,1536]{1,0:T(8,128)(2,1)S(1)}, u32[]{:S(2)}, u32[]{:S(2)}) %collective-permute-start.1) | collective-permute-done | bytes 442400 | tf_op jit(solution)/shard_map/ppermute | solution.py:982
  22.6 8.5 %attention_forward.3 = (bf16[4,8,1056,256]{3,2,1,0:T(8,128)(2,1)}, bf16[512,1024]{1,0:T(8,128)(2,1)}, bf16[512,1024]{1,0:T(8,128)(2,1)}, f32[8,1024]{1,0:T(8,128)}) custom-call(s32[2]{0:T(128)} %len_ref.9, bf16[2,1024,512]{2,1,0:T(8,128)(2,1)} %refs_5_.7, bf16[512,1536]{1,0:T(8,128)(2,1)} %copy-done, bf16[512,512]{1,0:T(8,128)(2,1)} %copy-done.20, ...), custom_call_target="tpu_custom_call" | custom-call | flops 8000000000 | bytes 24000000 | tf_op jit(solution)/shard_map/attention_forward/pallas_call | solution.py:265
  33.2 11.4 %collective-permute-done.3.refs_2_ = bf16[128,2560]{1,0:T(8,128)(2,1)S(1)} collective-permute-done((bf16[128,2560]{1,0:T(8,128)(2,1)S(1)}, bf16[128,2560]{1,0:T(8,128)(2,1)S(1)}, u32[]{:S(2)}, u32[]{:S(2)}) %collective-permute-start.3) | collective-permute-done | bytes 655392 | tf_op jit(solution)/shard_map/ppermute | solution.py:982
  45.2 21.3 %attention_forward.2 = (bf16[4,8,1056,256]{3,2,1,0:T(8,128)(2,1)}, bf16[512,1024]{1,0:T(8,128)(2,1)}, bf16[512,1024]{1,0:T(8,128)(2,1)}, f32[8,1024]{1,0:T(8,128)}) custom-call(s32[2]{0:T(128)} %len_ref.9, bf16[2,1024,512]{2,1,0:T(8,128)(2,1)} %refs_5_.7, bf16[512,1536]{1,0:T(8,128)(2,1)} %copy-done, bf16[512,512]{1,0:T(8,128)(2,1)} %copy-done.20, ...), custom_call_target="tpu_custom_call" | custom-call | flops 8000000000 | bytes 24000000 | tf_op jit(solution)/shard_map/attention_forward/pallas_call | solution.py:265
  66.5 47.3 %feed_forward.1 = (bf16[2,1024,512]{2,1,0:T(8,128)(2,1)}, bf16[2,1024,512]{2,1,0:T(8,128)(2,1)}, bf16[2,512,1024]{2,1,0:T(8,128)(2,1)}, bf16[1280,512]{1,0:T(8,1...) custom-call(s32[2]{0:T(128)} %len_ref.9, ...), custom_call_target="tpu_custom_call" | custom-call | flops 27000000512 | bytes 24000000 | tf_op jit(solution)/shard_map/feed_forward/pallas_call | solution.py:554
  114.4 17.5 %attention_backward.4 = (bf16[1280,768]{1,0:T(8,128)(2,1)}, f32[512,768]{1,0:T(8,128)}, f32[32,512]{1,0:T(8,128)}, f32[8,128]{1,0:T(8,128)}) custom-call(s32[2]{0:T(128)} %len_ref.9, s32[1]{0:T(128)} %bitcast.me_ref.refs_1_, bf16[512,1536]{1,0:T(8,128)(2,1)} %copy-done, bf16[512,1536]{1,0:T(8,128)(2,1)} %copy-done, bf16[32,512]{1,0:T(8,128)(2,1)} %copy-done.22, ...), custom_call_target="tpu_custom_call" | custom-call | flops 8000000000 | bytes 15000000 | tf_op jit(solution)/shard_map/attention_backward/pallas_call | solution.py:834
  133.9 3.4 %combine.8 = (bf16[640,512]{1,0:T(8,128)(2,1)S(1)}, bf16[640,512]{1,0:T(8,128)(2,1)}, bf16[256,512]{1,0:T(8,128)(2,1)S(1)}, bf16[256,512]{1,0:T(8,128)(2,1)}, bf...) custom-call(s32[1]{0:T(128)} %bitcast.1.place_ref, bf16[1280,512]{1,0:T(8,128)(2,1)S(1)} %copy-done.1, ...), custom_call_target="tpu_custom_call" | custom-call | flops 4718592 | bytes 9437184 | tf_op jit(solution)/shard_map/combine/pallas_call | solution.py:1076
  138.0 5.6 %collective-permute-start.12 = (bf16[256,512]{1,0:T(8,128)(2,1)}, bf16[256,512]{1,0:T(8,128)(2,1)}, u32[]{:S(2)}, u32[]{:S(2)}) collective-permute-start(bf16[256,512]{1,0:T(8,128)(2,1)} %get-tuple-element.125), channel_id=1, source_target_pairs={{0,4},{4,0},{8,12},{12,8},{16,20},{20,16},{24,28},{28,24},{1,5},{5... | collective-permute-start | bytes 786440 | tf_op jit(solution)/shard_map/ppermute | solution.py:982
  145.1 10.7 %collective-permute-start.11 = (bf16[640,512]{1,0:T(8,128)(2,1)}, bf16[640,512]{1,0:T(8,128)(2,1)S(1)}, u32[]{:S(2)}, u32[]{:S(2)}) collective-permute-start(bf16[640,512]{1,0:T(8,128)(2,1)} %get-tuple-element.123), channel_id=1, source_target_pairs={{0,2},{1,3},{2,0},{3,1},{4,6},{5,7},{6,4},{7,5},{8,10},{9,11},{10,... | collective-permute-start | bytes 1966088 | tf_op jit(solution)/shard_map/ppermute | solution.py:982
  155.7 6.7 %attention_backward.5 = (bf16[1280,768]{1,0:T(8,128)(2,1)}, bf16[256,768]{1,0:T(8,128)(2,1)}, bf16[256,768]{1,0:T(8,128)(2,1)}, f32[32,512]{1,0:T(8,128)}, f32[8,128]{1,0:T(8,128)}) custom-call(s32[2]{0:T(128)} %len_ref.9, s32[1]{0:T(128)} %bitcast.me_ref.refs_1_, bf16[512,1536]{1,0:T(8,128)(2,1)} %copy-done, bf16[512,1536]{1,0:T(8,128)(2,1)} %copy-done, ...), custom_call_target="tpu_custom_call" | custom-call | flops 8000000000 | bytes 15000000 | tf_op jit(solution)/shard_map/attention_backward/pallas_call | solution.py:834
  163.1 7.3 %collective-permute-done.11.refs_1_ = bf16[640,512]{1,0:T(8,128)(2,1)S(1)} collective-permute-done((bf16[640,512]{1,0:T(8,128)(2,1)}, bf16[640,512]{1,0:T(8,128)(2,1)S(1)}, u32[]{:S(2)}, u32[]{:S(2)}) %collective-permute-start.11) | collective-permute-done | bytes 655392 | tf_op jit(solution)/shard_map/ppermute | solution.py:982
  171.0 2.3 combine.9
  178.1 17.3 %attention_backward.6 = (bf16[1280,768]{1,0:T(8,128)(2,1)}, f32[512,768]{1,0:T(8,128)}, f32[32,512]{1,0:T(8,128)}, f32[8,128]{1,0:T(8,128)}) custom-call(s32[2]{0:T(128)} %len_ref.9, s32[1]{0:T(128)} %bitcast.me_ref.refs_1_, bf16[512,1536]{1,0:T(8,128)(2,1)} %copy-done, bf16[512,1536]{1,0:T(8,128)(2,1)} %copy-done, bf16[32,512]{1,0:T(8,128)(2,1)} %copy-done.22, ...), custom_call_target="tpu_custom_call" | custom-call | flops 8000000000 | bytes 15000000 | tf_op jit(solution)/shard_map/attention_backward/pallas_call | solution.py:834
  199.7 6.9 %attention_backward.7 = (bf16[1280,768]{1,0:T(8,128)(2,1)}, bf16[256,896]{1,0:T(8,128)(2,1)}, bf16[256,896]{1,0:T(8,128)(2,1)}, f32[8,128]{1,0:T(8,128)}) custom-call(s32[2]{0:T(128)} %len_ref.9, s32[1]{0:T(128)} %bitcast.me_ref.refs_1_, bf16[512,1536]{1,0:T(8,128)(2,1)} %copy-done, bf16[512,1536]{1,0:T(8,128)(2,1)} %copy-done, bf16[32,512]{1,0:T(8,128)(2,1)} %copy-done.22, ...), custom_call_target="tpu_custom_call" | custom-call | flops 8000000000 | bytes 15000000 | tf_op jit(solution)/shard_map/attention_backward/pallas_call | solution.py:834
  215.3 5.9 %collective-permute-start.27 = (bf16[160,512]{1,0:T(8,128)(2,1)S(1)}, bf16[160,512]{1,0:T(8,128)(2,1)S(1)}, u32[]{:S(2)}, u32[]{:S(2)}) collective-permute-start(bf16[160,512]{1,0:T(8,128)(2,1)S(1)} %get-tuple-element.163.refs_0_), channel_id=1, source_target_pairs={{0,12},{4,8},{8,4},{12,0},{16,28},{20,24},{24,20},{28,16},{1,13},{... | collective-permute-start | bytes 491528 | tf_op jit(solution)/shard_map/ppermute | solution.py:982
  221.2 7.7 %collective-permute-start.26 = (bf16[160,512]{1,0:T(8,128)(2,1)S(1)}, bf16[160,512]{1,0:T(8,128)(2,1)S(1)}, u32[]{:S(2)}, u32[]{:S(2)}) collective-permute-start(bf16[160,512]{1,0:T(8,128)(2,1)S(1)} %get-tuple-element.163.refs_0_), channel_id=1, source_target_pairs={{0,8},{4,12},{8,0},{12,4},{16,24},{20,28},{24,16},{28,20},{1,9},{5... | collective-permute-start | bytes 491528 | tf_op jit(solution)/shard_map/ppermute | solution.py:982
  229.4 6.5 %input_gradient.2 = (bf16[2,1024,512]{2,1,0:T(8,128)(2,1)}, f32[8,128]{1,0:T(8,128)}) custom-call(s32[2]{0:T(128)} %len_ref.9, bf16[512,1536]{1,0:T(8,128)(2,1)} %copy-done, bf16[2,1024,512]{2,1,0:T(8,128)(2,1)} %get-tuple-element.107.gh_hbm, bf16[1280,768]{1,0:T(8,128)(2,1)} %get-tuple-element.156.refs_0_, bf16[1280,768]{1,0:T(8,128)(2,1)} %get-tuple-element.157.refs_1_, ...), custom_call_target="tpu_custom_call" | custom-call | flops 2000000000 | bytes 7000000 | tf_op jit(solution)/shard_map/input_gradient/pallas_call | solution.py:949
  238.0 3.1 %collective-permute-start.31 = (bf16[64,896]{1,0:T(8,128)(2,1)}, bf16[64,896]{1,0:T(8,128)(2,1)S(1)}, u32[]{:S(2)}, u32[]{:S(2)}) collective-permute-start(bf16[64,896]{1,0:T(8,128)(2,1)} %get-tuple-element.166), channel_id=1, source_target_pairs={{0,4},{4,0},{8,12},{12,8},{16,20},{20,16},{24,28},{28,24},{1,5},{5... | collective-permute-start | bytes 344072 | tf_op jit(solution)/shard_map/ppermute | solution.py:982
  244.1 4.9 %input_gradient.3 = (bf16[2,1024,512]{2,1,0:T(8,128)(2,1)}, f32[8,128]{1,0:T(8,128)}) custom-call(s32[2]{0:T(128)} %len_ref.9, bf16[512,1536]{1,0:T(8,128)(2,1)} %copy-done, bf16[2,1024,512]{2,1,0:T(8,128)(2,1)} %get-tuple-element.107.gh_hbm, bf16[1280,768]{1,0:T(8,128)(2,1)} %get-tuple-element.121.refs_0_, ...), custom_call_target="tpu_custom_call", output_to_operand_aliasing={{0}: (6, {})} | custom-call | flops 2000000000 | bytes 7000000 | tf_op jit(solution)/shard_map/input_gradient/pallas_call | solution.py:949
  250.3 3.8 %collective-permute-start.34 = (bf16[64,896]{1,0:T(8,128)(2,1)S(1)}, bf16[64,896]{1,0:T(8,128)(2,1)S(1)}, u32[]{:S(2)}, u32[]{:S(2)}) collective-permute-start(bf16[64,896]{1,0:T(8,128)(2,1)S(1)} %get-tuple-element.170.refs_0_), channel_id=1, source_target_pairs={{0,16},{4,20},{8,24},{12,28},{16,0},{20,4},{24,8},{28,12},{1,17},{... | collective-permute-start | bytes 344072 | tf_op jit(solution)/shard_map/ppermute | solution.py:982
  254.1 2.5 collective-permute-start.29
  257.8 2.7 collective-permute-start.37
  262.0 2.8 %collective-permute-done.28.refs_5_ = bf16[128,512]{1,0:T(8,128)(2,1)S(1)} collective-permute-done((bf16[128,512]{1,0:T(8,128)(2,1)S(1)}, bf16[128,512]{1,0:T(8,128)(2,1)S(1)}, u32[]{:S(2)}, u32[]{:S(2)}) %collective-permute-start.28) | collective-permute-done | bytes 131104 | tf_op jit(solution)/shard_map/ppermute | solution.py:982
  (129 shorter events, 48.3 us)
Async XLA Ops:
  1.7 13.2 %collective-permute-start.1 = (bf16[144,1536]{1,0:T(8,128)(2,1)S(1)}, bf16[144,1536]{1,0:T(8,128)(2,1)S(1)}, u32[]{:S(2)}, u32[]{:S(2)}) collective-permute-start(bf16[144,1536]{1,0:T(8,128)(2,1)S(1)} %fusion.1.refs_0_), channel_id=1, source_target_pairs={{0,2},{1,3},{2,0},{3,1},{4,6},{5,7},{6,4},{7,5},{8,10},{9,11},{10,... | collective-permute-start | bytes 1327112 | tf_op jit(solution)/shard_map/ppermute | solution.py:982
  4.7 13.4 %collective-permute-start = (bf16[144,1536]{1,0:T(8,128)(2,1)S(1)}, bf16[144,1536]{1,0:T(8,128)(2,1)S(1)}, u32[]{:S(2)}, u32[]{:S(2)}) collective-permute-start(bf16[144,1536]{1,0:T(8,128)(2,1)S(1)} %fusion.1.refs_0_), channel_id=1, source_target_pairs={{0,1},{1,0},{2,3},{3,2},{4,5},{5,4},{6,7},{7,6},{8,9},{9,8},{10,11... | collective-permute-start | bytes 1327112 | tf_op jit(solution)/shard_map/ppermute | solution.py:982
  16.0 15.1 %collective-permute-start.6 = (bf16[512,512]{1,0:T(8,128)(2,1)}, bf16[512,512]{1,0:T(8,128)(2,1)}, u32[]{:S(2)}, u32[]{:S(2)}) collective-permute-start(bf16[512,512]{1,0:T(8,128)(2,1)} %refs_4_), channel_id=1, source_target_pairs={{0,2},{1,3},{2,0},{3,1},{4,6},{5,7},{6,4},{7,5},{8,10},{9,11},{10,... | collective-permute-start | bytes 1572872 | tf_op jit(solution)/shard_map/ppermute | solution.py:982
  17.8 26.9 %collective-permute-start.3 = (bf16[128,2560]{1,0:T(8,128)(2,1)S(1)}, bf16[128,2560]{1,0:T(8,128)(2,1)S(1)}, u32[]{:S(2)}, u32[]{:S(2)}) collective-permute-start(bf16[128,2560]{1,0:T(8,128)(2,1)S(1)} %pad_maximum_fusion.refs_0_), channel_id=1, source_target_pairs={{0,2},{1,3},{2,0},{3,1},{4,6},{5,7},{6,4},{7,5},{8,10},{9,11},{10,... | collective-permute-start | bytes 1966088 | tf_op jit(solution)/shard_map/ppermute | solution.py:982
  31.1 35.4 %collective-permute-start.7 = (bf16[512,512]{1,0:T(8,128)(2,1)}, bf16[512,512]{1,0:T(8,128)(2,1)}, u32[]{:S(2)}, u32[]{:S(2)}) collective-permute-start(bf16[512,512]{1,0:T(8,128)(2,1)} %refs_4_), channel_id=1, source_target_pairs={{0,1},{1,0},{2,3},{3,2},{4,5},{5,4},{6,7},{7,6},{8,9},{9,8},{10,11... | collective-permute-start | bytes 1572872 | tf_op jit(solution)/shard_map/ppermute | solution.py:982
  33.2 33.3 %collective-permute-start.8 = (bf16[512,512]{1,0:T(8,128)(2,1)}, bf16[512,512]{1,0:T(8,128)(2,1)}, u32[]{:S(2)}, u32[]{:S(2)}) collective-permute-start(bf16[512,512]{1,0:T(8,128)(2,1)} %collective-permute-done.6.refs_6_), channel_id=1, source_target_pairs={{0,1},{1,0},{2,3},{3,2},{4,5},{5,4},{6,7},{7,6},{8,9},{9,8},{10,11... | collective-permute-start | bytes 1572872 | tf_op jit(solution)/shard_map/ppermute | solution.py:982
  44.6 21.9 %collective-permute-start.4 = (bf16[128,2560]{1,0:T(8,128)(2,1)S(1)}, bf16[128,2560]{1,0:T(8,128)(2,1)}, u32[]{:S(2)}, u32[]{:S(2)}) collective-permute-start(bf16[128,2560]{1,0:T(8,128)(2,1)S(1)} %pad_maximum_fusion.refs_0_), channel_id=1, source_target_pairs={{0,1},{1,0},{2,3},{3,2},{4,5},{5,4},{6,7},{7,6},{8,9},{9,8},{10,11... | collective-permute-start | bytes 1966088 | tf_op jit(solution)/shard_map/ppermute | solution.py:982
  44.6 21.9 %collective-permute-start.5 = (bf16[128,2560]{1,0:T(8,128)(2,1)S(1)}, bf16[128,2560]{1,0:T(8,128)(2,1)}, u32[]{:S(2)}, u32[]{:S(2)}) collective-permute-start(bf16[128,2560]{1,0:T(8,128)(2,1)S(1)} %collective-permute-done.3.refs_2_), channel_id=1, source_target_pairs={{0,1},{1,0},{2,3},{3,2},{4,5},{5,4},{6,7},{7,6},{8,9},{9,8},{10,11... | collective-permute-start | bytes 1966088 | tf_op jit(solution)/shard_map/ppermute | solution.py:982
  113.8 18.1 %collective-permute-start.9 = (bf16[1280,512]{1,0:T(8,128)(2,1)}, bf16[1280,512]{1,0:T(8,128)(2,1)}, u32[]{:S(2)}, u32[]{:S(2)}) collective-permute-start(bf16[1280,512]{1,0:T(8,128)(2,1)} %get-tuple-element.116), channel_id=1, source_target_pairs={{0,1},{1,0},{2,3},{3,2},{4,5},{5,4},{6,7},{7,6},{8,9},{9,8},{10,11... | collective-permute-start | bytes 3932168 | tf_op jit(solution)/shard_map/ppermute | solution.py:982
  113.9 18.0 %collective-permute-start.10 = (bf16[1024,512]{1,0:T(8,128)(2,1)}, bf16[1024,512]{1,0:T(8,128)(2,1)}, u32[]{:S(2)}, u32[]{:S(2)}) collective-permute-start(bf16[1024,512]{1,0:T(8,128)(2,1)} %get-tuple-element.118), channel_id=1, source_target_pairs={{0,1},{1,0},{2,3},{3,2},{4,5},{5,4},{6,7},{7,6},{8,9},{9,8},{10,11... | collective-permute-start | bytes 3145736 | tf_op jit(solution)/shard_map/ppermute | solution.py:982
  138.0 25.1 %collective-permute-start.12 = (bf16[256,512]{1,0:T(8,128)(2,1)}, bf16[256,512]{1,0:T(8,128)(2,1)}, u32[]{:S(2)}, u32[]{:S(2)}) collective-permute-start(bf16[256,512]{1,0:T(8,128)(2,1)} %get-tuple-element.125), channel_id=1, source_target_pairs={{0,4},{4,0},{8,12},{12,8},{16,20},{20,16},{24,28},{28,24},{1,5},{5... | collective-permute-start | bytes 786440 | tf_op jit(solution)/shard_map/ppermute | solution.py:982
  143.6 19.5 %collective-permute-start.13 = (bf16[256,512]{1,0:T(8,128)(2,1)}, bf16[256,512]{1,0:T(8,128)(2,1)}, u32[]{:S(2)}, u32[]{:S(2)}) collective-permute-start(bf16[256,512]{1,0:T(8,128)(2,1)} %get-tuple-element.126), channel_id=1, source_target_pairs={{0,8},{4,12},{8,0},{12,4},{16,24},{20,28},{24,16},{28,20},{1,9},{5... | collective-permute-start | bytes 786440 | tf_op jit(solution)/shard_map/ppermute | solution.py:982
  143.8 19.3 %collective-permute-start.14 = (bf16[256,512]{1,0:T(8,128)(2,1)}, bf16[256,512]{1,0:T(8,128)(2,1)}, u32[]{:S(2)}, u32[]{:S(2)}) collective-permute-start(bf16[256,512]{1,0:T(8,128)(2,1)} %get-tuple-element.127), channel_id=1, source_target_pairs={{0,12},{4,8},{8,4},{12,0},{16,28},{20,24},{24,20},{28,16},{1,13},{... | collective-permute-start | bytes 786440 | tf_op jit(solution)/shard_map/ppermute | solution.py:982
  145.1 25.3 %collective-permute-start.11 = (bf16[640,512]{1,0:T(8,128)(2,1)}, bf16[640,512]{1,0:T(8,128)(2,1)S(1)}, u32[]{:S(2)}, u32[]{:S(2)}) collective-permute-start(bf16[640,512]{1,0:T(8,128)(2,1)} %get-tuple-element.123), channel_id=1, source_target_pairs={{0,2},{1,3},{2,0},{3,1},{4,6},{5,7},{6,4},{7,5},{8,10},{9,11},{10,... | collective-permute-start | bytes 1966088 | tf_op jit(solution)/shard_map/ppermute | solution.py:982
  162.4 33.1 %collective-permute-start.18 = (bf16[256,768]{1,0:T(8,128)(2,1)}, bf16[256,768]{1,0:T(8,128)(2,1)S(1)}, u32[]{:S(2)}, u32[]{:S(2)}) collective-permute-start(bf16[256,768]{1,0:T(8,128)(2,1)} %get-tuple-element.139), channel_id=1, source_target_pairs={{0,1},{1,0},{2,3},{3,2},{4,5},{5,4},{6,7},{7,6},{8,9},{9,8},{10,11... | collective-permute-start | bytes 1179656 | tf_op jit(solution)/shard_map/ppermute | solution.py:982
  174.6 20.9 %collective-permute-start.15 = (bf16[160,512]{1,0:T(8,128)(2,1)}, bf16[160,512]{1,0:T(8,128)(2,1)S(1)}, u32[]{:S(2)}, u32[]{:S(2)}) collective-permute-start(bf16[160,512]{1,0:T(8,128)(2,1)} %get-tuple-element.135), channel_id=1, source_target_pairs={{0,4},{4,0},{8,12},{12,8},{16,20},{20,16},{24,28},{28,24},{1,5},{5... | collective-permute-start | bytes 491528 | tf_op jit(solution)/shard_map/ppermute | solution.py:982
  175.2 20.4 %collective-permute-start.16 = (bf16[160,512]{1,0:T(8,128)(2,1)}, bf16[160,512]{1,0:T(8,128)(2,1)S(1)}, u32[]{:S(2)}, u32[]{:S(2)}) collective-permute-start(bf16[160,512]{1,0:T(8,128)(2,1)} %get-tuple-element.136), channel_id=1, source_target_pairs={{0,8},{4,12},{8,0},{12,4},{16,24},{20,28},{24,16},{28,20},{1,9},{5... | collective-permute-start | bytes 491528 | tf_op jit(solution)/shard_map/ppermute | solution.py:982
  177.0 18.6 %collective-permute-start.17 = (bf16[160,512]{1,0:T(8,128)(2,1)}, bf16[160,512]{1,0:T(8,128)(2,1)S(1)}, u32[]{:S(2)}, u32[]{:S(2)}) collective-permute-start(bf16[160,512]{1,0:T(8,128)(2,1)} %get-tuple-element.137), channel_id=1, source_target_pairs={{0,12},{4,8},{8,4},{12,0},{16,28},{20,24},{24,20},{28,16},{1,13},{... | collective-permute-start | bytes 491528 | tf_op jit(solution)/shard_map/ppermute | solution.py:982
  195.4 11.2 %collective-permute-start.19 = (bf16[128,512]{1,0:T(8,128)(2,1)}, bf16[128,512]{1,0:T(8,128)(2,1)}, u32[]{:S(2)}, u32[]{:S(2)}) collective-permute-start(bf16[128,512]{1,0:T(8,128)(2,1)} %get-tuple-element.144), channel_id=1, source_target_pairs={{0,2},{1,3},{2,0},{3,1},{4,6},{5,7},{6,4},{7,5},{8,10},{9,11},{10,... | collective-permute-start | bytes 393224 | tf_op jit(solution)/shard_map/ppermute | solution.py:982
  214.3 21.6 %collective-permute-start.23 = (bf16[128,896]{1,0:T(8,128)(2,1)S(1)}, bf16[128,896]{1,0:T(8,128)(2,1)S(1)}, u32[]{:S(2)}, u32[]{:S(2)}) collective-permute-start(bf16[128,896]{1,0:T(8,128)(2,1)S(1)} %get-tuple-element.154), channel_id=1, source_target_pairs={{0,2},{1,3},{2,0},{3,1},{4,6},{5,7},{6,4},{7,5},{8,10},{9,11},{10,... | collective-permute-start | bytes 688136 | tf_op jit(solution)/shard_map/ppermute | solution.py:982
  215.3 25.9 %collective-permute-start.27 = (bf16[160,512]{1,0:T(8,128)(2,1)S(1)}, bf16[160,512]{1,0:T(8,128)(2,1)S(1)}, u32[]{:S(2)}, u32[]{:S(2)}) collective-permute-start(bf16[160,512]{1,0:T(8,128)(2,1)S(1)} %get-tuple-element.163.refs_0_), channel_id=1, source_target_pairs={{0,12},{4,8},{8,4},{12,0},{16,28},{20,24},{24,20},{28,16},{1,13},{... | collective-permute-start | bytes 491528 | tf_op jit(solution)/shard_map/ppermute | solution.py:982
  221.2 21.4 %collective-permute-start.26 = (bf16[160,512]{1,0:T(8,128)(2,1)S(1)}, bf16[160,512]{1,0:T(8,128)(2,1)S(1)}, u32[]{:S(2)}, u32[]{:S(2)}) collective-permute-start(bf16[160,512]{1,0:T(8,128)(2,1)S(1)} %get-tuple-element.163.refs_0_), channel_id=1, source_target_pairs={{0,8},{4,12},{8,0},{12,4},{16,24},{20,28},{24,16},{28,20},{1,9},{5... | collective-permute-start | bytes 491528 | tf_op jit(solution)/shard_map/ppermute | solution.py:982
  228.9 20.1 %collective-permute-start.25 = (bf16[160,512]{1,0:T(8,128)(2,1)S(1)}, bf16[160,512]{1,0:T(8,128)(2,1)S(1)}, u32[]{:S(2)}, u32[]{:S(2)}) collective-permute-start(bf16[160,512]{1,0:T(8,128)(2,1)S(1)} %get-tuple-element.163.refs_0_), channel_id=1, source_target_pairs={{0,4},{4,0},{8,12},{12,8},{16,20},{20,16},{24,28},{28,24},{1,5},{5... | collective-permute-start | bytes 491528 | tf_op jit(solution)/shard_map/ppermute | solution.py:982
  242.6 19.4 %collective-permute-start.30 = (bf16[128,512]{1,0:T(8,128)(2,1)S(1)}, bf16[128,512]{1,0:T(8,128)(2,1)S(1)}, u32[]{:S(2)}, u32[]{:S(2)}) collective-permute-start(bf16[128,512]{1,0:T(8,128)(2,1)S(1)} %get-tuple-element.164.refs_4_), channel_id=1, source_target_pairs={{0,12},{4,8},{8,4},{12,0},{16,28},{20,24},{24,20},{28,16},{1,13},{... | collective-permute-start | bytes 393224 | tf_op jit(solution)/shard_map/ppermute | solution.py:982
  (42 other events, 258.9 us)

commit v2 on v1

--- a/solution.py
+++ b/solution.py
@@ -291,7 +291,7 @@
             pltpu.SemaphoreType.DMA((PAIRS,)),
             pltpu.SemaphoreType.DMA((3,)),
         ],
-        compiler_params=pltpu.CompilerParams(vmem_limit_bytes=VMEM_LIMIT),
+        compiler_params=pltpu.CompilerParams(vmem_limit_bytes=40 * 2**20),
         cost_estimate=pl.CostEstimate(
             flops=8 * 10**9, bytes_accessed=24 * 10**6, transcendentals=8 * 10**6
         ),
@@ -443,10 +443,11 @@
             cols = slice(j * D, (j + 1) * D)
             up = nn(low, wi_ref[:, cols]) + vec(MEM + 3 + j)
             square = up * up
-            gate = 0.5 + 0.5 * jnp.tanh(up * (GELU_A + GELU_B * square))
+            bent = jnp.tanh(up * (GELU_A + GELU_B * square))
+            gate = 0.5 + 0.5 * bent
             active = up * gate
             slopes[here, cols] = (
-                gate + active * (2.0 - 2.0 * gate) * (GELU_A + 3.0 * GELU_B * square)
+                gate + active * (1.0 - bent) * (GELU_A + 3.0 * GELU_B * square)
             ).astype(slopes.dtype)
             actives[here, cols] = active.astype(BF16)
         second = second + nn(actives[here, :], wb_ref[...])
@@ -465,11 +466,13 @@
             grad_up = (
                 nt(down, wb_ref[cols, :]) * slopes[here, cols].astype(F32)
             ).astype(BF16)
-            acc_b[cols, :] += tn(actives[here, cols], down)
             ups[here, cols] = grad_up
             add_sum(MEM + 3 + j, grad_up.astype(F32))
-            acc_i[:, cols] += nn(low_t, grad_up)
         grad_first = s_gsecond[here] + nt(ups[here, :], wi_ref[...])
+        for j in range(BLOCKS):
+            cols = slice(j * D, (j + 1) * D)
+            acc_b[cols, :] += tn(actives[here, cols], down)
+            acc_i[:, cols] += nn(low_t, ups[here, cols])
         normed_one = s_normed1[here]
         add_sum(MEM + 4 + BLOCKS, grad_first * normed_one)
         add_sum(MEM + 5 + BLOCKS, grad_first)
@@ -580,7 +583,7 @@
             pltpu.VMEM((D, D), F32),
             pltpu.VMEM((D, FF), F32),
             pltpu.VMEM((FF, D), F32),
-            pltpu.VMEM((2 * TILE, FF), F32),
+            pltpu.VMEM((2 * TILE, FF), BF16),
             pltpu.VMEM((2 * TILE, FF), BF16),
             pltpu.VMEM((2 * TILE, D), F32),
             pltpu.VMEM((2 * TILE, D), BF16),
@@ -589,7 +592,7 @@
             pltpu.SemaphoreType.DMA((8 + 3 * shards,)),
             pltpu.SemaphoreType.DMA((3,)),
         ],
-        compiler_params=pltpu.CompilerParams(vmem_limit_bytes=VMEM_LIMIT),
+        compiler_params=pltpu.CompilerParams(vmem_limit_bytes=48 * 2**20),
         cost_estimate=pl.CostEstimate(
             flops=27 * 10**9, bytes_accessed=24 * 10**6, transcendentals=4 * 10**6
         ),

time: 272 us -> 272 us (level)
  Pallas kernels: 150 us -> 142 us
  local copies, waits for them, and re-layouts: 14.5 us -> 22.4 us
  starting transfers between devices: 64.4 us -> 70.4 us
  waiting for transfers between devices: 36.2 us -> 30.3 us
    unnamed x56 -> x72, local copies, waits for them, and re-layouts: 14.5 us -> 22.4 us
    ppermute x38, starting transfers between devices: 64.4 us -> 70.4 us  [exchange(): return lax.ppermute(value, axis, [(i, i ^ bit) for i in range(size)])]
    ppermute x38, waiting for transfers between devices: 36.2 us -> 30.3 us  [exchange(): return lax.ppermute(value, axis, [(i, i ^ bit) for i in range(size)])]
    pallas_call x2, Pallas kernels: 29.8 us -> 23.9 us  [attention_forward(): pl.pallas_call(partial(fwd_kernel, seq_rows, seq), out_shape=(jax.ShapeDt...]
  transfers between devices with their start and end apart: 38 -> 38, of which waited for: 8 -> 10; matrix products, arithmetic and copies ran while one was open for 0% -> 0% of each run, Pallas kernels for 36% -> 34%
where the time goes in v2:
time: 272 us; the launch traced here: 268 us
  Pallas kernels  142 us (52%)
  starting transfers between devices  70.4 us (26%)
  waiting for transfers between devices  30.3 us (11%)
  local copies, waits for them, and re-layouts  22.4 us (8%)
    ppermute x38, starting transfers between devices, exchange(): return lax.ppermute(value, axis, [(i, i ^ bit) for i in range(size)])  70.4 us
    pallas_call x4, Pallas kernels, attention_backward(): pl.pallas_call(partial(bwd_kernel, seq_rows, groups, group, seq, shards,...  48.5 us
    pallas_call x1, Pallas kernels, feed_forward(): pl.pallas_call(partial(ffn_kernel, seq_rows, shards), out_shape=(jax.Shap...  44.7 us
    ppermute x38, waiting for transfers between devices, exchange(): return lax.ppermute(value, axis, [(i, i ^ bit) for i in range(size)])  30.3 us
    pallas_call x2, Pallas kernels, attention_forward(): pl.pallas_call(partial(fwd_kernel, seq_rows, seq), out_shape=(jax.ShapeDt...  23.9 us
    unnamed x72, local copies, waits for them, and re-layouts  22.4 us
    pallas_call x2, Pallas kernels, input_gradient(): pl.pallas_call(partial(input_kernel, seq_rows, groups, seq), out_shape=(j...  11.4 us
    pallas_call x8, Pallas kernels, combine(): pl.pallas_call(partial(combine_kernel, [[len(g) for g in i[0]] for i in i...  10.4 us
  transfers between devices with their start and end apart: 38, of which 10 were waited for; matrix products, arithmetic and copies ran while one was open for 0% of the time, Pallas kernels for 34%

profile of v2, /device:TPU:0, one launch (start us, length us, event | category | flops | bytes accessed | tf_op | source)
XLA Modules:
  0.0 268.4 jit_solution(1966020529669900574)
XLA Ops:
  1.7 3.0 %collective-permute-start.1 = (bf16[144,1536]{1,0:T(8,128)(2,1)S(1)}, bf16[144,1536]{1,0:T(8,128)(2,1)S(1)}, u32[]{:S(2)}, u32[]{:S(2)}) collective-permute-start(bf16[144,1536]{1,0:T(8,128)(2,1)S(1)} %fusion.1.refs_0_), channel_id=1, source_target_pairs={{0,2},{1,3},{2,0},{3,1},{4,6},{5,7},{6,4},{7,5},{8,10},{9,11},{10,... | collective-permute-start | bytes 1327112 | tf_op jit(solution)/shard_map/ppermute | solution.py:985
  4.7 10.2 %collective-permute-done.1.refs_2_ = bf16[144,1536]{1,0:T(8,128)(2,1)S(1)} collective-permute-done((bf16[144,1536]{1,0:T(8,128)(2,1)S(1)}, bf16[144,1536]{1,0:T(8,128)(2,1)S(1)}, u32[]{:S(2)}, u32[]{:S(2)}) %collective-permute-start.1) | collective-permute-done | bytes 442400 | tf_op jit(solution)/shard_map/ppermute | solution.py:985
  25.0 5.5 %attention_forward.3 = (bf16[4,8,1056,256]{3,2,1,0:T(8,128)(2,1)}, bf16[512,1024]{1,0:T(8,128)(2,1)S(1)}, bf16[512,1024]{1,0:T(8,128)(2,1)S(1)}, f32[8,1024]{1,0:T(8,128)S(1)}) custom-call(s32[2]{0:T(128)S(1)} %copy-done.25, bf16[2,1024,512]{2,1,0:T(8,128)(2,1)S(1)} %copy-done.26, bf16[512,1536]{1,0:T(8,128)(2,1)S(1)} %get-tuple-element.92.wk_ref.refs_2_.refs_3_.w_ref, ...), custom_call_target="tpu_custom_call" | custom-call | flops 8000000000 | bytes 24000000 | tf_op jit(solution)/shard_map/attention_forward/pallas_call | solution.py:265
  32.5 6.3 %collective-permute-start.7 = (bf16[512,512]{1,0:T(8,128)(2,1)}, bf16[512,512]{1,0:T(8,128)(2,1)S(1)}, u32[]{:S(2)}, u32[]{:S(2)}) collective-permute-start(bf16[512,512]{1,0:T(8,128)(2,1)} %refs_4_), channel_id=1, source_target_pairs={{0,1},{1,0},{2,3},{3,2},{4,5},{5,4},{6,7},{7,6},{8,9},{9,8},{10,11... | collective-permute-start | bytes 1572872 | tf_op jit(solution)/shard_map/ppermute | solution.py:985
  38.8 5.8 %collective-permute-done.3.refs_2_ = bf16[128,2560]{1,0:T(8,128)(2,1)S(1)} collective-permute-done((bf16[128,2560]{1,0:T(8,128)(2,1)S(1)}, bf16[128,2560]{1,0:T(8,128)(2,1)S(1)}, u32[]{:S(2)}, u32[]{:S(2)}) %collective-permute-start.3) | collective-permute-done | bytes 655392 | tf_op jit(solution)/shard_map/ppermute | solution.py:985
  45.2 18.4 %attention_forward.2 = (bf16[4,8,1056,256]{3,2,1,0:T(8,128)(2,1)}, bf16[512,1024]{1,0:T(8,128)(2,1)S(1)}, bf16[512,1024]{1,0:T(8,128)(2,1)S(1)}, f32[8,1024]{1,0:T(8,128)S(1)}) custom-call(s32[2]{0:T(128)S(1)} %copy-done.25, bf16[2,1024,512]{2,1,0:T(8,128)(2,1)S(1)} %copy-done.26, bf16[512,1536]{1,0:T(8,128)(2,1)S(1)} %get-tuple-element.92.wk_ref.refs_2_.refs_3_.w_ref, ...), custom_call_target="tpu_custom_call" | custom-call | flops 8000000000 | bytes 24000000 | tf_op jit(solution)/shard_map/attention_forward/pallas_call | solution.py:265
  65.5 44.7 %feed_forward.1 = (bf16[2,1024,512]{2,1,0:T(8,128)(2,1)}, bf16[2,1024,512]{2,1,0:T(8,128)(2,1)}, bf16[2,512,1024]{2,1,0:T(8,128)(2,1)}, bf16[1280,512]{1,0:T(8,1...) custom-call(s32[2]{0:T(128)S(1)} %copy-done.25, ...), custom_call_target="tpu_custom_call" | custom-call | flops 27000000512 | bytes 24000000 | tf_op jit(solution)/shard_map/feed_forward/pallas_call | solution.py:557
  112.4 17.6 %attention_backward.4 = (bf16[1280,768]{1,0:T(8,128)(2,1)}, f32[512,768]{1,0:T(8,128)}, f32[32,512]{1,0:T(8,128)}, f32[8,128]{1,0:T(8,128)}) custom-call(s32[2]{0:T(128)} %len_ref.9, s32[1]{0:T(128)} %bitcast.me_ref.refs_1_, bf16[512,1536]{1,0:T(8,128)(2,1)} %copy-done, bf16[512,1536]{1,0:T(8,128)(2,1)} %copy-done, bf16[32,512]{1,0:T(8,128)(2,1)} %copy-done.27, ...), custom_call_target="tpu_custom_call" | custom-call | flops 8000000000 | bytes 15000000 | tf_op jit(solution)/shard_map/attention_backward/pallas_call | solution.py:837
  131.9 3.4 %combine.8 = (bf16[640,512]{1,0:T(8,128)(2,1)S(1)}, bf16[640,512]{1,0:T(8,128)(2,1)}, bf16[256,512]{1,0:T(8,128)(2,1)S(1)}, bf16[256,512]{1,0:T(8,128)(2,1)}, bf...) custom-call(s32[1]{0:T(128)} %bitcast.1.place_ref, bf16[1280,512]{1,0:T(8,128)(2,1)S(1)} %copy-done.1, ...), custom_call_target="tpu_custom_call" | custom-call | flops 4718592 | bytes 9437184 | tf_op jit(solution)/shard_map/combine/pallas_call | solution.py:1079
  136.0 10.0 %collective-permute-start.12 = (bf16[256,512]{1,0:T(8,128)(2,1)}, bf16[256,512]{1,0:T(8,128)(2,1)}, u32[]{:S(2)}, u32[]{:S(2)}) collective-permute-start(bf16[256,512]{1,0:T(8,128)(2,1)} %get-tuple-element.125), channel_id=1, source_target_pairs={{0,4},{4,0},{8,12},{12,8},{16,20},{20,16},{24,28},{28,24},{1,5},{5... | collective-permute-start | bytes 786440 | tf_op jit(solution)/shard_map/ppermute | solution.py:985
  146.1 5.9 %collective-permute-start.13 = (bf16[256,512]{1,0:T(8,128)(2,1)}, bf16[256,512]{1,0:T(8,128)(2,1)}, u32[]{:S(2)}, u32[]{:S(2)}) collective-permute-start(bf16[256,512]{1,0:T(8,128)(2,1)} %get-tuple-element.126), channel_id=1, source_target_pairs={{0,8},{4,12},{8,0},{12,4},{16,24},{20,28},{24,16},{28,20},{1,9},{5... | collective-permute-start | bytes 786440 | tf_op jit(solution)/shard_map/ppermute | solution.py:985
  152.0 6.7 %attention_backward.5 = (bf16[1280,768]{1,0:T(8,128)(2,1)}, bf16[256,768]{1,0:T(8,128)(2,1)}, bf16[256,768]{1,0:T(8,128)(2,1)}, f32[32,512]{1,0:T(8,128)}, f32[8,128]{1,0:T(8,128)}) custom-call(s32[2]{0:T(128)} %len_ref.9, s32[1]{0:T(128)} %bitcast.me_ref.refs_1_, bf16[512,1536]{1,0:T(8,128)(2,1)} %copy-done, bf16[512,1536]{1,0:T(8,128)(2,1)} %copy-done, ...), custom_call_target="tpu_custom_call" | custom-call | flops 8000000000 | bytes 15000000 | tf_op jit(solution)/shard_map/attention_backward/pallas_call | solution.py:837
  158.7 4.1 %collective-permute-start.18 = (bf16[256,768]{1,0:T(8,128)(2,1)}, bf16[256,768]{1,0:T(8,128)(2,1)S(1)}, u32[]{:S(2)}, u32[]{:S(2)}) collective-permute-start(bf16[256,768]{1,0:T(8,128)(2,1)} %get-tuple-element.139), channel_id=1, source_target_pairs={{0,1},{1,0},{2,3},{3,2},{4,5},{5,4},{6,7},{7,6},{8,9},{9,8},{10,11... | collective-permute-start | bytes 1179656 | tf_op jit(solution)/shard_map/ppermute | solution.py:985
  163.8 4.5 %collective-permute-done.11.refs_1_ = bf16[640,512]{1,0:T(8,128)(2,1)S(1)} collective-permute-done((bf16[640,512]{1,0:T(8,128)(2,1)}, bf16[640,512]{1,0:T(8,128)(2,1)S(1)}, u32[]{:S(2)}, u32[]{:S(2)}) %collective-permute-start.11) | collective-permute-done | bytes 655392 | tf_op jit(solution)/shard_map/ppermute | solution.py:985
  176.0 17.3 %attention_backward.6 = (bf16[1280,768]{1,0:T(8,128)(2,1)}, f32[512,768]{1,0:T(8,128)}, f32[32,512]{1,0:T(8,128)}, f32[8,128]{1,0:T(8,128)}) custom-call(s32[2]{0:T(128)} %len_ref.9, s32[1]{0:T(128)} %bitcast.me_ref.refs_1_, bf16[512,1536]{1,0:T(8,128)(2,1)} %copy-done, bf16[512,1536]{1,0:T(8,128)(2,1)} %copy-done, bf16[32,512]{1,0:T(8,128)(2,1)} %copy-done.27, ...), custom_call_target="tpu_custom_call" | custom-call | flops 8000000000 | bytes 15000000 | tf_op jit(solution)/shard_map/attention_backward/pallas_call | solution.py:837
  196.0 4.1 %collective-permute-start.21 = (bf16[160,512]{1,0:T(8,128)(2,1)S(1)}, bf16[160,512]{1,0:T(8,128)(2,1)S(1)}, u32[]{:S(2)}, u32[]{:S(2)}) collective-permute-start(bf16[160,512]{1,0:T(8,128)(2,1)S(1)} %get-tuple-element.147.refs_4_), channel_id=1, source_target_pairs={{0,16},{4,20},{8,24},{12,28},{16,0},{20,4},{24,8},{28,12},{1,17},{... | collective-permute-start | bytes 491528 | tf_op jit(solution)/shard_map/ppermute | solution.py:985
  200.2 6.9 %attention_backward.7 = (bf16[1280,768]{1,0:T(8,128)(2,1)}, bf16[256,896]{1,0:T(8,128)(2,1)}, bf16[256,896]{1,0:T(8,128)(2,1)}, f32[8,128]{1,0:T(8,128)}) custom-call(s32[2]{0:T(128)} %len_ref.9, s32[1]{0:T(128)} %bitcast.me_ref.refs_1_, bf16[512,1536]{1,0:T(8,128)(2,1)} %copy-done, bf16[512,1536]{1,0:T(8,128)(2,1)} %copy-done, bf16[32,512]{1,0:T(8,128)(2,1)} %copy-done.27, ...), custom_call_target="tpu_custom_call" | custom-call | flops 8000000000 | bytes 15000000 | tf_op jit(solution)/shard_map/attention_backward/pallas_call | solution.py:837
  210.5 3.0 %collective-permute-start.22 = (bf16[256,896]{1,0:T(8,128)(2,1)S(1)}, bf16[256,896]{1,0:T(8,128)(2,1)S(1)}, u32[]{:S(2)}, u32[]{:S(2)}) collective-permute-start(bf16[256,896]{1,0:T(8,128)(2,1)S(1)} %get-tuple-element.152), channel_id=1, source_target_pairs={{0,1},{1,0},{2,3},{3,2},{4,5},{5,4},{6,7},{7,6},{8,9},{9,8},{10,11... | collective-permute-start | bytes 1376264 | tf_op jit(solution)/shard_map/ppermute | solution.py:985
  216.7 6.0 %collective-permute-start.23 = (bf16[128,896]{1,0:T(8,128)(2,1)S(1)}, bf16[128,896]{1,0:T(8,128)(2,1)S(1)}, u32[]{:S(2)}, u32[]{:S(2)}) collective-permute-start(bf16[128,896]{1,0:T(8,128)(2,1)S(1)} %get-tuple-element.154), channel_id=1, source_target_pairs={{0,2},{1,3},{2,0},{3,1},{4,6},{5,7},{6,4},{7,5},{8,10},{9,11},{10,... | collective-permute-start | bytes 688136 | tf_op jit(solution)/shard_map/ppermute | solution.py:985
  222.6 2.7 %collective-permute-start.27 = (bf16[160,512]{1,0:T(8,128)(2,1)S(1)}, bf16[160,512]{1,0:T(8,128)(2,1)S(1)}, u32[]{:S(2)}, u32[]{:S(2)}) collective-permute-start(bf16[160,512]{1,0:T(8,128)(2,1)S(1)} %get-tuple-element.163.refs_0_), channel_id=1, source_target_pairs={{0,12},{4,8},{8,4},{12,0},{16,28},{20,24},{24,20},{28,16},{1,13},{... | collective-permute-start | bytes 491528 | tf_op jit(solution)/shard_map/ppermute | solution.py:985
  227.8 6.5 %input_gradient.2 = (bf16[2,1024,512]{2,1,0:T(8,128)(2,1)}, f32[8,128]{1,0:T(8,128)}) custom-call(s32[2]{0:T(128)} %len_ref.9, bf16[512,1536]{1,0:T(8,128)(2,1)} %copy-done, bf16[2,1024,512]{2,1,0:T(8,128)(2,1)} %get-tuple-element.107.gh_hbm, bf16[1280,768]{1,0:T(8,128)(2,1)} %get-tuple-element.156.refs_0_, bf16[1280,768]{1,0:T(8,128)(2,1)} %get-tuple-element.157.refs_1_, ...), custom_call_target="tpu_custom_call" | custom-call | flops 2000000000 | bytes 7000000 | tf_op jit(solution)/shard_map/input_gradient/pallas_call | solution.py:952
  243.1 4.9 %input_gradient.3 = (bf16[2,1024,512]{2,1,0:T(8,128)(2,1)}, f32[8,128]{1,0:T(8,128)}) custom-call(s32[2]{0:T(128)} %len_ref.9, bf16[512,1536]{1,0:T(8,128)(2,1)} %copy-done, bf16[2,1024,512]{2,1,0:T(8,128)(2,1)} %get-tuple-element.107.gh_hbm, bf16[1280,768]{1,0:T(8,128)(2,1)} %get-tuple-element.121.refs_0_, ...), custom_call_target="tpu_custom_call", output_to_operand_aliasing={{0}: (6, {})} | custom-call | flops 2000000000 | bytes 7000000 | tf_op jit(solution)/shard_map/input_gradient/pallas_call | solution.py:952
  252.5 3.1 %collective-permute-start.28 = (bf16[128,512]{1,0:T(8,128)(2,1)S(1)}, bf16[128,512]{1,0:T(8,128)(2,1)S(1)}, u32[]{:S(2)}, u32[]{:S(2)}) collective-permute-start(bf16[128,512]{1,0:T(8,128)(2,1)S(1)} %get-tuple-element.164.refs_4_), channel_id=1, source_target_pairs={{0,4},{4,0},{8,12},{12,8},{16,20},{20,16},{24,28},{28,24},{1,5},{5... | collective-permute-start | bytes 393224 | tf_op jit(solution)/shard_map/ppermute | solution.py:985
  258.8 2.7 %collective-permute-start.36 = (bf16[64,896]{1,0:T(8,128)(2,1)S(1)}, bf16[64,896]{1,0:T(8,128)(2,1)S(1)}, u32[]{:S(2)}, u32[]{:S(2)}) collective-permute-start(bf16[64,896]{1,0:T(8,128)(2,1)S(1)} %get-tuple-element.171.refs_8_), channel_id=1, source_target_pairs={{0,8},{4,12},{8,0},{12,4},{16,24},{20,28},{24,16},{28,20},{1,9},{5... | collective-permute-start | bytes 344072 | tf_op jit(solution)/shard_map/ppermute | solution.py:985
  (145 shorter events, 63.9 us)
Async XLA Ops:
  1.7 13.2 %collective-permute-start.1 = (bf16[144,1536]{1,0:T(8,128)(2,1)S(1)}, bf16[144,1536]{1,0:T(8,128)(2,1)S(1)}, u32[]{:S(2)}, u32[]{:S(2)}) collective-permute-start(bf16[144,1536]{1,0:T(8,128)(2,1)S(1)} %fusion.1.refs_0_), channel_id=1, source_target_pairs={{0,2},{1,3},{2,0},{3,1},{4,6},{5,7},{6,4},{7,5},{8,10},{9,11},{10,... | collective-permute-start | bytes 1327112 | tf_op jit(solution)/shard_map/ppermute | solution.py:985
  4.7 13.4 %collective-permute-start = (bf16[144,1536]{1,0:T(8,128)(2,1)S(1)}, bf16[144,1536]{1,0:T(8,128)(2,1)S(1)}, u32[]{:S(2)}, u32[]{:S(2)}) collective-permute-start(bf16[144,1536]{1,0:T(8,128)(2,1)S(1)} %fusion.1.refs_0_), channel_id=1, source_target_pairs={{0,1},{1,0},{2,3},{3,2},{4,5},{5,4},{6,7},{7,6},{8,9},{9,8},{10,11... | collective-permute-start | bytes 1327112 | tf_op jit(solution)/shard_map/ppermute | solution.py:985
  16.0 16.6 %collective-permute-start.6 = (bf16[512,512]{1,0:T(8,128)(2,1)}, bf16[512,512]{1,0:T(8,128)(2,1)S(1)}, u32[]{:S(2)}, u32[]{:S(2)}) collective-permute-start(bf16[512,512]{1,0:T(8,128)(2,1)} %refs_4_), channel_id=1, source_target_pairs={{0,2},{1,3},{2,0},{3,1},{4,6},{5,7},{6,4},{7,5},{8,10},{9,11},{10,... | collective-permute-start | bytes 1572872 | tf_op jit(solution)/shard_map/ppermute | solution.py:985
  17.8 26.9 %collective-permute-start.3 = (bf16[128,2560]{1,0:T(8,128)(2,1)S(1)}, bf16[128,2560]{1,0:T(8,128)(2,1)S(1)}, u32[]{:S(2)}, u32[]{:S(2)}) collective-permute-start(bf16[128,2560]{1,0:T(8,128)(2,1)S(1)} %pad_maximum_fusion.refs_0_), channel_id=1, source_target_pairs={{0,2},{1,3},{2,0},{3,1},{4,6},{5,7},{6,4},{7,5},{8,10},{9,11},{10,... | collective-permute-start | bytes 1966088 | tf_op jit(solution)/shard_map/ppermute | solution.py:985
  32.5 33.0 %collective-permute-start.7 = (bf16[512,512]{1,0:T(8,128)(2,1)}, bf16[512,512]{1,0:T(8,128)(2,1)S(1)}, u32[]{:S(2)}, u32[]{:S(2)}) collective-permute-start(bf16[512,512]{1,0:T(8,128)(2,1)} %refs_4_), channel_id=1, source_target_pairs={{0,1},{1,0},{2,3},{3,2},{4,5},{5,4},{6,7},{7,6},{8,9},{9,8},{10,11... | collective-permute-start | bytes 1572872 | tf_op jit(solution)/shard_map/ppermute | solution.py:985
  38.8 26.7 %collective-permute-start.8 = (bf16[512,512]{1,0:T(8,128)(2,1)S(1)}, bf16[512,512]{1,0:T(8,128)(2,1)S(1)}, u32[]{:S(2)}, u32[]{:S(2)}) collective-permute-start(bf16[512,512]{1,0:T(8,128)(2,1)S(1)} %collective-permute-done.6.refs_6_), channel_id=1, source_target_pairs={{0,1},{1,0},{2,3},{3,2},{4,5},{5,4},{6,7},{7,6},{8,9},{9,8},{10,11... | collective-permute-start | bytes 1572872 | tf_op jit(solution)/shard_map/ppermute | solution.py:985
  44.6 20.9 %collective-permute-start.4 = (bf16[128,2560]{1,0:T(8,128)(2,1)S(1)}, bf16[128,2560]{1,0:T(8,128)(2,1)S(1)}, u32[]{:S(2)}, u32[]{:S(2)}) collective-permute-start(bf16[128,2560]{1,0:T(8,128)(2,1)S(1)} %pad_maximum_fusion.refs_0_), channel_id=1, source_target_pairs={{0,1},{1,0},{2,3},{3,2},{4,5},{5,4},{6,7},{7,6},{8,9},{9,8},{10,11... | collective-permute-start | bytes 1966088 | tf_op jit(solution)/shard_map/ppermute | solution.py:985
  44.6 20.9 %collective-permute-start.5 = (bf16[128,2560]{1,0:T(8,128)(2,1)S(1)}, bf16[128,2560]{1,0:T(8,128)(2,1)S(1)}, u32[]{:S(2)}, u32[]{:S(2)}) collective-permute-start(bf16[128,2560]{1,0:T(8,128)(2,1)S(1)} %collective-permute-done.3.refs_2_), channel_id=1, source_target_pairs={{0,1},{1,0},{2,3},{3,2},{4,5},{5,4},{6,7},{7,6},{8,9},{9,8},{10,11... | collective-permute-start | bytes 1966088 | tf_op jit(solution)/shard_map/ppermute | solution.py:985
  111.9 18.1 %collective-permute-start.9 = (bf16[1280,512]{1,0:T(8,128)(2,1)}, bf16[1280,512]{1,0:T(8,128)(2,1)}, u32[]{:S(2)}, u32[]{:S(2)}) collective-permute-start(bf16[1280,512]{1,0:T(8,128)(2,1)} %get-tuple-element.116), channel_id=1, source_target_pairs={{0,1},{1,0},{2,3},{3,2},{4,5},{5,4},{6,7},{7,6},{8,9},{9,8},{10,11... | collective-permute-start | bytes 3932168 | tf_op jit(solution)/shard_map/ppermute | solution.py:985
  111.9 18.1 %collective-permute-start.10 = (bf16[1024,512]{1,0:T(8,128)(2,1)}, bf16[1024,512]{1,0:T(8,128)(2,1)}, u32[]{:S(2)}, u32[]{:S(2)}) collective-permute-start(bf16[1024,512]{1,0:T(8,128)(2,1)} %get-tuple-element.118), channel_id=1, source_target_pairs={{0,1},{1,0},{2,3},{3,2},{4,5},{5,4},{6,7},{7,6},{8,9},{9,8},{10,11... | collective-permute-start | bytes 3145736 | tf_op jit(solution)/shard_map/ppermute | solution.py:985
  136.0 26.8 %collective-permute-start.12 = (bf16[256,512]{1,0:T(8,128)(2,1)}, bf16[256,512]{1,0:T(8,128)(2,1)}, u32[]{:S(2)}, u32[]{:S(2)}) collective-permute-start(bf16[256,512]{1,0:T(8,128)(2,1)} %get-tuple-element.125), channel_id=1, source_target_pairs={{0,4},{4,0},{8,12},{12,8},{16,20},{20,16},{24,28},{28,24},{1,5},{5... | collective-permute-start | bytes 786440 | tf_op jit(solution)/shard_map/ppermute | solution.py:985
  146.1 16.7 %collective-permute-start.13 = (bf16[256,512]{1,0:T(8,128)(2,1)}, bf16[256,512]{1,0:T(8,128)(2,1)}, u32[]{:S(2)}, u32[]{:S(2)}) collective-permute-start(bf16[256,512]{1,0:T(8,128)(2,1)} %get-tuple-element.126), channel_id=1, source_target_pairs={{0,8},{4,12},{8,0},{12,4},{16,24},{20,28},{24,16},{28,20},{1,9},{5... | collective-permute-start | bytes 786440 | tf_op jit(solution)/shard_map/ppermute | solution.py:985
  152.0 11.8 %collective-permute-start.14 = (bf16[256,512]{1,0:T(8,128)(2,1)}, bf16[256,512]{1,0:T(8,128)(2,1)}, u32[]{:S(2)}, u32[]{:S(2)}) collective-permute-start(bf16[256,512]{1,0:T(8,128)(2,1)} %get-tuple-element.127), channel_id=1, source_target_pairs={{0,12},{4,8},{8,4},{12,0},{16,28},{20,24},{24,20},{28,16},{1,13},{... | collective-permute-start | bytes 786440 | tf_op jit(solution)/shard_map/ppermute | solution.py:985
  152.0 16.3 %collective-permute-start.11 = (bf16[640,512]{1,0:T(8,128)(2,1)}, bf16[640,512]{1,0:T(8,128)(2,1)S(1)}, u32[]{:S(2)}, u32[]{:S(2)}) collective-permute-start(bf16[640,512]{1,0:T(8,128)(2,1)} %get-tuple-element.123), channel_id=1, source_target_pairs={{0,2},{1,3},{2,0},{3,1},{4,6},{5,7},{6,4},{7,5},{8,10},{9,11},{10,... | collective-permute-start | bytes 1966088 | tf_op jit(solution)/shard_map/ppermute | solution.py:985
  158.7 35.1 %collective-permute-start.18 = (bf16[256,768]{1,0:T(8,128)(2,1)}, bf16[256,768]{1,0:T(8,128)(2,1)S(1)}, u32[]{:S(2)}, u32[]{:S(2)}) collective-permute-start(bf16[256,768]{1,0:T(8,128)(2,1)} %get-tuple-element.139), channel_id=1, source_target_pairs={{0,1},{1,0},{2,3},{3,2},{4,5},{5,4},{6,7},{7,6},{8,9},{9,8},{10,11... | collective-permute-start | bytes 1179656 | tf_op jit(solution)/shard_map/ppermute | solution.py:985
  172.5 21.3 %collective-permute-start.15 = (bf16[160,512]{1,0:T(8,128)(2,1)}, bf16[160,512]{1,0:T(8,128)(2,1)S(1)}, u32[]{:S(2)}, u32[]{:S(2)}) collective-permute-start(bf16[160,512]{1,0:T(8,128)(2,1)} %get-tuple-element.135), channel_id=1, source_target_pairs={{0,4},{4,0},{8,12},{12,8},{16,20},{20,16},{24,28},{28,24},{1,5},{5... | collective-permute-start | bytes 491528 | tf_op jit(solution)/shard_map/ppermute | solution.py:985
  174.0 19.8 %collective-permute-start.16 = (bf16[160,512]{1,0:T(8,128)(2,1)}, bf16[160,512]{1,0:T(8,128)(2,1)S(1)}, u32[]{:S(2)}, u32[]{:S(2)}) collective-permute-start(bf16[160,512]{1,0:T(8,128)(2,1)} %get-tuple-element.136), channel_id=1, source_target_pairs={{0,8},{4,12},{8,0},{12,4},{16,24},{20,28},{24,16},{28,20},{1,9},{5... | collective-permute-start | bytes 491528 | tf_op jit(solution)/shard_map/ppermute | solution.py:985
  175.7 18.1 %collective-permute-start.17 = (bf16[160,512]{1,0:T(8,128)(2,1)}, bf16[160,512]{1,0:T(8,128)(2,1)S(1)}, u32[]{:S(2)}, u32[]{:S(2)}) collective-permute-start(bf16[160,512]{1,0:T(8,128)(2,1)} %get-tuple-element.137), channel_id=1, source_target_pairs={{0,12},{4,8},{8,4},{12,0},{16,28},{20,24},{24,20},{28,16},{1,13},{... | collective-permute-start | bytes 491528 | tf_op jit(solution)/shard_map/ppermute | solution.py:985
  193.3 13.8 %collective-permute-start.19 = (bf16[128,512]{1,0:T(8,128)(2,1)}, bf16[128,512]{1,0:T(8,128)(2,1)}, u32[]{:S(2)}, u32[]{:S(2)}) collective-permute-start(bf16[128,512]{1,0:T(8,128)(2,1)} %get-tuple-element.144), channel_id=1, source_target_pairs={{0,2},{1,3},{2,0},{3,1},{4,6},{5,7},{6,4},{7,5},{8,10},{9,11},{10,... | collective-permute-start | bytes 393224 | tf_op jit(solution)/shard_map/ppermute | solution.py:985
  216.7 18.6 %collective-permute-start.23 = (bf16[128,896]{1,0:T(8,128)(2,1)S(1)}, bf16[128,896]{1,0:T(8,128)(2,1)S(1)}, u32[]{:S(2)}, u32[]{:S(2)}) collective-permute-start(bf16[128,896]{1,0:T(8,128)(2,1)S(1)} %get-tuple-element.154), channel_id=1, source_target_pairs={{0,2},{1,3},{2,0},{3,1},{4,6},{5,7},{6,4},{7,5},{8,10},{9,11},{10,... | collective-permute-start | bytes 688136 | tf_op jit(solution)/shard_map/ppermute | solution.py:985
  222.6 17.6 %collective-permute-start.27 = (bf16[160,512]{1,0:T(8,128)(2,1)S(1)}, bf16[160,512]{1,0:T(8,128)(2,1)S(1)}, u32[]{:S(2)}, u32[]{:S(2)}) collective-permute-start(bf16[160,512]{1,0:T(8,128)(2,1)S(1)} %get-tuple-element.163.refs_0_), channel_id=1, source_target_pairs={{0,12},{4,8},{8,4},{12,0},{16,28},{20,24},{24,20},{28,16},{1,13},{... | collective-permute-start | bytes 491528 | tf_op jit(solution)/shard_map/ppermute | solution.py:985
  225.4 16.3 %collective-permute-start.26 = (bf16[160,512]{1,0:T(8,128)(2,1)S(1)}, bf16[160,512]{1,0:T(8,128)(2,1)S(1)}, u32[]{:S(2)}, u32[]{:S(2)}) collective-permute-start(bf16[160,512]{1,0:T(8,128)(2,1)S(1)} %get-tuple-element.163.refs_0_), channel_id=1, source_target_pairs={{0,8},{4,12},{8,0},{12,4},{16,24},{20,28},{24,16},{28,20},{1,9},{5... | collective-permute-start | bytes 491528 | tf_op jit(solution)/shard_map/ppermute | solution.py:985
  225.4 22.7 %collective-permute-start.25 = (bf16[160,512]{1,0:T(8,128)(2,1)S(1)}, bf16[160,512]{1,0:T(8,128)(2,1)S(1)}, u32[]{:S(2)}, u32[]{:S(2)}) collective-permute-start(bf16[160,512]{1,0:T(8,128)(2,1)S(1)} %get-tuple-element.163.refs_0_), channel_id=1, source_target_pairs={{0,4},{4,0},{8,12},{12,8},{16,20},{20,16},{24,28},{28,24},{1,5},{5... | collective-permute-start | bytes 491528 | tf_op jit(solution)/shard_map/ppermute | solution.py:985
  241.7 19.9 %collective-permute-start.30 = (bf16[128,512]{1,0:T(8,128)(2,1)S(1)}, bf16[128,512]{1,0:T(8,128)(2,1)S(1)}, u32[]{:S(2)}, u32[]{:S(2)}) collective-permute-start(bf16[128,512]{1,0:T(8,128)(2,1)S(1)} %get-tuple-element.164.refs_4_), channel_id=1, source_target_pairs={{0,12},{4,8},{8,4},{12,0},{16,28},{20,24},{24,20},{28,16},{1,13},{... | collective-permute-start | bytes 393224 | tf_op jit(solution)/shard_map/ppermute | solution.py:985
  (50 other events, 313.6 us)

commit v3 on v2

--- a/solution.py
+++ b/solution.py
@@ -291,7 +291,7 @@
             pltpu.SemaphoreType.DMA((PAIRS,)),
             pltpu.SemaphoreType.DMA((3,)),
         ],
-        compiler_params=pltpu.CompilerParams(vmem_limit_bytes=40 * 2**20),
+        compiler_params=pltpu.CompilerParams(vmem_limit_bytes=44 * 2**20),
         cost_estimate=pl.CostEstimate(
             flops=8 * 10**9, bytes_accessed=24 * 10**6, transcendentals=8 * 10**6
         ),
@@ -592,7 +592,7 @@
             pltpu.SemaphoreType.DMA((8 + 3 * shards,)),
             pltpu.SemaphoreType.DMA((3,)),
         ],
-        compiler_params=pltpu.CompilerParams(vmem_limit_bytes=48 * 2**20),
+        compiler_params=pltpu.CompilerParams(vmem_limit_bytes=56 * 2**20),
         cost_estimate=pl.CostEstimate(
             flops=27 * 10**9, bytes_accessed=24 * 10**6, transcendentals=4 * 10**6
         ),
@@ -876,7 +876,7 @@
             pltpu.SemaphoreType.DMA,
             pltpu.SemaphoreType.DMA,
         ],
-        compiler_params=pltpu.CompilerParams(vmem_limit_bytes=VMEM_LIMIT),
+        compiler_params=pltpu.CompilerParams(vmem_limit_bytes=62 * 2**20),
         cost_estimate=pl.CostEstimate(
             flops=8 * 10**9, bytes_accessed=15 * 10**6, transcendentals=0
         ),

time: 272 us -> 272 us (level)
  waiting for transfers between devices: 30.3 us -> 43 us
  local copies, waits for them, and re-layouts: 22.4 us -> 14.1 us
  starting transfers between devices: 70.4 us -> 63 us
    ppermute x38, waiting for transfers between devices: 30.3 us -> 43 us  [exchange(): return lax.ppermute(value, axis, [(i, i ^ bit) for i in range(size)])]
    unnamed x72 -> x78, local copies, waits for them, and re-layouts: 22.4 us -> 14.1 us
    ppermute x38, starting transfers between devices: 70.4 us -> 63 us  [exchange(): return lax.ppermute(value, axis, [(i, i ^ bit) for i in range(size)])]
where the time goes in v3:
time: 272 us; the launch traced here: 267 us
  Pallas kernels  144 us (53%)
  starting transfers between devices  63 us (23%)
  waiting for transfers between devices  43 us (16%)
  local copies, waits for them, and re-layouts  14.1 us (5%)
    ppermute x38, starting transfers between devices, exchange(): return lax.ppermute(value, axis, [(i, i ^ bit) for i in range(size)])  63 us
    pallas_call x4, Pallas kernels, attention_backward(): pl.pallas_call(partial(bwd_kernel, seq_rows, groups, group, seq, shards,...  48.4 us
    pallas_call x1, Pallas kernels, feed_forward(): pl.pallas_call(partial(ffn_kernel, seq_rows, shards), out_shape=(jax.Shap...  46.4 us
    ppermute x38, waiting for transfers between devices, exchange(): return lax.ppermute(value, axis, [(i, i ^ bit) for i in range(size)])  43 us
    pallas_call x2, Pallas kernels, attention_forward(): pl.pallas_call(partial(fwd_kernel, seq_rows, seq), out_shape=(jax.ShapeDt...  23.9 us
    unnamed x78, local copies, waits for them, and re-layouts  14.1 us
    pallas_call x2, Pallas kernels, input_gradient(): pl.pallas_call(partial(input_kernel, seq_rows, groups, seq), out_shape=(j...  11.4 us
    pallas_call x8, Pallas kernels, combine(): pl.pallas_call(partial(combine_kernel, [[len(g) for g in i[0]] for i in i...  10.4 us
  transfers between devices with their start and end apart: 38, of which 10 were waited for; matrix products, arithmetic and copies ran while one was open for 0% of the time, Pallas kernels for 34%

profile of v3, /device:TPU:0, one launch (start us, length us, event | category | flops | bytes accessed | tf_op | source)
XLA Modules:
  0.0 267.3 jit_solution(8486337328613082465)
XLA Ops:
  1.7 3.0 %collective-permute-start.1 = (bf16[144,1536]{1,0:T(8,128)(2,1)S(1)}, bf16[144,1536]{1,0:T(8,128)(2,1)S(1)}, u32[]{:S(2)}, u32[]{:S(2)}) collective-permute-start(bf16[144,1536]{1,0:T(8,128)(2,1)S(1)} %fusion.1.refs_0_), channel_id=1, source_target_pairs={{0,2},{1,3},{2,0},{3,1},{4,6},{5,7},{6,4},{7,5},{8,10},{9,11},{10,... | collective-permute-start | bytes 1327112 | tf_op jit(solution)/shard_map/ppermute | solution.py:985
  4.7 10.2 %collective-permute-done.1.refs_2_ = bf16[144,1536]{1,0:T(8,128)(2,1)S(1)} collective-permute-done((bf16[144,1536]{1,0:T(8,128)(2,1)S(1)}, bf16[144,1536]{1,0:T(8,128)(2,1)S(1)}, u32[]{:S(2)}, u32[]{:S(2)}) %collective-permute-start.1) | collective-permute-done | bytes 442400 | tf_op jit(solution)/shard_map/ppermute | solution.py:985
  19.5 5.6 %attention_forward.3 = (bf16[4,8,1056,256]{3,2,1,0:T(8,128)(2,1)}, bf16[512,1024]{1,0:T(8,128)(2,1)S(1)}, bf16[512,1024]{1,0:T(8,128)(2,1)S(1)}, f32[8,1024]{1,0:T(8,128)S(1)}) custom-call(s32[2]{0:T(128)S(1)} %copy-done.20, bf16[2,1024,512]{2,1,0:T(8,128)(2,1)S(1)} %copy-done.21, bf16[512,1536]{1,0:T(8,128)(2,1)S(1)} %get-tuple-element.92.wk_ref.refs_2_.refs_3_.w_ref, ...), custom_call_target="tpu_custom_call" | custom-call | flops 8000000000 | bytes 24000000 | tf_op jit(solution)/shard_map/attention_forward/pallas_call | solution.py:265
  25.1 6.0 %collective-permute-done.6.refs_6_ = bf16[512,512]{1,0:T(8,128)(2,1)S(1)} collective-permute-done((bf16[512,512]{1,0:T(8,128)(2,1)}, bf16[512,512]{1,0:T(8,128)(2,1)S(1)}, u32[]{:S(2)}, u32[]{:S(2)}) %collective-permute-start.6) | collective-permute-done | bytes 524320 | tf_op jit(solution)/shard_map/ppermute | solution.py:985
  31.7 13.1 %collective-permute-done.3.refs_2_ = bf16[128,2560]{1,0:T(8,128)(2,1)S(1)} collective-permute-done((bf16[128,2560]{1,0:T(8,128)(2,1)S(1)}, bf16[128,2560]{1,0:T(8,128)(2,1)S(1)}, u32[]{:S(2)}, u32[]{:S(2)}) %collective-permute-start.3) | collective-permute-done | bytes 655392 | tf_op jit(solution)/shard_map/ppermute | solution.py:985
  45.3 18.4 %attention_forward.2 = (bf16[4,8,1056,256]{3,2,1,0:T(8,128)(2,1)}, bf16[512,1024]{1,0:T(8,128)(2,1)S(1)}, bf16[512,1024]{1,0:T(8,128)(2,1)S(1)}, f32[8,1024]{1,0:T(8,128)S(1)}) custom-call(s32[2]{0:T(128)S(1)} %copy-done.20, bf16[2,1024,512]{2,1,0:T(8,128)(2,1)S(1)} %copy-done.21, bf16[512,1536]{1,0:T(8,128)(2,1)S(1)} %get-tuple-element.92.wk_ref.refs_2_.refs_3_.w_ref, ...), custom_call_target="tpu_custom_call" | custom-call | flops 8000000000 | bytes 24000000 | tf_op jit(solution)/shard_map/attention_forward/pallas_call | solution.py:265
  66.8 46.4 %feed_forward.1 = (bf16[2,1024,512]{2,1,0:T(8,128)(2,1)}, bf16[2,1024,512]{2,1,0:T(8,128)(2,1)}, bf16[2,512,1024]{2,1,0:T(8,128)(2,1)}, bf16[1280,512]{1,0:T(8,1...) custom-call(s32[2]{0:T(128)} %len_ref.9, ...), custom_call_target="tpu_custom_call" | custom-call | flops 27000000512 | bytes 24000000 | tf_op jit(solution)/shard_map/feed_forward/pallas_call | solution.py:557
  113.2 9.5 %collective-permute-start.9 = (bf16[1280,512]{1,0:T(8,128)(2,1)}, bf16[1280,512]{1,0:T(8,128)(2,1)}, u32[]{:S(2)}, u32[]{:S(2)}) collective-permute-start(bf16[1280,512]{1,0:T(8,128)(2,1)} %get-tuple-element.116), channel_id=1, source_target_pairs={{0,1},{1,0},{2,3},{3,2},{4,5},{5,4},{6,7},{7,6},{8,9},{9,8},{10,11... | collective-permute-start | bytes 3932168 | tf_op jit(solution)/shard_map/ppermute | solution.py:985
  122.8 17.5 %attention_backward.4 = (bf16[1280,768]{1,0:T(8,128)(2,1)}, f32[512,768]{1,0:T(8,128)}, f32[32,512]{1,0:T(8,128)}, f32[8,128]{1,0:T(8,128)}) custom-call(s32[2]{0:T(128)} %len_ref.9, s32[1]{0:T(128)} %bitcast.me_ref.refs_1_, bf16[512,1536]{1,0:T(8,128)(2,1)} %copy-done, bf16[512,1536]{1,0:T(8,128)(2,1)} %copy-done, bf16[32,512]{1,0:T(8,128)(2,1)} %copy-done.22, ...), custom_call_target="tpu_custom_call" | custom-call | flops 8000000000 | bytes 15000000 | tf_op jit(solution)/shard_map/attention_backward/pallas_call | solution.py:837
  142.3 3.4 %combine.8 = (bf16[640,512]{1,0:T(8,128)(2,1)S(1)}, bf16[640,512]{1,0:T(8,128)(2,1)}, bf16[256,512]{1,0:T(8,128)(2,1)S(1)}, bf16[256,512]{1,0:T(8,128)(2,1)}, bf...) custom-call(s32[1]{0:T(128)} %bitcast.1.place_ref, bf16[1280,512]{1,0:T(8,128)(2,1)S(1)} %copy-done.1, ...), custom_call_target="tpu_custom_call" | custom-call | flops 4718592 | bytes 9437184 | tf_op jit(solution)/shard_map/combine/pallas_call | solution.py:1079
  146.4 3.5 %collective-permute-start.14 = (bf16[256,512]{1,0:T(8,128)(2,1)}, bf16[256,512]{1,0:T(8,128)(2,1)}, u32[]{:S(2)}, u32[]{:S(2)}) collective-permute-start(bf16[256,512]{1,0:T(8,128)(2,1)} %get-tuple-element.127), channel_id=1, source_target_pairs={{0,12},{4,8},{8,4},{12,0},{16,28},{20,24},{24,20},{28,16},{1,13},{... | collective-permute-start | bytes 786440 | tf_op jit(solution)/shard_map/ppermute | solution.py:985
  149.8 5.5 %collective-permute-start.11 = (bf16[640,512]{1,0:T(8,128)(2,1)}, bf16[640,512]{1,0:T(8,128)(2,1)S(1)}, u32[]{:S(2)}, u32[]{:S(2)}) collective-permute-start(bf16[640,512]{1,0:T(8,128)(2,1)} %get-tuple-element.123), channel_id=1, source_target_pairs={{0,2},{1,3},{2,0},{3,1},{4,6},{5,7},{6,4},{7,5},{8,10},{9,11},{10,... | collective-permute-start | bytes 1966088 | tf_op jit(solution)/shard_map/ppermute | solution.py:985
  155.3 6.7 %attention_backward.5 = (bf16[1280,768]{1,0:T(8,128)(2,1)}, bf16[256,768]{1,0:T(8,128)(2,1)}, bf16[256,768]{1,0:T(8,128)(2,1)}, f32[32,512]{1,0:T(8,128)}, f32[8,128]{1,0:T(8,128)}) custom-call(s32[2]{0:T(128)} %len_ref.9, s32[1]{0:T(128)} %bitcast.me_ref.refs_1_, bf16[512,1536]{1,0:T(8,128)(2,1)} %copy-done, bf16[512,1536]{1,0:T(8,128)(2,1)} %copy-done, ...), custom_call_target="tpu_custom_call" | custom-call | flops 8000000000 | bytes 15000000 | tf_op jit(solution)/shard_map/attention_backward/pallas_call | solution.py:837
  162.0 3.4 %collective-permute-start.18 = (bf16[256,768]{1,0:T(8,128)(2,1)}, bf16[256,768]{1,0:T(8,128)(2,1)S(1)}, u32[]{:S(2)}, u32[]{:S(2)}) collective-permute-start(bf16[256,768]{1,0:T(8,128)(2,1)} %get-tuple-element.139), channel_id=1, source_target_pairs={{0,1},{1,0},{2,3},{3,2},{4,5},{5,4},{6,7},{7,6},{8,9},{9,8},{10,11... | collective-permute-start | bytes 1179656 | tf_op jit(solution)/shard_map/ppermute | solution.py:985
  165.4 4.0 %collective-permute-done.11.refs_1_ = bf16[640,512]{1,0:T(8,128)(2,1)S(1)} collective-permute-done((bf16[640,512]{1,0:T(8,128)(2,1)}, bf16[640,512]{1,0:T(8,128)(2,1)S(1)}, u32[]{:S(2)}, u32[]{:S(2)}) %collective-permute-start.11) | collective-permute-done | bytes 655392 | tf_op jit(solution)/shard_map/ppermute | solution.py:985
  177.2 17.3 %attention_backward.6 = (bf16[1280,768]{1,0:T(8,128)(2,1)}, f32[512,768]{1,0:T(8,128)}, f32[32,512]{1,0:T(8,128)}, f32[8,128]{1,0:T(8,128)}) custom-call(s32[2]{0:T(128)} %len_ref.9, s32[1]{0:T(128)} %bitcast.me_ref.refs_1_, bf16[512,1536]{1,0:T(8,128)(2,1)} %copy-done, bf16[512,1536]{1,0:T(8,128)(2,1)} %copy-done, bf16[32,512]{1,0:T(8,128)(2,1)} %copy-done.22, ...), custom_call_target="tpu_custom_call" | custom-call | flops 8000000000 | bytes 15000000 | tf_op jit(solution)/shard_map/attention_backward/pallas_call | solution.py:837
  197.5 2.6 collective-permute-start.21
  200.1 6.9 %attention_backward.7 = (bf16[1280,768]{1,0:T(8,128)(2,1)}, bf16[256,896]{1,0:T(8,128)(2,1)}, bf16[256,896]{1,0:T(8,128)(2,1)}, f32[8,128]{1,0:T(8,128)}) custom-call(s32[2]{0:T(128)} %len_ref.9, s32[1]{0:T(128)} %bitcast.me_ref.refs_1_, bf16[512,1536]{1,0:T(8,128)(2,1)} %copy-done, bf16[512,1536]{1,0:T(8,128)(2,1)} %copy-done, bf16[32,512]{1,0:T(8,128)(2,1)} %copy-done.22, ...), custom_call_target="tpu_custom_call" | custom-call | flops 8000000000 | bytes 15000000 | tf_op jit(solution)/shard_map/attention_backward/pallas_call | solution.py:837
  214.8 10.1 %collective-permute-start.23 = (bf16[128,896]{1,0:T(8,128)(2,1)S(1)}, bf16[128,896]{1,0:T(8,128)(2,1)S(1)}, u32[]{:S(2)}, u32[]{:S(2)}) collective-permute-start(bf16[128,896]{1,0:T(8,128)(2,1)S(1)} %get-tuple-element.154), channel_id=1, source_target_pairs={{0,2},{1,3},{2,0},{3,1},{4,6},{5,7},{6,4},{7,5},{8,10},{9,11},{10,... | collective-permute-start | bytes 688136 | tf_op jit(solution)/shard_map/ppermute | solution.py:985
  224.9 3.4 %collective-permute-start.25 = (bf16[160,512]{1,0:T(8,128)(2,1)S(1)}, bf16[160,512]{1,0:T(8,128)(2,1)S(1)}, u32[]{:S(2)}, u32[]{:S(2)}) collective-permute-start(bf16[160,512]{1,0:T(8,128)(2,1)S(1)} %get-tuple-element.163.refs_0_), channel_id=1, source_target_pairs={{0,4},{4,0},{8,12},{12,8},{16,20},{20,16},{24,28},{28,24},{1,5},{5... | collective-permute-start | bytes 491528 | tf_op jit(solution)/shard_map/ppermute | solution.py:985
  228.7 6.5 %input_gradient.2 = (bf16[2,1024,512]{2,1,0:T(8,128)(2,1)}, f32[8,128]{1,0:T(8,128)}) custom-call(s32[2]{0:T(128)} %len_ref.9, bf16[512,1536]{1,0:T(8,128)(2,1)} %copy-done, bf16[2,1024,512]{2,1,0:T(8,128)(2,1)} %get-tuple-element.107.gh_hbm, bf16[1280,768]{1,0:T(8,128)(2,1)} %get-tuple-element.156.refs_0_, bf16[1280,768]{1,0:T(8,128)(2,1)} %get-tuple-element.157.refs_1_, ...), custom_call_target="tpu_custom_call" | custom-call | flops 2000000000 | bytes 7000000 | tf_op jit(solution)/shard_map/input_gradient/pallas_call | solution.py:952
  244.1 4.9 %input_gradient.3 = (bf16[2,1024,512]{2,1,0:T(8,128)(2,1)}, f32[8,128]{1,0:T(8,128)}) custom-call(s32[2]{0:T(128)} %len_ref.9, bf16[512,1536]{1,0:T(8,128)(2,1)} %copy-done, bf16[2,1024,512]{2,1,0:T(8,128)(2,1)} %get-tuple-element.107.gh_hbm, bf16[1280,768]{1,0:T(8,128)(2,1)} %get-tuple-element.121.refs_0_, ...), custom_call_target="tpu_custom_call", output_to_operand_aliasing={{0}: (6, {})} | custom-call | flops 2000000000 | bytes 7000000 | tf_op jit(solution)/shard_map/input_gradient/pallas_call | solution.py:952
  251.7 2.5 collective-permute-start.29
  254.8 3.0 %collective-permute-done.34.refs_1_ = bf16[64,896]{1,0:T(8,128)(2,1)S(1)} collective-permute-done((bf16[64,896]{1,0:T(8,128)(2,1)S(1)}, bf16[64,896]{1,0:T(8,128)(2,1)S(1)}, u32[]{:S(2)}, u32[]{:S(2)}) %collective-permute-start.34) | collective-permute-done | bytes 114720 | tf_op jit(solution)/shard_map/ppermute | solution.py:985
  (151 shorter events, 52.5 us)
Async XLA Ops:
  1.7 13.2 %collective-permute-start.1 = (bf16[144,1536]{1,0:T(8,128)(2,1)S(1)}, bf16[144,1536]{1,0:T(8,128)(2,1)S(1)}, u32[]{:S(2)}, u32[]{:S(2)}) collective-permute-start(bf16[144,1536]{1,0:T(8,128)(2,1)S(1)} %fusion.1.refs_0_), channel_id=1, source_target_pairs={{0,2},{1,3},{2,0},{3,1},{4,6},{5,7},{6,4},{7,5},{8,10},{9,11},{10,... | collective-permute-start | bytes 1327112 | tf_op jit(solution)/shard_map/ppermute | solution.py:985
  4.7 13.5 %collective-permute-start = (bf16[144,1536]{1,0:T(8,128)(2,1)S(1)}, bf16[144,1536]{1,0:T(8,128)(2,1)S(1)}, u32[]{:S(2)}, u32[]{:S(2)}) collective-permute-start(bf16[144,1536]{1,0:T(8,128)(2,1)S(1)} %fusion.1.refs_0_), channel_id=1, source_target_pairs={{0,1},{1,0},{2,3},{3,2},{4,5},{5,4},{6,7},{7,6},{8,9},{9,8},{10,11... | collective-permute-start | bytes 1327112 | tf_op jit(solution)/shard_map/ppermute | solution.py:985
  16.1 15.0 %collective-permute-start.6 = (bf16[512,512]{1,0:T(8,128)(2,1)}, bf16[512,512]{1,0:T(8,128)(2,1)S(1)}, u32[]{:S(2)}, u32[]{:S(2)}) collective-permute-start(bf16[512,512]{1,0:T(8,128)(2,1)} %refs_4_), channel_id=1, source_target_pairs={{0,2},{1,3},{2,0},{3,1},{4,6},{5,7},{6,4},{7,5},{8,10},{9,11},{10,... | collective-permute-start | bytes 1572872 | tf_op jit(solution)/shard_map/ppermute | solution.py:985
  17.9 26.9 %collective-permute-start.3 = (bf16[128,2560]{1,0:T(8,128)(2,1)S(1)}, bf16[128,2560]{1,0:T(8,128)(2,1)S(1)}, u32[]{:S(2)}, u32[]{:S(2)}) collective-permute-start(bf16[128,2560]{1,0:T(8,128)(2,1)S(1)} %pad_maximum_fusion.refs_0_), channel_id=1, source_target_pairs={{0,2},{1,3},{2,0},{3,1},{4,6},{5,7},{6,4},{7,5},{8,10},{9,11},{10,... | collective-permute-start | bytes 1966088 | tf_op jit(solution)/shard_map/ppermute | solution.py:985
  31.1 34.2 %collective-permute-start.7 = (bf16[512,512]{1,0:T(8,128)(2,1)}, bf16[512,512]{1,0:T(8,128)(2,1)S(1)}, u32[]{:S(2)}, u32[]{:S(2)}) collective-permute-start(bf16[512,512]{1,0:T(8,128)(2,1)} %refs_4_), channel_id=1, source_target_pairs={{0,1},{1,0},{2,3},{3,2},{4,5},{5,4},{6,7},{7,6},{8,9},{9,8},{10,11... | collective-permute-start | bytes 1572872 | tf_op jit(solution)/shard_map/ppermute | solution.py:985
  31.4 34.0 %collective-permute-start.8 = (bf16[512,512]{1,0:T(8,128)(2,1)S(1)}, bf16[512,512]{1,0:T(8,128)(2,1)S(1)}, u32[]{:S(2)}, u32[]{:S(2)}) collective-permute-start(bf16[512,512]{1,0:T(8,128)(2,1)S(1)} %collective-permute-done.6.refs_6_), channel_id=1, source_target_pairs={{0,1},{1,0},{2,3},{3,2},{4,5},{5,4},{6,7},{7,6},{8,9},{9,8},{10,11... | collective-permute-start | bytes 1572872 | tf_op jit(solution)/shard_map/ppermute | solution.py:985
  44.8 20.6 %collective-permute-start.4 = (bf16[128,2560]{1,0:T(8,128)(2,1)S(1)}, bf16[128,2560]{1,0:T(8,128)(2,1)S(1)}, u32[]{:S(2)}, u32[]{:S(2)}) collective-permute-start(bf16[128,2560]{1,0:T(8,128)(2,1)S(1)} %pad_maximum_fusion.refs_0_), channel_id=1, source_target_pairs={{0,1},{1,0},{2,3},{3,2},{4,5},{5,4},{6,7},{7,6},{8,9},{9,8},{10,11... | collective-permute-start | bytes 1966088 | tf_op jit(solution)/shard_map/ppermute | solution.py:985
  44.8 20.6 %collective-permute-start.5 = (bf16[128,2560]{1,0:T(8,128)(2,1)S(1)}, bf16[128,2560]{1,0:T(8,128)(2,1)S(1)}, u32[]{:S(2)}, u32[]{:S(2)}) collective-permute-start(bf16[128,2560]{1,0:T(8,128)(2,1)S(1)} %collective-permute-done.3.refs_2_), channel_id=1, source_target_pairs={{0,1},{1,0},{2,3},{3,2},{4,5},{5,4},{6,7},{7,6},{8,9},{9,8},{10,11... | collective-permute-start | bytes 1966088 | tf_op jit(solution)/shard_map/ppermute | solution.py:985
  113.2 27.1 %collective-permute-start.9 = (bf16[1280,512]{1,0:T(8,128)(2,1)}, bf16[1280,512]{1,0:T(8,128)(2,1)}, u32[]{:S(2)}, u32[]{:S(2)}) collective-permute-start(bf16[1280,512]{1,0:T(8,128)(2,1)} %get-tuple-element.116), channel_id=1, source_target_pairs={{0,1},{1,0},{2,3},{3,2},{4,5},{5,4},{6,7},{7,6},{8,9},{9,8},{10,11... | collective-permute-start | bytes 3932168 | tf_op jit(solution)/shard_map/ppermute | solution.py:985
  122.7 17.6 %collective-permute-start.10 = (bf16[1024,512]{1,0:T(8,128)(2,1)}, bf16[1024,512]{1,0:T(8,128)(2,1)}, u32[]{:S(2)}, u32[]{:S(2)}) collective-permute-start(bf16[1024,512]{1,0:T(8,128)(2,1)} %get-tuple-element.118), channel_id=1, source_target_pairs={{0,1},{1,0},{2,3},{3,2},{4,5},{5,4},{6,7},{7,6},{8,9},{9,8},{10,11... | collective-permute-start | bytes 3145736 | tf_op jit(solution)/shard_map/ppermute | solution.py:985
  146.3 19.0 %collective-permute-start.12 = (bf16[256,512]{1,0:T(8,128)(2,1)}, bf16[256,512]{1,0:T(8,128)(2,1)}, u32[]{:S(2)}, u32[]{:S(2)}) collective-permute-start(bf16[256,512]{1,0:T(8,128)(2,1)} %get-tuple-element.125), channel_id=1, source_target_pairs={{0,4},{4,0},{8,12},{12,8},{16,20},{20,16},{24,28},{28,24},{1,5},{5... | collective-permute-start | bytes 786440 | tf_op jit(solution)/shard_map/ppermute | solution.py:985
  146.4 19.0 %collective-permute-start.13 = (bf16[256,512]{1,0:T(8,128)(2,1)}, bf16[256,512]{1,0:T(8,128)(2,1)}, u32[]{:S(2)}, u32[]{:S(2)}) collective-permute-start(bf16[256,512]{1,0:T(8,128)(2,1)} %get-tuple-element.126), channel_id=1, source_target_pairs={{0,8},{4,12},{8,0},{12,4},{16,24},{20,28},{24,16},{28,20},{1,9},{5... | collective-permute-start | bytes 786440 | tf_op jit(solution)/shard_map/ppermute | solution.py:985
  146.4 19.0 %collective-permute-start.14 = (bf16[256,512]{1,0:T(8,128)(2,1)}, bf16[256,512]{1,0:T(8,128)(2,1)}, u32[]{:S(2)}, u32[]{:S(2)}) collective-permute-start(bf16[256,512]{1,0:T(8,128)(2,1)} %get-tuple-element.127), channel_id=1, source_target_pairs={{0,12},{4,8},{8,4},{12,0},{16,28},{20,24},{24,20},{28,16},{1,13},{... | collective-permute-start | bytes 786440 | tf_op jit(solution)/shard_map/ppermute | solution.py:985
  149.8 19.6 %collective-permute-start.11 = (bf16[640,512]{1,0:T(8,128)(2,1)}, bf16[640,512]{1,0:T(8,128)(2,1)S(1)}, u32[]{:S(2)}, u32[]{:S(2)}) collective-permute-start(bf16[640,512]{1,0:T(8,128)(2,1)} %get-tuple-element.123), channel_id=1, source_target_pairs={{0,2},{1,3},{2,0},{3,1},{4,6},{5,7},{6,4},{7,5},{8,10},{9,11},{10,... | collective-permute-start | bytes 1966088 | tf_op jit(solution)/shard_map/ppermute | solution.py:985
  162.0 33.3 %collective-permute-start.18 = (bf16[256,768]{1,0:T(8,128)(2,1)}, bf16[256,768]{1,0:T(8,128)(2,1)S(1)}, u32[]{:S(2)}, u32[]{:S(2)}) collective-permute-start(bf16[256,768]{1,0:T(8,128)(2,1)} %get-tuple-element.139), channel_id=1, source_target_pairs={{0,1},{1,0},{2,3},{3,2},{4,5},{5,4},{6,7},{7,6},{8,9},{9,8},{10,11... | collective-permute-start | bytes 1179656 | tf_op jit(solution)/shard_map/ppermute | solution.py:985
  173.7 21.6 %collective-permute-start.15 = (bf16[160,512]{1,0:T(8,128)(2,1)}, bf16[160,512]{1,0:T(8,128)(2,1)S(1)}, u32[]{:S(2)}, u32[]{:S(2)}) collective-permute-start(bf16[160,512]{1,0:T(8,128)(2,1)} %get-tuple-element.135), channel_id=1, source_target_pairs={{0,4},{4,0},{8,12},{12,8},{16,20},{20,16},{24,28},{28,24},{1,5},{5... | collective-permute-start | bytes 491528 | tf_op jit(solution)/shard_map/ppermute | solution.py:985
  175.7 19.5 %collective-permute-start.16 = (bf16[160,512]{1,0:T(8,128)(2,1)}, bf16[160,512]{1,0:T(8,128)(2,1)S(1)}, u32[]{:S(2)}, u32[]{:S(2)}) collective-permute-start(bf16[160,512]{1,0:T(8,128)(2,1)} %get-tuple-element.136), channel_id=1, source_target_pairs={{0,8},{4,12},{8,0},{12,4},{16,24},{20,28},{24,16},{28,20},{1,9},{5... | collective-permute-start | bytes 491528 | tf_op jit(solution)/shard_map/ppermute | solution.py:985
  175.7 19.5 %collective-permute-start.17 = (bf16[160,512]{1,0:T(8,128)(2,1)}, bf16[160,512]{1,0:T(8,128)(2,1)S(1)}, u32[]{:S(2)}, u32[]{:S(2)}) collective-permute-start(bf16[160,512]{1,0:T(8,128)(2,1)} %get-tuple-element.137), channel_id=1, source_target_pairs={{0,12},{4,8},{8,4},{12,0},{16,28},{20,24},{24,20},{28,16},{1,13},{... | collective-permute-start | bytes 491528 | tf_op jit(solution)/shard_map/ppermute | solution.py:985
  194.5 12.5 %collective-permute-start.19 = (bf16[128,512]{1,0:T(8,128)(2,1)}, bf16[128,512]{1,0:T(8,128)(2,1)}, u32[]{:S(2)}, u32[]{:S(2)}) collective-permute-start(bf16[128,512]{1,0:T(8,128)(2,1)} %get-tuple-element.144), channel_id=1, source_target_pairs={{0,2},{1,3},{2,0},{3,1},{4,6},{5,7},{6,4},{7,5},{8,10},{9,11},{10,... | collective-permute-start | bytes 393224 | tf_op jit(solution)/shard_map/ppermute | solution.py:985
  214.8 22.0 %collective-permute-start.23 = (bf16[128,896]{1,0:T(8,128)(2,1)S(1)}, bf16[128,896]{1,0:T(8,128)(2,1)S(1)}, u32[]{:S(2)}, u32[]{:S(2)}) collective-permute-start(bf16[128,896]{1,0:T(8,128)(2,1)S(1)} %get-tuple-element.154), channel_id=1, source_target_pairs={{0,2},{1,3},{2,0},{3,1},{4,6},{5,7},{6,4},{7,5},{8,10},{9,11},{10,... | collective-permute-start | bytes 688136 | tf_op jit(solution)/shard_map/ppermute | solution.py:985
  224.9 16.3 %collective-permute-start.27 = (bf16[160,512]{1,0:T(8,128)(2,1)S(1)}, bf16[160,512]{1,0:T(8,128)(2,1)S(1)}, u32[]{:S(2)}, u32[]{:S(2)}) collective-permute-start(bf16[160,512]{1,0:T(8,128)(2,1)S(1)} %get-tuple-element.163.refs_0_), channel_id=1, source_target_pairs={{0,12},{4,8},{8,4},{12,0},{16,28},{20,24},{24,20},{28,16},{1,13},{... | collective-permute-start | bytes 491528 | tf_op jit(solution)/shard_map/ppermute | solution.py:985
  224.9 17.6 %collective-permute-start.26 = (bf16[160,512]{1,0:T(8,128)(2,1)S(1)}, bf16[160,512]{1,0:T(8,128)(2,1)S(1)}, u32[]{:S(2)}, u32[]{:S(2)}) collective-permute-start(bf16[160,512]{1,0:T(8,128)(2,1)S(1)} %get-tuple-element.163.refs_0_), channel_id=1, source_target_pairs={{0,8},{4,12},{8,0},{12,4},{16,24},{20,28},{24,16},{28,20},{1,9},{5... | collective-permute-start | bytes 491528 | tf_op jit(solution)/shard_map/ppermute | solution.py:985
  224.9 24.1 %collective-permute-start.25 = (bf16[160,512]{1,0:T(8,128)(2,1)S(1)}, bf16[160,512]{1,0:T(8,128)(2,1)S(1)}, u32[]{:S(2)}, u32[]{:S(2)}) collective-permute-start(bf16[160,512]{1,0:T(8,128)(2,1)S(1)} %get-tuple-element.163.refs_0_), channel_id=1, source_target_pairs={{0,4},{4,0},{8,12},{12,8},{16,20},{20,16},{24,28},{28,24},{1,5},{5... | collective-permute-start | bytes 491528 | tf_op jit(solution)/shard_map/ppermute | solution.py:985
  242.5 17.9 %collective-permute-start.30 = (bf16[128,512]{1,0:T(8,128)(2,1)S(1)}, bf16[128,512]{1,0:T(8,128)(2,1)S(1)}, u32[]{:S(2)}, u32[]{:S(2)}) collective-permute-start(bf16[128,512]{1,0:T(8,128)(2,1)S(1)} %get-tuple-element.164.refs_4_), channel_id=1, source_target_pairs={{0,12},{4,8},{8,4},{12,0},{16,28},{20,24},{24,20},{28,16},{1,13},{... | collective-permute-start | bytes 393224 | tf_op jit(solution)/shard_map/ppermute | solution.py:985
  (53 other events, 524.4 us)

commit v4 on v3

--- a/solution.py
+++ b/solution.py
@@ -1205,15 +1205,15 @@
 
     axis = ("shard", shards)
     far = far_pieces(pack(w_qkv, vectors), *axis)
-    start = held_until(
-        {0: jnp.concatenate([w_out, w_in], 1), 1: w_back}, far[max(far)]
-    )
-    far_up, far_back = far_pieces(start[0], *axis), far_pieces(start[1], *axis)
+    start = held_until({0: jnp.concatenate([w_out, w_in], 1)}, far[max(far)])
+    far_up = far_pieces(start[0], *axis)
     whole, wqt, wvt, table = prepare(me, near_pieces(far, *axis))
     fwd = [
         attention_forward(s, lengths, inputs, whole, wqt, wvt, table) for s in range(count)
     ]
-    far_up, far_back = held_until(far_up, fwd[-1][3]), held_until(far_back, fwd[-1][3])
+    far_up = held_until(far_up, fwd[-1][3])
+    far_back = far_pieces(held_until({0: w_back}, fwd[-1][3])[0], *axis)
+    far_back = held_until(far_back, fwd[0][3])
     out, gh, dot, *grads, sums = feed_forward(
         lengths, me, inputs, cotangent, [f[2] for f in fwd], [f[3] for f in fwd],
         near_pieces(far_up, *axis), near_pieces(far_back, *axis), table,

time: 272 us -> 266 us (0.978)
  waiting for transfers between devices: 43 us -> 26.8 us
  starting transfers between devices: 63 us -> 74.2 us
    ppermute x38, waiting for transfers between devices: 43 us -> 26.8 us  [exchange(): return lax.ppermute(value, axis, [(i, i ^ bit) for i in range(size)])]
    ppermute x38, starting transfers between devices: 63 us -> 74.2 us  [exchange(): return lax.ppermute(value, axis, [(i, i ^ bit) for i in range(size)])]
    unnamed x78 -> x80, local copies, waits for them, and re-layouts: 14.1 us -> 14.4 us
where the time goes in v4:
time: 266 us; the launch traced here: 263 us
  Pallas kernels  144 us (54%)
  starting transfers between devices  74.2 us (28%)
  waiting for transfers between devices  26.8 us (10%)
  local copies, waits for them, and re-layouts  14.4 us (5%)
    ppermute x38, starting transfers between devices, exchange(): return lax.ppermute(value, axis, [(i, i ^ bit) for i in range(size)])  74.2 us
    pallas_call x4, Pallas kernels, attention_backward(): pl.pallas_call(partial(bwd_kernel, seq_rows, groups, group, seq, shards,...  48.5 us
    pallas_call x1, Pallas kernels, feed_forward(): pl.pallas_call(partial(ffn_kernel, seq_rows, shards), out_shape=(jax.Shap...  46.4 us
    ppermute x38, waiting for transfers between devices, exchange(): return lax.ppermute(value, axis, [(i, i ^ bit) for i in range(size)])  26.8 us
    pallas_call x2, Pallas kernels, attention_forward(): pl.pallas_call(partial(fwd_kernel, seq_rows, seq), out_shape=(jax.ShapeDt...  24 us
    unnamed x80, local copies, waits for them, and re-layouts  14.4 us
    pallas_call x2, Pallas kernels, input_gradient(): pl.pallas_call(partial(input_kernel, seq_rows, groups, seq), out_shape=(j...  11.4 us
    pallas_call x8, Pallas kernels, combine(): pl.pallas_call(partial(combine_kernel, [[len(g) for g in i[0]] for i in i...  10.4 us
  transfers between devices with their start and end apart: 38, of which 10 were waited for; matrix products, arithmetic and copies ran while one was open for 0% of the time, Pallas kernels for 34%

profile of v4, /device:TPU:0, one launch (start us, length us, event | category | flops | bytes accessed | tf_op | source)
XLA Modules:
  0.0 262.8 jit_solution(7651323735769591984)
XLA Ops:
  1.7 3.0 %collective-permute-start.1 = (bf16[144,1536]{1,0:T(8,128)(2,1)S(1)}, bf16[144,1536]{1,0:T(8,128)(2,1)S(1)}, u32[]{:S(2)}, u32[]{:S(2)}) collective-permute-start(bf16[144,1536]{1,0:T(8,128)(2,1)S(1)} %fusion.1.refs_0_), channel_id=1, source_target_pairs={{0,2},{1,3},{2,0},{3,1},{4,6},{5,7},{6,4},{7,5},{8,10},{9,11},{10,... | collective-permute-start | bytes 1327112 | tf_op jit(solution)/shard_map/ppermute | solution.py:985
  4.7 10.2 %collective-permute-done.1.refs_2_ = bf16[144,1536]{1,0:T(8,128)(2,1)S(1)} collective-permute-done((bf16[144,1536]{1,0:T(8,128)(2,1)S(1)}, bf16[144,1536]{1,0:T(8,128)(2,1)S(1)}, u32[]{:S(2)}, u32[]{:S(2)}) %collective-permute-start.1) | collective-permute-done | bytes 442400 | tf_op jit(solution)/shard_map/ppermute | solution.py:985
  19.2 5.6 %attention_forward.3 = (bf16[4,8,1056,256]{3,2,1,0:T(8,128)(2,1)}, bf16[512,1024]{1,0:T(8,128)(2,1)S(1)}, bf16[512,1024]{1,0:T(8,128)(2,1)S(1)}, f32[8,1024]{1,0:T(8,128)S(1)}) custom-call(s32[2]{0:T(128)S(1)} %copy-done.20, bf16[2,1024,512]{2,1,0:T(8,128)(2,1)S(1)} %copy-done.21, bf16[512,1536]{1,0:T(8,128)(2,1)S(1)} %get-tuple-element.92.wk_ref.refs_2_.refs_3_.w_ref, ...), custom_call_target="tpu_custom_call" | custom-call | flops 8000000000 | bytes 24000000 | tf_op jit(solution)/shard_map/attention_forward/pallas_call | solution.py:265
  24.9 2.4 collective-permute-start.6
  27.3 6.0 %collective-permute-done.3.refs_2_ = bf16[128,2560]{1,0:T(8,128)(2,1)S(1)} collective-permute-done((bf16[128,2560]{1,0:T(8,128)(2,1)S(1)}, bf16[128,2560]{1,0:T(8,128)(2,1)S(1)}, u32[]{:S(2)}, u32[]{:S(2)}) %collective-permute-start.3) | collective-permute-done | bytes 655392 | tf_op jit(solution)/shard_map/ppermute | solution.py:985
  33.4 4.5 %collective-permute-start.4 = (bf16[128,2560]{1,0:T(8,128)(2,1)S(1)}, bf16[128,2560]{1,0:T(8,128)(2,1)S(1)}, u32[]{:S(2)}, u32[]{:S(2)}) collective-permute-start(bf16[128,2560]{1,0:T(8,128)(2,1)S(1)} %pad_maximum_fusion.refs_0_), channel_id=1, source_target_pairs={{0,1},{1,0},{2,3},{3,2},{4,5},{5,4},{6,7},{7,6},{8,9},{9,8},{10,11... | collective-permute-start | bytes 1966088 | tf_op jit(solution)/shard_map/ppermute | solution.py:985
  38.0 18.4 %attention_forward.2 = (bf16[4,8,1056,256]{3,2,1,0:T(8,128)(2,1)}, bf16[512,1024]{1,0:T(8,128)(2,1)S(1)}, bf16[512,1024]{1,0:T(8,128)(2,1)S(1)}, f32[8,1024]{1,0:T(8,128)S(1)}) custom-call(s32[2]{0:T(128)S(1)} %copy-done.20, bf16[2,1024,512]{2,1,0:T(8,128)(2,1)S(1)} %copy-done.21, bf16[512,1536]{1,0:T(8,128)(2,1)S(1)} %get-tuple-element.92.wk_ref.refs_2_.refs_3_.w_ref, ...), custom_call_target="tpu_custom_call" | custom-call | flops 8000000000 | bytes 24000000 | tf_op jit(solution)/shard_map/attention_forward/pallas_call | solution.py:265
  61.5 46.4 %feed_forward.1 = (bf16[2,1024,512]{2,1,0:T(8,128)(2,1)}, bf16[2,1024,512]{2,1,0:T(8,128)(2,1)}, bf16[2,512,1024]{2,1,0:T(8,128)(2,1)}, bf16[1280,512]{1,0:T(8,1...) custom-call(s32[2]{0:T(128)} %len_ref.9, ...), custom_call_target="tpu_custom_call" | custom-call | flops 27000000512 | bytes 24000000 | tf_op jit(solution)/shard_map/feed_forward/pallas_call | solution.py:557
  107.9 4.7 %collective-permute-start.9 = (bf16[1280,512]{1,0:T(8,128)(2,1)}, bf16[1280,512]{1,0:T(8,128)(2,1)}, u32[]{:S(2)}, u32[]{:S(2)}) collective-permute-start(bf16[1280,512]{1,0:T(8,128)(2,1)} %get-tuple-element.116), channel_id=1, source_target_pairs={{0,1},{1,0},{2,3},{3,2},{4,5},{5,4},{6,7},{7,6},{8,9},{9,8},{10,11... | collective-permute-start | bytes 3932168 | tf_op jit(solution)/shard_map/ppermute | solution.py:985
  112.7 17.6 %attention_backward.4 = (bf16[1280,768]{1,0:T(8,128)(2,1)}, f32[512,768]{1,0:T(8,128)}, f32[32,512]{1,0:T(8,128)}, f32[8,128]{1,0:T(8,128)}) custom-call(s32[2]{0:T(128)} %len_ref.9, s32[1]{0:T(128)} %bitcast.me_ref.refs_1_, bf16[512,1536]{1,0:T(8,128)(2,1)} %copy-done, bf16[512,1536]{1,0:T(8,128)(2,1)} %copy-done, bf16[32,512]{1,0:T(8,128)(2,1)} %copy-done.22, ...), custom_call_target="tpu_custom_call" | custom-call | flops 8000000000 | bytes 15000000 | tf_op jit(solution)/shard_map/attention_backward/pallas_call | solution.py:837
  132.2 3.4 %combine.8 = (bf16[640,512]{1,0:T(8,128)(2,1)S(1)}, bf16[640,512]{1,0:T(8,128)(2,1)}, bf16[256,512]{1,0:T(8,128)(2,1)S(1)}, bf16[256,512]{1,0:T(8,128)(2,1)}, bf...) custom-call(s32[1]{0:T(128)} %bitcast.1.place_ref, bf16[1280,512]{1,0:T(8,128)(2,1)S(1)} %copy-done.1, ...), custom_call_target="tpu_custom_call" | custom-call | flops 4718592 | bytes 9437184 | tf_op jit(solution)/shard_map/combine/pallas_call | solution.py:1079
  136.3 9.6 %collective-permute-start.12 = (bf16[256,512]{1,0:T(8,128)(2,1)}, bf16[256,512]{1,0:T(8,128)(2,1)}, u32[]{:S(2)}, u32[]{:S(2)}) collective-permute-start(bf16[256,512]{1,0:T(8,128)(2,1)} %get-tuple-element.125), channel_id=1, source_target_pairs={{0,4},{4,0},{8,12},{12,8},{16,20},{20,16},{24,28},{28,24},{1,5},{5... | collective-permute-start | bytes 786440 | tf_op jit(solution)/shard_map/ppermute | solution.py:985
  147.4 6.7 %attention_backward.5 = (bf16[1280,768]{1,0:T(8,128)(2,1)}, bf16[256,768]{1,0:T(8,128)(2,1)}, bf16[256,768]{1,0:T(8,128)(2,1)}, f32[32,512]{1,0:T(8,128)}, f32[8,128]{1,0:T(8,128)}) custom-call(s32[2]{0:T(128)} %len_ref.9, s32[1]{0:T(128)} %bitcast.me_ref.refs_1_, bf16[512,1536]{1,0:T(8,128)(2,1)} %copy-done, bf16[512,1536]{1,0:T(8,128)(2,1)} %copy-done, ...), custom_call_target="tpu_custom_call" | custom-call | flops 8000000000 | bytes 15000000 | tf_op jit(solution)/shard_map/attention_backward/pallas_call | solution.py:837
  154.1 9.8 %collective-permute-start.18 = (bf16[256,768]{1,0:T(8,128)(2,1)}, bf16[256,768]{1,0:T(8,128)(2,1)S(1)}, u32[]{:S(2)}, u32[]{:S(2)}) collective-permute-start(bf16[256,768]{1,0:T(8,128)(2,1)} %get-tuple-element.139), channel_id=1, source_target_pairs={{0,1},{1,0},{2,3},{3,2},{4,5},{5,4},{6,7},{7,6},{8,9},{9,8},{10,11... | collective-permute-start | bytes 1179656 | tf_op jit(solution)/shard_map/ppermute | solution.py:985
  164.6 2.3 combine.9
  169.4 2.2 collective-permute-start.17
  171.7 17.3 %attention_backward.6 = (bf16[1280,768]{1,0:T(8,128)(2,1)}, f32[512,768]{1,0:T(8,128)}, f32[32,512]{1,0:T(8,128)}, f32[8,128]{1,0:T(8,128)}) custom-call(s32[2]{0:T(128)} %len_ref.9, s32[1]{0:T(128)} %bitcast.me_ref.refs_1_, bf16[512,1536]{1,0:T(8,128)(2,1)} %copy-done, bf16[512,1536]{1,0:T(8,128)(2,1)} %copy-done, bf16[32,512]{1,0:T(8,128)(2,1)} %copy-done.22, ...), custom_call_target="tpu_custom_call" | custom-call | flops 8000000000 | bytes 15000000 | tf_op jit(solution)/shard_map/attention_backward/pallas_call | solution.py:837
  191.3 3.9 %collective-permute-start.21 = (bf16[160,512]{1,0:T(8,128)(2,1)S(1)}, bf16[160,512]{1,0:T(8,128)(2,1)S(1)}, u32[]{:S(2)}, u32[]{:S(2)}) collective-permute-start(bf16[160,512]{1,0:T(8,128)(2,1)S(1)} %get-tuple-element.147.refs_4_), channel_id=1, source_target_pairs={{0,16},{4,20},{8,24},{12,28},{16,0},{20,4},{24,8},{28,12},{1,17},{... | collective-permute-start | bytes 491528 | tf_op jit(solution)/shard_map/ppermute | solution.py:985
  195.2 6.9 %attention_backward.7 = (bf16[1280,768]{1,0:T(8,128)(2,1)}, bf16[256,896]{1,0:T(8,128)(2,1)}, bf16[256,896]{1,0:T(8,128)(2,1)}, f32[8,128]{1,0:T(8,128)}) custom-call(s32[2]{0:T(128)} %len_ref.9, s32[1]{0:T(128)} %bitcast.me_ref.refs_1_, bf16[512,1536]{1,0:T(8,128)(2,1)} %copy-done, bf16[512,1536]{1,0:T(8,128)(2,1)} %copy-done, bf16[32,512]{1,0:T(8,128)(2,1)} %copy-done.22, ...), custom_call_target="tpu_custom_call" | custom-call | flops 8000000000 | bytes 15000000 | tf_op jit(solution)/shard_map/attention_backward/pallas_call | solution.py:837
  205.5 8.7 %collective-permute-start.22 = (bf16[256,896]{1,0:T(8,128)(2,1)S(1)}, bf16[256,896]{1,0:T(8,128)(2,1)S(1)}, u32[]{:S(2)}, u32[]{:S(2)}) collective-permute-start(bf16[256,896]{1,0:T(8,128)(2,1)S(1)} %get-tuple-element.152), channel_id=1, source_target_pairs={{0,1},{1,0},{2,3},{3,2},{4,5},{5,4},{6,7},{7,6},{8,9},{9,8},{10,11... | collective-permute-start | bytes 1376264 | tf_op jit(solution)/shard_map/ppermute | solution.py:985
  222.6 6.5 %input_gradient.2 = (bf16[2,1024,512]{2,1,0:T(8,128)(2,1)}, f32[8,128]{1,0:T(8,128)}) custom-call(s32[2]{0:T(128)} %len_ref.9, bf16[512,1536]{1,0:T(8,128)(2,1)} %copy-done, bf16[2,1024,512]{2,1,0:T(8,128)(2,1)} %get-tuple-element.107.gh_hbm, bf16[1280,768]{1,0:T(8,128)(2,1)} %get-tuple-element.156.refs_0_, bf16[1280,768]{1,0:T(8,128)(2,1)} %get-tuple-element.157.refs_1_, ...), custom_call_target="tpu_custom_call" | custom-call | flops 2000000000 | bytes 7000000 | tf_op jit(solution)/shard_map/input_gradient/pallas_call | solution.py:952
  237.4 4.9 %input_gradient.3 = (bf16[2,1024,512]{2,1,0:T(8,128)(2,1)}, f32[8,128]{1,0:T(8,128)}) custom-call(s32[2]{0:T(128)} %len_ref.9, bf16[512,1536]{1,0:T(8,128)(2,1)} %copy-done, bf16[2,1024,512]{2,1,0:T(8,128)(2,1)} %get-tuple-element.107.gh_hbm, bf16[1280,768]{1,0:T(8,128)(2,1)} %get-tuple-element.121.refs_0_, ...), custom_call_target="tpu_custom_call", output_to_operand_aliasing={{0}: (6, {})} | custom-call | flops 2000000000 | bytes 7000000 | tf_op jit(solution)/shard_map/input_gradient/pallas_call | solution.py:952
  243.6 3.2 %collective-permute-start.34 = (bf16[64,896]{1,0:T(8,128)(2,1)S(1)}, bf16[64,896]{1,0:T(8,128)(2,1)S(1)}, u32[]{:S(2)}, u32[]{:S(2)}) collective-permute-start(bf16[64,896]{1,0:T(8,128)(2,1)S(1)} %get-tuple-element.170.refs_0_), channel_id=1, source_target_pairs={{0,16},{4,20},{8,24},{12,28},{16,0},{20,4},{24,8},{28,12},{1,17},{... | collective-permute-start | bytes 344072 | tf_op jit(solution)/shard_map/ppermute | solution.py:985
  253.5 2.4 collective-permute-start.36
  (153 shorter events, 54.8 us)
Async XLA Ops:
  1.7 13.2 %collective-permute-start.1 = (bf16[144,1536]{1,0:T(8,128)(2,1)S(1)}, bf16[144,1536]{1,0:T(8,128)(2,1)S(1)}, u32[]{:S(2)}, u32[]{:S(2)}) collective-permute-start(bf16[144,1536]{1,0:T(8,128)(2,1)S(1)} %fusion.1.refs_0_), channel_id=1, source_target_pairs={{0,2},{1,3},{2,0},{3,1},{4,6},{5,7},{6,4},{7,5},{8,10},{9,11},{10,... | collective-permute-start | bytes 1327112 | tf_op jit(solution)/shard_map/ppermute | solution.py:985
  4.7 13.3 %collective-permute-start = (bf16[144,1536]{1,0:T(8,128)(2,1)S(1)}, bf16[144,1536]{1,0:T(8,128)(2,1)S(1)}, u32[]{:S(2)}, u32[]{:S(2)}) collective-permute-start(bf16[144,1536]{1,0:T(8,128)(2,1)S(1)} %fusion.1.refs_0_), channel_id=1, source_target_pairs={{0,1},{1,0},{2,3},{3,2},{4,5},{5,4},{6,7},{7,6},{8,9},{9,8},{10,11... | collective-permute-start | bytes 1327112 | tf_op jit(solution)/shard_map/ppermute | solution.py:985
  16.1 17.2 %collective-permute-start.3 = (bf16[128,2560]{1,0:T(8,128)(2,1)S(1)}, bf16[128,2560]{1,0:T(8,128)(2,1)S(1)}, u32[]{:S(2)}, u32[]{:S(2)}) collective-permute-start(bf16[128,2560]{1,0:T(8,128)(2,1)S(1)} %pad_maximum_fusion.refs_0_), channel_id=1, source_target_pairs={{0,2},{1,3},{2,0},{3,1},{4,6},{5,7},{6,4},{7,5},{8,10},{9,11},{10,... | collective-permute-start | bytes 1966088 | tf_op jit(solution)/shard_map/ppermute | solution.py:985
  24.9 33.1 %collective-permute-start.6 = (bf16[512,512]{1,0:T(8,128)(2,1)S(1)}, bf16[512,512]{1,0:T(8,128)(2,1)S(1)}, u32[]{:S(2)}, u32[]{:S(2)}) collective-permute-start(bf16[512,512]{1,0:T(8,128)(2,1)S(1)} %copy-done.36), channel_id=1, source_target_pairs={{0,2},{1,3},{2,0},{3,1},{4,6},{5,7},{6,4},{7,5},{8,10},{9,11},{10,... | collective-permute-start | bytes 1572872 | tf_op jit(solution)/shard_map/ppermute | solution.py:985
  33.4 25.2 %collective-permute-start.4 = (bf16[128,2560]{1,0:T(8,128)(2,1)S(1)}, bf16[128,2560]{1,0:T(8,128)(2,1)S(1)}, u32[]{:S(2)}, u32[]{:S(2)}) collective-permute-start(bf16[128,2560]{1,0:T(8,128)(2,1)S(1)} %pad_maximum_fusion.refs_0_), channel_id=1, source_target_pairs={{0,1},{1,0},{2,3},{3,2},{4,5},{5,4},{6,7},{7,6},{8,9},{9,8},{10,11... | collective-permute-start | bytes 1966088 | tf_op jit(solution)/shard_map/ppermute | solution.py:985
  37.9 20.6 %collective-permute-start.5 = (bf16[128,2560]{1,0:T(8,128)(2,1)S(1)}, bf16[128,2560]{1,0:T(8,128)(2,1)S(1)}, u32[]{:S(2)}, u32[]{:S(2)}) collective-permute-start(bf16[128,2560]{1,0:T(8,128)(2,1)S(1)} %collective-permute-done.3.refs_2_), channel_id=1, source_target_pairs={{0,1},{1,0},{2,3},{3,2},{4,5},{5,4},{6,7},{7,6},{8,9},{9,8},{10,11... | collective-permute-start | bytes 1966088 | tf_op jit(solution)/shard_map/ppermute | solution.py:985
  107.9 22.4 %collective-permute-start.9 = (bf16[1280,512]{1,0:T(8,128)(2,1)}, bf16[1280,512]{1,0:T(8,128)(2,1)}, u32[]{:S(2)}, u32[]{:S(2)}) collective-permute-start(bf16[1280,512]{1,0:T(8,128)(2,1)} %get-tuple-element.116), channel_id=1, source_target_pairs={{0,1},{1,0},{2,3},{3,2},{4,5},{5,4},{6,7},{7,6},{8,9},{9,8},{10,11... | collective-permute-start | bytes 3932168 | tf_op jit(solution)/shard_map/ppermute | solution.py:985
  112.6 17.7 %collective-permute-start.10 = (bf16[1024,512]{1,0:T(8,128)(2,1)}, bf16[1024,512]{1,0:T(8,128)(2,1)}, u32[]{:S(2)}, u32[]{:S(2)}) collective-permute-start(bf16[1024,512]{1,0:T(8,128)(2,1)} %get-tuple-element.118), channel_id=1, source_target_pairs={{0,1},{1,0},{2,3},{3,2},{4,5},{5,4},{6,7},{7,6},{8,9},{9,8},{10,11... | collective-permute-start | bytes 3145736 | tf_op jit(solution)/shard_map/ppermute | solution.py:985
  136.3 27.5 %collective-permute-start.12 = (bf16[256,512]{1,0:T(8,128)(2,1)}, bf16[256,512]{1,0:T(8,128)(2,1)}, u32[]{:S(2)}, u32[]{:S(2)}) collective-permute-start(bf16[256,512]{1,0:T(8,128)(2,1)} %get-tuple-element.125), channel_id=1, source_target_pairs={{0,4},{4,0},{8,12},{12,8},{16,20},{20,16},{24,28},{28,24},{1,5},{5... | collective-permute-start | bytes 786440 | tf_op jit(solution)/shard_map/ppermute | solution.py:985
  145.9 17.9 %collective-permute-start.13 = (bf16[256,512]{1,0:T(8,128)(2,1)}, bf16[256,512]{1,0:T(8,128)(2,1)}, u32[]{:S(2)}, u32[]{:S(2)}) collective-permute-start(bf16[256,512]{1,0:T(8,128)(2,1)} %get-tuple-element.126), channel_id=1, source_target_pairs={{0,8},{4,12},{8,0},{12,4},{16,24},{20,28},{24,16},{28,20},{1,9},{5... | collective-permute-start | bytes 786440 | tf_op jit(solution)/shard_map/ppermute | solution.py:985
  145.9 17.9 %collective-permute-start.14 = (bf16[256,512]{1,0:T(8,128)(2,1)}, bf16[256,512]{1,0:T(8,128)(2,1)}, u32[]{:S(2)}, u32[]{:S(2)}) collective-permute-start(bf16[256,512]{1,0:T(8,128)(2,1)} %get-tuple-element.127), channel_id=1, source_target_pairs={{0,12},{4,8},{8,4},{12,0},{16,28},{20,24},{24,20},{28,16},{1,13},{... | collective-permute-start | bytes 786440 | tf_op jit(solution)/shard_map/ppermute | solution.py:985
  147.4 16.5 %collective-permute-start.11 = (bf16[640,512]{1,0:T(8,128)(2,1)}, bf16[640,512]{1,0:T(8,128)(2,1)S(1)}, u32[]{:S(2)}, u32[]{:S(2)}) collective-permute-start(bf16[640,512]{1,0:T(8,128)(2,1)} %get-tuple-element.123), channel_id=1, source_target_pairs={{0,2},{1,3},{2,0},{3,1},{4,6},{5,7},{6,4},{7,5},{8,10},{9,11},{10,... | collective-permute-start | bytes 1966088 | tf_op jit(solution)/shard_map/ppermute | solution.py:985
  154.1 34.9 %collective-permute-start.18 = (bf16[256,768]{1,0:T(8,128)(2,1)}, bf16[256,768]{1,0:T(8,128)(2,1)S(1)}, u32[]{:S(2)}, u32[]{:S(2)}) collective-permute-start(bf16[256,768]{1,0:T(8,128)(2,1)} %get-tuple-element.139), channel_id=1, source_target_pairs={{0,1},{1,0},{2,3},{3,2},{4,5},{5,4},{6,7},{7,6},{8,9},{9,8},{10,11... | collective-permute-start | bytes 1179656 | tf_op jit(solution)/shard_map/ppermute | solution.py:985
  168.2 20.9 %collective-permute-start.15 = (bf16[160,512]{1,0:T(8,128)(2,1)}, bf16[160,512]{1,0:T(8,128)(2,1)S(1)}, u32[]{:S(2)}, u32[]{:S(2)}) collective-permute-start(bf16[160,512]{1,0:T(8,128)(2,1)} %get-tuple-element.135), channel_id=1, source_target_pairs={{0,4},{4,0},{8,12},{12,8},{16,20},{20,16},{24,28},{28,24},{1,5},{5... | collective-permute-start | bytes 491528 | tf_op jit(solution)/shard_map/ppermute | solution.py:985
  169.4 19.6 %collective-permute-start.16 = (bf16[160,512]{1,0:T(8,128)(2,1)}, bf16[160,512]{1,0:T(8,128)(2,1)S(1)}, u32[]{:S(2)}, u32[]{:S(2)}) collective-permute-start(bf16[160,512]{1,0:T(8,128)(2,1)} %get-tuple-element.136), channel_id=1, source_target_pairs={{0,8},{4,12},{8,0},{12,4},{16,24},{20,28},{24,16},{28,20},{1,9},{5... | collective-permute-start | bytes 491528 | tf_op jit(solution)/shard_map/ppermute | solution.py:985
  169.4 19.6 %collective-permute-start.17 = (bf16[160,512]{1,0:T(8,128)(2,1)}, bf16[160,512]{1,0:T(8,128)(2,1)S(1)}, u32[]{:S(2)}, u32[]{:S(2)}) collective-permute-start(bf16[160,512]{1,0:T(8,128)(2,1)} %get-tuple-element.137), channel_id=1, source_target_pairs={{0,12},{4,8},{8,4},{12,0},{16,28},{20,24},{24,20},{28,16},{1,13},{... | collective-permute-start | bytes 491528 | tf_op jit(solution)/shard_map/ppermute | solution.py:985
  189.0 13.2 %collective-permute-start.19 = (bf16[128,512]{1,0:T(8,128)(2,1)}, bf16[128,512]{1,0:T(8,128)(2,1)}, u32[]{:S(2)}, u32[]{:S(2)}) collective-permute-start(bf16[128,512]{1,0:T(8,128)(2,1)} %get-tuple-element.144), channel_id=1, source_target_pairs={{0,2},{1,3},{2,0},{3,1},{4,6},{5,7},{6,4},{7,5},{8,10},{9,11},{10,... | collective-permute-start | bytes 393224 | tf_op jit(solution)/shard_map/ppermute | solution.py:985
  191.3 10.9 %collective-permute-start.21 = (bf16[160,512]{1,0:T(8,128)(2,1)S(1)}, bf16[160,512]{1,0:T(8,128)(2,1)S(1)}, u32[]{:S(2)}, u32[]{:S(2)}) collective-permute-start(bf16[160,512]{1,0:T(8,128)(2,1)S(1)} %get-tuple-element.147.refs_4_), channel_id=1, source_target_pairs={{0,16},{4,20},{8,24},{12,28},{16,0},{20,4},{24,8},{28,12},{1,17},{... | collective-permute-start | bytes 491528 | tf_op jit(solution)/shard_map/ppermute | solution.py:985
  205.5 10.1 %collective-permute-start.22 = (bf16[256,896]{1,0:T(8,128)(2,1)S(1)}, bf16[256,896]{1,0:T(8,128)(2,1)S(1)}, u32[]{:S(2)}, u32[]{:S(2)}) collective-permute-start(bf16[256,896]{1,0:T(8,128)(2,1)S(1)} %get-tuple-element.152), channel_id=1, source_target_pairs={{0,1},{1,0},{2,3},{3,2},{4,5},{5,4},{6,7},{7,6},{8,9},{9,8},{10,11... | collective-permute-start | bytes 1376264 | tf_op jit(solution)/shard_map/ppermute | solution.py:985
  217.3 13.3 %collective-permute-start.23 = (bf16[128,896]{1,0:T(8,128)(2,1)S(1)}, bf16[128,896]{1,0:T(8,128)(2,1)S(1)}, u32[]{:S(2)}, u32[]{:S(2)}) collective-permute-start(bf16[128,896]{1,0:T(8,128)(2,1)S(1)} %get-tuple-element.154), channel_id=1, source_target_pairs={{0,2},{1,3},{2,0},{3,1},{4,6},{5,7},{6,4},{7,5},{8,10},{9,11},{10,... | collective-permute-start | bytes 688136 | tf_op jit(solution)/shard_map/ppermute | solution.py:985
  219.0 15.5 %collective-permute-start.27 = (bf16[160,512]{1,0:T(8,128)(2,1)S(1)}, bf16[160,512]{1,0:T(8,128)(2,1)S(1)}, u32[]{:S(2)}, u32[]{:S(2)}) collective-permute-start(bf16[160,512]{1,0:T(8,128)(2,1)S(1)} %get-tuple-element.163.refs_0_), channel_id=1, source_target_pairs={{0,12},{4,8},{8,4},{12,0},{16,28},{20,24},{24,20},{28,16},{1,13},{... | collective-permute-start | bytes 491528 | tf_op jit(solution)/shard_map/ppermute | solution.py:985
  220.8 15.5 %collective-permute-start.26 = (bf16[160,512]{1,0:T(8,128)(2,1)S(1)}, bf16[160,512]{1,0:T(8,128)(2,1)S(1)}, u32[]{:S(2)}, u32[]{:S(2)}) collective-permute-start(bf16[160,512]{1,0:T(8,128)(2,1)S(1)} %get-tuple-element.163.refs_0_), channel_id=1, source_target_pairs={{0,8},{4,12},{8,0},{12,4},{16,24},{20,28},{24,16},{28,20},{1,9},{5... | collective-permute-start | bytes 491528 | tf_op jit(solution)/shard_map/ppermute | solution.py:985
  221.4 20.9 %collective-permute-start.25 = (bf16[160,512]{1,0:T(8,128)(2,1)S(1)}, bf16[160,512]{1,0:T(8,128)(2,1)S(1)}, u32[]{:S(2)}, u32[]{:S(2)}) collective-permute-start(bf16[160,512]{1,0:T(8,128)(2,1)S(1)} %get-tuple-element.163.refs_0_), channel_id=1, source_target_pairs={{0,4},{4,0},{8,12},{12,8},{16,20},{20,16},{24,28},{28,24},{1,5},{5... | collective-permute-start | bytes 491528 | tf_op jit(solution)/shard_map/ppermute | solution.py:985
  236.3 19.6 %collective-permute-start.30 = (bf16[128,512]{1,0:T(8,128)(2,1)S(1)}, bf16[128,512]{1,0:T(8,128)(2,1)S(1)}, u32[]{:S(2)}, u32[]{:S(2)}) collective-permute-start(bf16[128,512]{1,0:T(8,128)(2,1)S(1)} %get-tuple-element.164.refs_4_), channel_id=1, source_target_pairs={{0,12},{4,8},{8,4},{12,0},{16,28},{20,24},{24,20},{28,16},{1,13},{... | collective-permute-start | bytes 393224 | tf_op jit(solution)/shard_map/ppermute | solution.py:985
  (54 other events, 451.0 us)

commit v5 on v4

--- a/solution.py
+++ b/solution.py
@@ -876,7 +876,7 @@
             pltpu.SemaphoreType.DMA,
             pltpu.SemaphoreType.DMA,
         ],
-        compiler_params=pltpu.CompilerParams(vmem_limit_bytes=62 * 2**20),
+        compiler_params=pltpu.CompilerParams(vmem_limit_bytes=57 * 2**20),
         cost_estimate=pl.CostEstimate(
             flops=8 * 10**9, bytes_accessed=15 * 10**6, transcendentals=0
         ),
@@ -966,7 +966,7 @@
             pltpu.SemaphoreType.DMA((seq_rows // TILE, 1 + groups)),
             pltpu.SemaphoreType.DMA,
         ],
-        compiler_params=pltpu.CompilerParams(vmem_limit_bytes=VMEM_LIMIT),
+        compiler_params=pltpu.CompilerParams(vmem_limit_bytes=52 * 2**20),
         cost_estimate=pl.CostEstimate(
             flops=2 * 10**9, bytes_accessed=7 * 10**6, transcendentals=0
         ),

time: 266 us -> 252 us (0.947)
  Pallas kernels: 144 us -> 134 us
  local copies, waits for them, and re-layouts: 14.4 us -> 8.75 us
  starting transfers between devices: 74.2 us -> 79.4 us
  waiting for transfers between devices: 26.8 us -> 22.4 us
    pallas_call x8, Pallas kernels: 10.4 us -> 3.67 us  [combine(): pl.pallas_call(partial(combine_kernel, [[len(g) for g in i[0]] for i in i...]
    unnamed x80 -> x64, local copies, waits for them, and re-layouts: 14.4 us -> 8.75 us
    ppermute x38, starting transfers between devices: 74.2 us -> 79.4 us  [exchange(): return lax.ppermute(value, axis, [(i, i ^ bit) for i in range(size)])]
    ppermute x38, waiting for transfers between devices: 26.8 us -> 22.4 us  [exchange(): return lax.ppermute(value, axis, [(i, i ^ bit) for i in range(size)])]
    pallas_call x2, Pallas kernels: 11.4 us -> 8.45 us  [input_gradient(): pl.pallas_call(partial(input_kernel, seq_rows, groups, seq), out_shape=(j...]
  transfers between devices with their start and end apart: 38 -> 38, of which waited for: 10 -> 10; matrix products, arithmetic and copies ran while one was open for 0% -> 1% of each run, Pallas kernels for 34% -> 34%
where the time goes in v5:
time: 252 us; the launch traced here: 248 us
  Pallas kernels  134 us (53%)
  starting transfers between devices  79.4 us (32%)
  waiting for transfers between devices  22.4 us (9%)
  local copies, waits for them, and re-layouts  8.75 us (3%)
    ppermute x38, starting transfers between devices, exchange(): return lax.ppermute(value, axis, [(i, i ^ bit) for i in range(size)])  79.4 us
    pallas_call x4, Pallas kernels, attention_backward(): pl.pallas_call(partial(bwd_kernel, seq_rows, groups, group, seq, shards,...  48.4 us
    pallas_call x1, Pallas kernels, feed_forward(): pl.pallas_call(partial(ffn_kernel, seq_rows, shards), out_shape=(jax.Shap...  46.4 us
    pallas_call x2, Pallas kernels, attention_forward(): pl.pallas_call(partial(fwd_kernel, seq_rows, seq), out_shape=(jax.ShapeDt...  23.9 us
    ppermute x38, waiting for transfers between devices, exchange(): return lax.ppermute(value, axis, [(i, i ^ bit) for i in range(size)])  22.4 us
    unnamed x64, local copies, waits for them, and re-layouts  8.75 us
    pallas_call x2, Pallas kernels, input_gradient(): pl.pallas_call(partial(input_kernel, seq_rows, groups, seq), out_shape=(j...  8.45 us
  transfers between devices with their start and end apart: 38, of which 10 were waited for; matrix products, arithmetic and copies ran while one was open for 1% of the time, Pallas kernels for 34%

profile of v5, /device:TPU:0, one launch (start us, length us, event | category | flops | bytes accessed | tf_op | source)
XLA Modules:
  0.0 248.1 jit_solution(9761215265762615569)
XLA Ops:
  1.7 3.0 %collective-permute-start.1 = (bf16[144,1536]{1,0:T(8,128)(2,1)S(1)}, bf16[144,1536]{1,0:T(8,128)(2,1)S(1)}, u32[]{:S(2)}, u32[]{:S(2)}) collective-permute-start(bf16[144,1536]{1,0:T(8,128)(2,1)S(1)} %fusion.1.refs_0_), channel_id=1, source_target_pairs={{0,2},{1,3},{2,0},{3,1},{4,6},{5,7},{6,4},{7,5},{8,10},{9,11},{10,... | collective-permute-start | bytes 1327112 | tf_op jit(solution)/shard_map/ppermute | solution.py:985
  4.7 10.2 %collective-permute-done.1.refs_2_ = bf16[144,1536]{1,0:T(8,128)(2,1)S(1)} collective-permute-done((bf16[144,1536]{1,0:T(8,128)(2,1)S(1)}, bf16[144,1536]{1,0:T(8,128)(2,1)S(1)}, u32[]{:S(2)}, u32[]{:S(2)}) %collective-permute-start.1) | collective-permute-done | bytes 442400 | tf_op jit(solution)/shard_map/ppermute | solution.py:985
  19.2 5.5 %attention_forward.3 = (bf16[4,8,1056,256]{3,2,1,0:T(8,128)(2,1)}, bf16[512,1024]{1,0:T(8,128)(2,1)S(1)}, bf16[512,1024]{1,0:T(8,128)(2,1)S(1)}, f32[8,1024]{1,0:T(8,128)S(1)}) custom-call(s32[2]{0:T(128)S(1)} %copy-done.11, bf16[2,1024,512]{2,1,0:T(8,128)(2,1)S(1)} %copy-done.13, bf16[512,1536]{1,0:T(8,128)(2,1)S(1)} %get-tuple-element.92.wk_ref.refs_2_.refs_3_.w_ref, ...), custom_call_target="tpu_custom_call" | custom-call | flops 8000000000 | bytes 24000000 | tf_op jit(solution)/shard_map/attention_forward/pallas_call | solution.py:265
  24.8 12.0 %collective-permute-start.6 = (bf16[512,512]{1,0:T(8,128)(2,1)S(1)}, bf16[512,512]{1,0:T(8,128)(2,1)S(1)}, u32[]{:S(2)}, u32[]{:S(2)}) collective-permute-start(bf16[512,512]{1,0:T(8,128)(2,1)S(1)} %copy-done.28), channel_id=1, source_target_pairs={{0,2},{1,3},{2,0},{3,1},{4,6},{5,7},{6,4},{7,5},{8,10},{9,11},{10,... | collective-permute-start | bytes 1572872 | tf_op jit(solution)/shard_map/ppermute | solution.py:985
  37.4 18.4 %attention_forward.2 = (bf16[4,8,1056,256]{3,2,1,0:T(8,128)(2,1)}, bf16[512,1024]{1,0:T(8,128)(2,1)S(1)}, bf16[512,1024]{1,0:T(8,128)(2,1)S(1)}, f32[8,1024]{1,0:T(8,128)S(1)}) custom-call(s32[2]{0:T(128)S(1)} %copy-done.11, bf16[2,1024,512]{2,1,0:T(8,128)(2,1)S(1)} %copy-done.13, bf16[512,1536]{1,0:T(8,128)(2,1)S(1)} %get-tuple-element.92.wk_ref.refs_2_.refs_3_.w_ref, ...), custom_call_target="tpu_custom_call" | custom-call | flops 8000000000 | bytes 24000000 | tf_op jit(solution)/shard_map/attention_forward/pallas_call | solution.py:265
  60.9 46.4 %feed_forward.1 = (bf16[2,1024,512]{2,1,0:T(8,128)(2,1)}, bf16[2,1024,512]{2,1,0:T(8,128)(2,1)}, bf16[2,512,1024]{2,1,0:T(8,128)(2,1)}, bf16[1280,512]{1,0:T(8,1...) custom-call(s32[2]{0:T(128)} %len_ref.9, ...), custom_call_target="tpu_custom_call" | custom-call | flops 27000000512 | bytes 24000000 | tf_op jit(solution)/shard_map/feed_forward/pallas_call | solution.py:557
  107.9 17.6 %attention_backward.4 = (bf16[1280,768]{1,0:T(8,128)(2,1)}, f32[512,768]{1,0:T(8,128)}, f32[32,512]{1,0:T(8,128)}, f32[8,128]{1,0:T(8,128)}) custom-call(s32[2]{0:T(128)} %len_ref.9, s32[1]{0:T(128)} %bitcast.me_ref.refs_1_, bf16[512,1536]{1,0:T(8,128)(2,1)} %copy-done, bf16[512,1536]{1,0:T(8,128)(2,1)} %copy-done, bf16[32,512]{1,0:T(8,128)(2,1)} %copy-done.14, ...), custom_call_target="tpu_custom_call" | custom-call | flops 8000000000 | bytes 15000000 | tf_op jit(solution)/shard_map/attention_backward/pallas_call | solution.py:837
  127.1 9.5 %collective-permute-start.12 = (bf16[256,512]{1,0:T(8,128)(2,1)S(1)}, bf16[256,512]{1,0:T(8,128)(2,1)S(1)}, u32[]{:S(2)}, u32[]{:S(2)}) collective-permute-start(bf16[256,512]{1,0:T(8,128)(2,1)S(1)} %get-tuple-element.125), channel_id=1, source_target_pairs={{0,4},{4,0},{8,12},{12,8},{16,20},{20,16},{24,28},{28,24},{1,5},{5... | collective-permute-start | bytes 786440 | tf_op jit(solution)/shard_map/ppermute | solution.py:985
  139.8 6.6 %attention_backward.5 = (bf16[1280,768]{1,0:T(8,128)(2,1)}, bf16[256,768]{1,0:T(8,128)(2,1)}, bf16[256,768]{1,0:T(8,128)(2,1)}, f32[32,512]{1,0:T(8,128)}, f32[8,128]{1,0:T(8,128)}) custom-call(s32[2]{0:T(128)} %len_ref.9, s32[1]{0:T(128)} %bitcast.me_ref.refs_1_, bf16[512,1536]{1,0:T(8,128)(2,1)} %copy-done, bf16[512,1536]{1,0:T(8,128)(2,1)} %copy-done, ...), custom_call_target="tpu_custom_call" | custom-call | flops 8000000000 | bytes 15000000 | tf_op jit(solution)/shard_map/attention_backward/pallas_call | solution.py:837
  146.4 12.9 %collective-permute-start.18 = (bf16[256,768]{1,0:T(8,128)(2,1)}, bf16[256,768]{1,0:T(8,128)(2,1)S(1)}, u32[]{:S(2)}, u32[]{:S(2)}) collective-permute-start(bf16[256,768]{1,0:T(8,128)(2,1)} %get-tuple-element.139), channel_id=1, source_target_pairs={{0,1},{1,0},{2,3},{3,2},{4,5},{5,4},{6,7},{7,6},{8,9},{9,8},{10,11... | collective-permute-start | bytes 1179656 | tf_op jit(solution)/shard_map/ppermute | solution.py:985
  162.0 2.0 collective-permute-start.17
  164.0 17.3 %attention_backward.6 = (bf16[1280,768]{1,0:T(8,128)(2,1)}, f32[512,768]{1,0:T(8,128)}, f32[32,512]{1,0:T(8,128)}, f32[8,128]{1,0:T(8,128)}) custom-call(s32[2]{0:T(128)} %len_ref.9, s32[1]{0:T(128)} %bitcast.me_ref.refs_1_, bf16[512,1536]{1,0:T(8,128)(2,1)} %copy-done, bf16[512,1536]{1,0:T(8,128)(2,1)} %copy-done, bf16[32,512]{1,0:T(8,128)(2,1)} %copy-done.14, ...), custom_call_target="tpu_custom_call" | custom-call | flops 8000000000 | bytes 15000000 | tf_op jit(solution)/shard_map/attention_backward/pallas_call | solution.py:837
  183.0 2.0 collective-permute-start.21
  185.0 2.0 collective-permute-start.20
  187.0 6.9 %attention_backward.7 = (bf16[1280,768]{1,0:T(8,128)(2,1)}, bf16[256,896]{1,0:T(8,128)(2,1)}, bf16[256,896]{1,0:T(8,128)(2,1)}, f32[8,128]{1,0:T(8,128)}) custom-call(s32[2]{0:T(128)} %len_ref.9, s32[1]{0:T(128)} %bitcast.me_ref.refs_1_, bf16[512,1536]{1,0:T(8,128)(2,1)} %copy-done, bf16[512,1536]{1,0:T(8,128)(2,1)} %copy-done, bf16[32,512]{1,0:T(8,128)(2,1)} %copy-done.14, ...), custom_call_target="tpu_custom_call" | custom-call | flops 8000000000 | bytes 15000000 | tf_op jit(solution)/shard_map/attention_backward/pallas_call | solution.py:837
  196.5 3.1 %collective-permute-start.22 = (bf16[256,896]{1,0:T(8,128)(2,1)S(1)}, bf16[256,896]{1,0:T(8,128)(2,1)S(1)}, u32[]{:S(2)}, u32[]{:S(2)}) collective-permute-start(bf16[256,896]{1,0:T(8,128)(2,1)S(1)} %get-tuple-element.152), channel_id=1, source_target_pairs={{0,1},{1,0},{2,3},{3,2},{4,5},{5,4},{6,7},{7,6},{8,9},{9,8},{10,11... | collective-permute-start | bytes 1376264 | tf_op jit(solution)/shard_map/ppermute | solution.py:985
  202.2 6.3 %collective-permute-start.23 = (bf16[128,896]{1,0:T(8,128)(2,1)S(1)}, bf16[128,896]{1,0:T(8,128)(2,1)S(1)}, u32[]{:S(2)}, u32[]{:S(2)}) collective-permute-start(bf16[128,896]{1,0:T(8,128)(2,1)S(1)} %get-tuple-element.154), channel_id=1, source_target_pairs={{0,2},{1,3},{2,0},{3,1},{4,6},{5,7},{6,4},{7,5},{8,10},{9,11},{10,... | collective-permute-start | bytes 688136 | tf_op jit(solution)/shard_map/ppermute | solution.py:985
  209.4 2.5 %collective-permute-start.25 = (bf16[160,512]{1,0:T(8,128)(2,1)S(1)}, bf16[160,512]{1,0:T(8,128)(2,1)S(1)}, u32[]{:S(2)}, u32[]{:S(2)}) collective-permute-start(bf16[160,512]{1,0:T(8,128)(2,1)S(1)} %get-tuple-element.163.refs_0_), channel_id=1, source_target_pairs={{0,4},{4,0},{8,12},{12,8},{16,20},{20,16},{24,28},{28,24},{1,5},{5... | collective-permute-start | bytes 491528 | tf_op jit(solution)/shard_map/ppermute | solution.py:985
  211.9 5.0 %input_gradient.2 = (bf16[2,1024,512]{2,1,0:T(8,128)(2,1)}, f32[8,128]{1,0:T(8,128)S(1)}) custom-call(s32[2]{0:T(128)S(1)} %copy-done.12, bf16[512,1536]{1,0:T(8,128)(2,1)S(1)} %copy-done.1, bf16[2,1024,512]{2,1,0:T(8,128)(2,1)} %get-tuple-element.107.gh_hbm, bf16[1280,768]{1,0:T(8,128)(2,1)} %get-tuple-element.156.refs_0_, ...), custom_call_target="tpu_custom_call" | custom-call | flops 2000000000 | bytes 7000000 | tf_op jit(solution)/shard_map/input_gradient/pallas_call | solution.py:952
  218.7 2.0 collective-permute-start.31
  225.2 3.5 %input_gradient.3 = (bf16[2,1024,512]{2,1,0:T(8,128)(2,1)}, f32[8,128]{1,0:T(8,128)S(1)}) custom-call(s32[2]{0:T(128)S(1)} %copy-done.12, bf16[512,1536]{1,0:T(8,128)(2,1)S(1)} %copy-done.1, bf16[2,1024,512]{2,1,0:T(8,128)(2,1)} %get-tuple-element.107.gh_hbm, bf16[1280,768]{1,0:T(8,128)(2,1)} %get-tuple-element.121.refs_0_, ...), custom_call_target="tpu_custom_call", output_to_operand_aliasing={{0}: (6, {})} | custom-call | flops 2000000000 | bytes 7000000 | tf_op jit(solution)/shard_map/input_gradient/pallas_call | solution.py:952
  236.8 2.2 collective-permute-start.37
  239.0 2.3 collective-permute-start.36
  242.5 2.7 %collective-permute-done.36.refs_10_ = bf16[64,896]{1,0:T(8,128)(2,1)S(1)} collective-permute-done((bf16[64,896]{1,0:T(8,128)(2,1)S(1)}, bf16[64,896]{1,0:T(8,128)(2,1)S(1)}, u32[]{:S(2)}, u32[]{:S(2)}) %collective-permute-start.36) | collective-permute-done | bytes 114720 | tf_op jit(solution)/shard_map/ppermute | solution.py:985
  (137 shorter events, 44.7 us)
Async XLA Ops:
  1.7 13.2 %collective-permute-start.1 = (bf16[144,1536]{1,0:T(8,128)(2,1)S(1)}, bf16[144,1536]{1,0:T(8,128)(2,1)S(1)}, u32[]{:S(2)}, u32[]{:S(2)}) collective-permute-start(bf16[144,1536]{1,0:T(8,128)(2,1)S(1)} %fusion.1.refs_0_), channel_id=1, source_target_pairs={{0,2},{1,3},{2,0},{3,1},{4,6},{5,7},{6,4},{7,5},{8,10},{9,11},{10,... | collective-permute-start | bytes 1327112 | tf_op jit(solution)/shard_map/ppermute | solution.py:985
  4.7 13.3 %collective-permute-start = (bf16[144,1536]{1,0:T(8,128)(2,1)S(1)}, bf16[144,1536]{1,0:T(8,128)(2,1)S(1)}, u32[]{:S(2)}, u32[]{:S(2)}) collective-permute-start(bf16[144,1536]{1,0:T(8,128)(2,1)S(1)} %fusion.1.refs_0_), channel_id=1, source_target_pairs={{0,1},{1,0},{2,3},{3,2},{4,5},{5,4},{6,7},{7,6},{8,9},{9,8},{10,11... | collective-permute-start | bytes 1327112 | tf_op jit(solution)/shard_map/ppermute | solution.py:985
  16.1 20.7 %collective-permute-start.3 = (bf16[128,2560]{1,0:T(8,128)(2,1)S(1)}, bf16[128,2560]{1,0:T(8,128)(2,1)S(1)}, u32[]{:S(2)}, u32[]{:S(2)}) collective-permute-start(bf16[128,2560]{1,0:T(8,128)(2,1)S(1)} %pad_maximum_fusion.refs_0_), channel_id=1, source_target_pairs={{0,2},{1,3},{2,0},{3,1},{4,6},{5,7},{6,4},{7,5},{8,10},{9,11},{10,... | collective-permute-start | bytes 1966088 | tf_op jit(solution)/shard_map/ppermute | solution.py:985
  24.8 32.6 %collective-permute-start.6 = (bf16[512,512]{1,0:T(8,128)(2,1)S(1)}, bf16[512,512]{1,0:T(8,128)(2,1)S(1)}, u32[]{:S(2)}, u32[]{:S(2)}) collective-permute-start(bf16[512,512]{1,0:T(8,128)(2,1)S(1)} %copy-done.28), channel_id=1, source_target_pairs={{0,2},{1,3},{2,0},{3,1},{4,6},{5,7},{6,4},{7,5},{8,10},{9,11},{10,... | collective-permute-start | bytes 1572872 | tf_op jit(solution)/shard_map/ppermute | solution.py:985
  36.9 21.1 %collective-permute-start.4 = (bf16[128,2560]{1,0:T(8,128)(2,1)S(1)}, bf16[128,2560]{1,0:T(8,128)(2,1)S(1)}, u32[]{:S(2)}, u32[]{:S(2)}) collective-permute-start(bf16[128,2560]{1,0:T(8,128)(2,1)S(1)} %pad_maximum_fusion.refs_0_), channel_id=1, source_target_pairs={{0,1},{1,0},{2,3},{3,2},{4,5},{5,4},{6,7},{7,6},{8,9},{9,8},{10,11... | collective-permute-start | bytes 1966088 | tf_op jit(solution)/shard_map/ppermute | solution.py:985
  36.9 21.0 %collective-permute-start.5 = (bf16[128,2560]{1,0:T(8,128)(2,1)S(1)}, bf16[128,2560]{1,0:T(8,128)(2,1)S(1)}, u32[]{:S(2)}, u32[]{:S(2)}) collective-permute-start(bf16[128,2560]{1,0:T(8,128)(2,1)S(1)} %collective-permute-done.3.refs_2_), channel_id=1, source_target_pairs={{0,1},{1,0},{2,3},{3,2},{4,5},{5,4},{6,7},{7,6},{8,9},{9,8},{10,11... | collective-permute-start | bytes 1966088 | tf_op jit(solution)/shard_map/ppermute | solution.py:985
  107.3 18.2 %collective-permute-start.9 = (bf16[1280,512]{1,0:T(8,128)(2,1)}, bf16[1280,512]{1,0:T(8,128)(2,1)S(1)}, u32[]{:S(2)}, u32[]{:S(2)}) collective-permute-start(bf16[1280,512]{1,0:T(8,128)(2,1)} %get-tuple-element.116), channel_id=1, source_target_pairs={{0,1},{1,0},{2,3},{3,2},{4,5},{5,4},{6,7},{7,6},{8,9},{9,8},{10,11... | collective-permute-start | bytes 3932168 | tf_op jit(solution)/shard_map/ppermute | solution.py:985
  107.5 18.0 %collective-permute-start.10 = (bf16[1024,512]{1,0:T(8,128)(2,1)}, bf16[1024,512]{1,0:T(8,128)(2,1)S(1)}, u32[]{:S(2)}, u32[]{:S(2)}) collective-permute-start(bf16[1024,512]{1,0:T(8,128)(2,1)} %get-tuple-element.118), channel_id=1, source_target_pairs={{0,1},{1,0},{2,3},{3,2},{4,5},{5,4},{6,7},{7,6},{8,9},{9,8},{10,11... | collective-permute-start | bytes 3145736 | tf_op jit(solution)/shard_map/ppermute | solution.py:985
  127.1 32.3 %collective-permute-start.12 = (bf16[256,512]{1,0:T(8,128)(2,1)S(1)}, bf16[256,512]{1,0:T(8,128)(2,1)S(1)}, u32[]{:S(2)}, u32[]{:S(2)}) collective-permute-start(bf16[256,512]{1,0:T(8,128)(2,1)S(1)} %get-tuple-element.125), channel_id=1, source_target_pairs={{0,4},{4,0},{8,12},{12,8},{16,20},{20,16},{24,28},{28,24},{1,5},{5... | collective-permute-start | bytes 786440 | tf_op jit(solution)/shard_map/ppermute | solution.py:985
  136.6 22.8 %collective-permute-start.13 = (bf16[256,512]{1,0:T(8,128)(2,1)S(1)}, bf16[256,512]{1,0:T(8,128)(2,1)S(1)}, u32[]{:S(2)}, u32[]{:S(2)}) collective-permute-start(bf16[256,512]{1,0:T(8,128)(2,1)S(1)} %get-tuple-element.126), channel_id=1, source_target_pairs={{0,8},{4,12},{8,0},{12,4},{16,24},{20,28},{24,16},{28,20},{1,9},{5... | collective-permute-start | bytes 786440 | tf_op jit(solution)/shard_map/ppermute | solution.py:985
  136.6 22.8 %collective-permute-start.14 = (bf16[256,512]{1,0:T(8,128)(2,1)S(1)}, bf16[256,512]{1,0:T(8,128)(2,1)S(1)}, u32[]{:S(2)}, u32[]{:S(2)}) collective-permute-start(bf16[256,512]{1,0:T(8,128)(2,1)S(1)} %get-tuple-element.127), channel_id=1, source_target_pairs={{0,12},{4,8},{8,4},{12,0},{16,28},{20,24},{24,20},{28,16},{1,13},{... | collective-permute-start | bytes 786440 | tf_op jit(solution)/shard_map/ppermute | solution.py:985
  138.1 21.3 %collective-permute-start.11 = (bf16[640,512]{1,0:T(8,128)(2,1)S(1)}, bf16[640,512]{1,0:T(8,128)(2,1)S(1)}, u32[]{:S(2)}, u32[]{:S(2)}) collective-permute-start(bf16[640,512]{1,0:T(8,128)(2,1)S(1)} %get-tuple-element.123), channel_id=1, source_target_pairs={{0,2},{1,3},{2,0},{3,1},{4,6},{5,7},{6,4},{7,5},{8,10},{9,11},{10,... | collective-permute-start | bytes 1966088 | tf_op jit(solution)/shard_map/ppermute | solution.py:985
  146.4 35.0 %collective-permute-start.18 = (bf16[256,768]{1,0:T(8,128)(2,1)}, bf16[256,768]{1,0:T(8,128)(2,1)S(1)}, u32[]{:S(2)}, u32[]{:S(2)}) collective-permute-start(bf16[256,768]{1,0:T(8,128)(2,1)} %get-tuple-element.139), channel_id=1, source_target_pairs={{0,1},{1,0},{2,3},{3,2},{4,5},{5,4},{6,7},{7,6},{8,9},{9,8},{10,11... | collective-permute-start | bytes 1179656 | tf_op jit(solution)/shard_map/ppermute | solution.py:985
  160.5 21.0 %collective-permute-start.15 = (bf16[160,512]{1,0:T(8,128)(2,1)S(1)}, bf16[160,512]{1,0:T(8,128)(2,1)S(1)}, u32[]{:S(2)}, u32[]{:S(2)}) collective-permute-start(bf16[160,512]{1,0:T(8,128)(2,1)S(1)} %get-tuple-element.135), channel_id=1, source_target_pairs={{0,4},{4,0},{8,12},{12,8},{16,20},{20,16},{24,28},{28,24},{1,5},{5... | collective-permute-start | bytes 491528 | tf_op jit(solution)/shard_map/ppermute | solution.py:985
  162.0 19.5 %collective-permute-start.16 = (bf16[160,512]{1,0:T(8,128)(2,1)S(1)}, bf16[160,512]{1,0:T(8,128)(2,1)S(1)}, u32[]{:S(2)}, u32[]{:S(2)}) collective-permute-start(bf16[160,512]{1,0:T(8,128)(2,1)S(1)} %get-tuple-element.136), channel_id=1, source_target_pairs={{0,8},{4,12},{8,0},{12,4},{16,24},{20,28},{24,16},{28,20},{1,9},{5... | collective-permute-start | bytes 491528 | tf_op jit(solution)/shard_map/ppermute | solution.py:985
  162.0 19.5 %collective-permute-start.17 = (bf16[160,512]{1,0:T(8,128)(2,1)S(1)}, bf16[160,512]{1,0:T(8,128)(2,1)S(1)}, u32[]{:S(2)}, u32[]{:S(2)}) collective-permute-start(bf16[160,512]{1,0:T(8,128)(2,1)S(1)} %get-tuple-element.137), channel_id=1, source_target_pairs={{0,12},{4,8},{8,4},{12,0},{16,28},{20,24},{24,20},{28,16},{1,13},{... | collective-permute-start | bytes 491528 | tf_op jit(solution)/shard_map/ppermute | solution.py:985
  181.4 12.5 %collective-permute-start.19 = (bf16[128,512]{1,0:T(8,128)(2,1)S(1)}, bf16[128,512]{1,0:T(8,128)(2,1)S(1)}, u32[]{:S(2)}, u32[]{:S(2)}) collective-permute-start(bf16[128,512]{1,0:T(8,128)(2,1)S(1)} %get-tuple-element.144), channel_id=1, source_target_pairs={{0,2},{1,3},{2,0},{3,1},{4,6},{5,7},{6,4},{7,5},{8,10},{9,11},{10,... | collective-permute-start | bytes 393224 | tf_op jit(solution)/shard_map/ppermute | solution.py:985
  183.0 10.9 %collective-permute-start.21 = (bf16[160,512]{1,0:T(8,128)(2,1)S(1)}, bf16[160,512]{1,0:T(8,128)(2,1)S(1)}, u32[]{:S(2)}, u32[]{:S(2)}) collective-permute-start(bf16[160,512]{1,0:T(8,128)(2,1)S(1)} %get-tuple-element.147.refs_4_), channel_id=1, source_target_pairs={{0,16},{4,20},{8,24},{12,28},{16,0},{20,4},{24,8},{28,12},{1,17},{... | collective-permute-start | bytes 491528 | tf_op jit(solution)/shard_map/ppermute | solution.py:985
  202.2 16.4 %collective-permute-start.23 = (bf16[128,896]{1,0:T(8,128)(2,1)S(1)}, bf16[128,896]{1,0:T(8,128)(2,1)S(1)}, u32[]{:S(2)}, u32[]{:S(2)}) collective-permute-start(bf16[128,896]{1,0:T(8,128)(2,1)S(1)} %get-tuple-element.154), channel_id=1, source_target_pairs={{0,2},{1,3},{2,0},{3,1},{4,6},{5,7},{6,4},{7,5},{8,10},{9,11},{10,... | collective-permute-start | bytes 688136 | tf_op jit(solution)/shard_map/ppermute | solution.py:985
  208.4 13.8 %collective-permute-start.27 = (bf16[160,512]{1,0:T(8,128)(2,1)S(1)}, bf16[160,512]{1,0:T(8,128)(2,1)S(1)}, u32[]{:S(2)}, u32[]{:S(2)}) collective-permute-start(bf16[160,512]{1,0:T(8,128)(2,1)S(1)} %get-tuple-element.163.refs_0_), channel_id=1, source_target_pairs={{0,12},{4,8},{8,4},{12,0},{16,28},{20,24},{24,20},{28,16},{1,13},{... | collective-permute-start | bytes 491528 | tf_op jit(solution)/shard_map/ppermute | solution.py:985
  208.4 15.2 %collective-permute-start.26 = (bf16[160,512]{1,0:T(8,128)(2,1)S(1)}, bf16[160,512]{1,0:T(8,128)(2,1)S(1)}, u32[]{:S(2)}, u32[]{:S(2)}) collective-permute-start(bf16[160,512]{1,0:T(8,128)(2,1)S(1)} %get-tuple-element.163.refs_0_), channel_id=1, source_target_pairs={{0,8},{4,12},{8,0},{12,4},{16,24},{20,28},{24,16},{28,20},{1,9},{5... | collective-permute-start | bytes 491528 | tf_op jit(solution)/shard_map/ppermute | solution.py:985
  209.4 19.2 %collective-permute-start.25 = (bf16[160,512]{1,0:T(8,128)(2,1)S(1)}, bf16[160,512]{1,0:T(8,128)(2,1)S(1)}, u32[]{:S(2)}, u32[]{:S(2)}) collective-permute-start(bf16[160,512]{1,0:T(8,128)(2,1)S(1)} %get-tuple-element.163.refs_0_), channel_id=1, source_target_pairs={{0,4},{4,0},{8,12},{12,8},{16,20},{20,16},{24,28},{28,24},{1,5},{5... | collective-permute-start | bytes 491528 | tf_op jit(solution)/shard_map/ppermute | solution.py:985
  218.7 9.9 %collective-permute-start.31 = (bf16[64,896]{1,0:T(8,128)(2,1)S(1)}, bf16[64,896]{1,0:T(8,128)(2,1)S(1)}, u32[]{:S(2)}, u32[]{:S(2)}) collective-permute-start(bf16[64,896]{1,0:T(8,128)(2,1)S(1)} %get-tuple-element.166), channel_id=1, source_target_pairs={{0,4},{4,0},{8,12},{12,8},{16,20},{20,16},{24,28},{28,24},{1,5},{5... | collective-permute-start | bytes 344072 | tf_op jit(solution)/shard_map/ppermute | solution.py:985
  223.6 17.6 %collective-permute-start.30 = (bf16[128,512]{1,0:T(8,128)(2,1)S(1)}, bf16[128,512]{1,0:T(8,128)(2,1)S(1)}, u32[]{:S(2)}, u32[]{:S(2)}) collective-permute-start(bf16[128,512]{1,0:T(8,128)(2,1)S(1)} %get-tuple-element.164.refs_4_), channel_id=1, source_target_pairs={{0,12},{4,8},{8,4},{12,0},{16,28},{20,24},{24,20},{28,16},{1,13},{... | collective-permute-start | bytes 393224 | tf_op jit(solution)/shard_map/ppermute | solution.py:985
  (46 other events, 457.0 us)
